TPU v7x, 32 devices: a whole 2x2x4 slice. The times are simulated.
32 devices in a mesh: win: 8 (over y, x, core), dp: 4 (over z).
Axes of the slice: x: 2, y: 2, z: 4, core: 2. Of those that a mesh axis runs over, the one named last changes fastest.
Arguments:
- patches: bfloat16 [4, 384, 49, 512], P('dp', 'win'), may hold values from -6 to 6
- regional: bfloat16 [4, 384, 512], P('dp', 'win'), may hold values from -6 to 6
- window_image: int32 [4, 384], P('dp'), may hold values from 0 to 2, as said below
- in_gain: bfloat16 [512], replicated, may hold values from 0.25 to 1.75
- in_shift: bfloat16 [512], replicated, may hold values from -4 to 4
- w_qkv: bfloat16 [512, 1536], replicated, may hold values from -0.25 to 0.25
- qkv_bias: bfloat16 [2, 512], replicated, may hold values from -4 to 4
- w_out: bfloat16 [512, 512], replicated, may hold values from -1 to 1
- out_bias: bfloat16 [512], replicated, may hold values from -4 to 4
- mlp_gain: bfloat16 [512], replicated, may hold values from 0.25 to 1.75
- mlp_shift: bfloat16 [512], replicated, may hold values from -4 to 4
- w_up: bfloat16 [512, 2048], replicated, may hold values from -0.25 to 0.25
- up_bias: bfloat16 [2048], replicated, may hold values from -4 to 4
- w_down: bfloat16 [2048, 512], replicated, may hold values from -0.125 to 0.125
- down_bias: bfloat16 [512], replicated, may hold values from -4 to 4
- patch_cot: bfloat16 [4, 384, 49, 512], P('dp', 'win'), may hold values from -6 to 6
- region_cot: bfloat16 [4, 384, 512], P('dp', 'win'), may hold values from -6 to 6
Outputs:
- patch_out: bfloat16 [4, 384, 49, 512], P('dp', 'win')
- region_out: bfloat16 [4, 384, 512], P('dp', 'win')
- patch_grad: bfloat16 [4, 384, 49, 512], P('dp', 'win')
- region_grad: bfloat16 [4, 384, 512], P('dp', 'win')
- in_gain_grad: float32 [512], replicated
- in_shift_grad: float32 [512], replicated
- qkv_grad: float32 [512, 1536], replicated
- qkv_bias_grad: float32 [2, 512], replicated
- out_grad: float32 [512, 512], replicated
- out_bias_grad: float32 [512], replicated
- mlp_gain_grad: float32 [512], replicated
- mlp_shift_grad: float32 [512], replicated
- up_grad: float32 [512, 2048], replicated
- up_bias_grad: float32 [2048], replicated
- down_grad: float32 [2048, 512], replicated
- down_bias_grad: float32 [512], replicated
Inputs may be any that keep to these rules, and one draw needn't show every extreme that they name: `window_image`: numbers a group's images from 0; each image but the highest-numbered one holds 49, 81 or 144 windows, and the highest-numbered one holds the rest of the group's windows; an image's windows lie at scattered places of the group, and the group's first and last windows belong to image 0.
All inputs are finite; a program needn't handle non-finite values.
Results may differ from a plain program's by a relative error of at most 0.018.
Values may be sent and summed in bfloat16 or wider, within the bound.
A program may use at most 256 MiB of HBM per device.

v0:
```python
from functools import partial

import jax
import jax.numpy as jnp
from jax import lax
from jax.sharding import PartitionSpec as P

D = 512
HEADS = 16
HD = 32


EPSILON = 1e-06
MASKED_SCORE = -1e30


def norm_rows(rows, norm_gain, norm_shift):
    average = jnp.mean(rows, axis=-1, keepdims=True)
    centred = rows - average
    spread = jnp.mean(centred * centred, axis=-1, keepdims=True)
    return centred * lax.rsqrt(spread + EPSILON) * norm_gain + norm_shift


def norm_back(rows, norm_gain, norm_shift, grad_out):
    _, pullback = jax.vjp(norm_rows, rows, norm_gain, norm_shift)
    return pullback(grad_out)


def project(normed, w_qkv, bias_row):
    return (jnp.dot(normed, w_qkv, preferred_element_type=jnp.float32) + bias_row).astype(
        jnp.bfloat16
    )


def masked_scores(query_rows, key_rows, same_image, scaling):
    queries = query_rows.reshape(query_rows.shape[0], HEADS, HD)
    keys_split = key_rows.reshape(key_rows.shape[0], HEADS, HD)
    scores = (
        jnp.einsum("qhe,khe->hqk", queries, keys_split, preferred_element_type=jnp.float32)
        * scaling
    )
    return jnp.where(same_image[None], scores, MASKED_SCORE)


def region_probs(own_query, all_keys, same_image, scaling):
    return jax.nn.softmax(masked_scores(own_query, all_keys, same_image, scaling), axis=-1)


def local_probs_of(local_triple, scaling):
    scores = (
        jnp.einsum(
            "wqhe,wkhe->whqk",
            local_triple[:, :, 0],
            local_triple[:, :, 1],
            preferred_element_type=jnp.float32,
        )
        * scaling
    )
    return jax.nn.softmax(scores, axis=-1)


def column_sums(matrix):
    return jnp.sum(matrix.astype(jnp.float32), axis=0)


def shards(
    patches,
    regional,
    window_image,
    in_gain,
    in_shift,
    w_qkv,
    qkv_bias,
    w_out,
    out_bias,
    mlp_gain,
    mlp_shift,
    w_up,
    up_bias,
    w_down,
    down_bias,
    patch_cot,
    region_cot,
):
    win_count = regional.shape[1]
    window_len = patches.shape[2] + 1
    scaling = HD ** (-0.5)
    first_gain = in_gain.astype(jnp.float32)
    first_shift = in_shift.astype(jnp.float32)
    second_gain = mlp_gain.astype(jnp.float32)
    second_shift = mlp_shift.astype(jnp.float32)
    bias_row = jnp.concatenate([qkv_bias[0], jnp.zeros_like(qkv_bias[0]), qkv_bias[1]]).astype(
        jnp.float32
    )
    all_images = window_image[0]
    own_images = lax.dynamic_slice_in_dim(all_images, lax.axis_index("win") * win_count, win_count)
    same_image = own_images[:, None] == all_images[None, :]
    region_rows = regional[0].astype(jnp.float32)
    region_in = norm_rows(region_rows, first_gain, first_shift).astype(jnp.bfloat16)
    region_triple = project(region_in, w_qkv, bias_row)
    own_query = region_triple[:, :D]
    all_keys, all_values = (
        lax.all_gather(region_triple[:, D : 2 * D], "win", axis=0, tiled=True),
        lax.all_gather(region_triple[:, 2 * D :], "win", axis=0, tiled=True),
    )
    probs_fwd = region_probs(own_query, all_keys, same_image, scaling)
    region_merged = jnp.einsum(
        "hqk,khe->qhe",
        probs_fwd.astype(jnp.bfloat16),
        all_values.reshape(-1, HEADS, HD),
        preferred_element_type=jnp.float32,
    )
    region_merged = region_merged.reshape(win_count, D).astype(jnp.bfloat16)
    region_mid = (
        region_rows
        + jnp.dot(region_merged, w_out, preferred_element_type=jnp.float32)
        + out_bias.astype(jnp.float32)
    )
    tokens = jnp.concatenate([region_mid[:, None, :], patches[0].astype(jnp.float32)], axis=1)
    flat_rows = tokens.reshape(-1, D)
    local_in = norm_rows(flat_rows, first_gain, first_shift).astype(jnp.bfloat16)
    local_triple = project(local_in, w_qkv, bias_row).reshape(win_count, window_len, 3, HEADS, HD)
    local_low = local_probs_of(local_triple, scaling).astype(jnp.bfloat16)
    local_merged = jnp.einsum(
        "whqk,wkhe->wqhe", local_low, local_triple[:, :, 2], preferred_element_type=jnp.float32
    )
    local_merged = local_merged.reshape(-1, D).astype(jnp.bfloat16)
    middle = (
        flat_rows
        + jnp.dot(local_merged, w_out, preferred_element_type=jnp.float32)
        + out_bias.astype(jnp.float32)
    )
    mlp_in = norm_rows(middle, second_gain, second_shift).astype(jnp.bfloat16)
    hidden = jnp.dot(mlp_in, w_up, preferred_element_type=jnp.float32) + up_bias.astype(jnp.float32)
    active_full, gelu_back = jax.vjp(partial(jax.nn.gelu, approximate=False), hidden)
    active = active_full.astype(jnp.bfloat16)
    result = (
        middle
        + jnp.dot(active, w_down, preferred_element_type=jnp.float32)
        + down_bias.astype(jnp.float32)
    )
    result = result.reshape(win_count, window_len, D)
    patch_out = result[:, 1:].astype(jnp.bfloat16)[None]
    region_out = result[:, 0].astype(jnp.bfloat16)[None]
    grad_result = jnp.concatenate([region_cot[0][:, None, :], patch_cot[0]], axis=1).reshape(-1, D)
    down_grad = jnp.einsum("nf,nd->fd", active, grad_result, preferred_element_type=jnp.float32)
    down_bias_grad = column_sums(grad_result)
    grad_active = jnp.einsum("nd,fd->nf", grad_result, w_down, preferred_element_type=jnp.float32)
    grad_hidden = gelu_back(grad_active)[0].astype(jnp.bfloat16)
    up_grad = jnp.einsum("nd,nf->df", mlp_in, grad_hidden, preferred_element_type=jnp.float32)
    up_bias_grad = column_sums(grad_hidden)
    grad_mlp_in = jnp.einsum("nf,df->nd", grad_hidden, w_up, preferred_element_type=jnp.float32)
    grad_norm_two, mlp_gain_grad, mlp_shift_grad = norm_back(
        middle, second_gain, second_shift, grad_mlp_in
    )
    grad_middle = grad_result.astype(jnp.float32) + grad_norm_two
    grad_local_attn = grad_middle.astype(jnp.bfloat16)
    out_grad = jnp.einsum(
        "nd,ne->de", local_merged, grad_local_attn, preferred_element_type=jnp.float32
    )
    out_bias_grad = column_sums(grad_local_attn)
    grad_local_merged = jnp.einsum(
        "ne,de->nd", grad_local_attn, w_out, preferred_element_type=jnp.float32
    )
    grad_local_merged = grad_local_merged.astype(jnp.bfloat16).reshape(
        win_count, window_len, HEADS, HD
    )
    again_probs = local_probs_of(local_triple, scaling)
    grad_local_probs = jnp.einsum(
        "wqhe,wkhe->whqk",
        grad_local_merged,
        local_triple[:, :, 2],
        preferred_element_type=jnp.float32,
    )
    grad_local_scores = again_probs * (
        grad_local_probs - jnp.sum(grad_local_probs * again_probs, axis=-1, keepdims=True)
    )
    grad_local_scores = grad_local_scores.astype(jnp.bfloat16)
    grad_query = (
        jnp.einsum(
            "whqk,wkhe->wqhe",
            grad_local_scores,
            local_triple[:, :, 1],
            preferred_element_type=jnp.float32,
        )
        * scaling
    )
    grad_keys = (
        jnp.einsum(
            "whqk,wqhe->wkhe",
            grad_local_scores,
            local_triple[:, :, 0],
            preferred_element_type=jnp.float32,
        )
        * scaling
    )
    grad_values = jnp.einsum(
        "whqk,wqhe->wkhe",
        again_probs.astype(jnp.bfloat16),
        grad_local_merged,
        preferred_element_type=jnp.float32,
    )
    grad_triple = (
        jnp.stack([grad_query, grad_keys, grad_values], axis=2)
        .reshape(-1, 3 * D)
        .astype(jnp.bfloat16)
    )
    qkv_grad = jnp.einsum("nd,ne->de", local_in, grad_triple, preferred_element_type=jnp.float32)
    triple_sums = column_sums(grad_triple)
    grad_local_in = jnp.einsum("ne,de->nd", grad_triple, w_qkv, preferred_element_type=jnp.float32)
    grad_norm_one, in_gain_grad, in_shift_grad = norm_back(
        flat_rows, first_gain, first_shift, grad_local_in
    )
    grad_tokens = (grad_middle + grad_norm_one).reshape(win_count, window_len, D)
    patch_grad = grad_tokens[:, 1:].astype(jnp.bfloat16)[None]
    grad_region_mid = grad_tokens[:, 0]
    grad_region_attn = grad_region_mid.astype(jnp.bfloat16)
    out_grad = out_grad + jnp.einsum(
        "nd,ne->de", region_merged, grad_region_attn, preferred_element_type=jnp.float32
    )
    out_bias_grad = out_bias_grad + column_sums(grad_region_attn)
    grad_region_merged = jnp.einsum(
        "ne,de->nd", grad_region_attn, w_out, preferred_element_type=jnp.float32
    )
    grad_region_merged = grad_region_merged.astype(jnp.bfloat16).reshape(win_count, HEADS, HD)
    keys_back, values_back = (all_keys, all_values)
    scores_back = masked_scores(own_query, keys_back, same_image, scaling)
    probs_back = jax.nn.softmax(scores_back, axis=-1)
    grad_region_probs = jnp.einsum(
        "qhe,khe->hqk",
        grad_region_merged,
        values_back.reshape(-1, HEADS, HD),
        preferred_element_type=jnp.float32,
    )
    row_terms = jnp.sum(grad_region_probs * probs_back, axis=-1)
    grad_region_scores = probs_back * (grad_region_probs - row_terms[:, :, None])
    grad_region_scores = grad_region_scores.astype(jnp.bfloat16)
    grad_region_query = (
        jnp.einsum(
            "hqk,khe->qhe",
            grad_region_scores,
            keys_back.reshape(-1, HEADS, HD),
            preferred_element_type=jnp.float32,
        )
        * scaling
    )
    key_terms = (
        jnp.einsum(
            "hqk,qhe->khe",
            grad_region_scores,
            own_query.reshape(win_count, HEADS, HD),
            preferred_element_type=jnp.float32,
        )
        * scaling
    )
    value_terms = jnp.einsum(
        "hqk,qhe->khe",
        probs_back.astype(jnp.bfloat16),
        grad_region_merged,
        preferred_element_type=jnp.float32,
    )
    key_sums, value_sums = (
        lax.psum_scatter(
            key_terms.reshape(-1, D).astype(jnp.bfloat16), "win", scatter_dimension=0, tiled=True
        ).astype(jnp.float32),
        lax.psum_scatter(
            value_terms.reshape(-1, D).astype(jnp.bfloat16), "win", scatter_dimension=0, tiled=True
        ).astype(jnp.float32),
    )
    region_grad_triple = jnp.concatenate(
        [grad_region_query.reshape(win_count, D), key_sums, value_sums], axis=1
    ).astype(jnp.bfloat16)
    qkv_grad = qkv_grad + jnp.einsum(
        "nd,ne->de", region_in, region_grad_triple, preferred_element_type=jnp.float32
    )
    triple_sums = triple_sums + column_sums(region_grad_triple)
    grad_region_in = jnp.einsum(
        "ne,de->nd", region_grad_triple, w_qkv, preferred_element_type=jnp.float32
    )
    grad_norm_region, gain_part, shift_part = norm_back(
        region_rows, first_gain, first_shift, grad_region_in
    )
    in_gain_grad = in_gain_grad + gain_part
    in_shift_grad = in_shift_grad + shift_part
    region_grad = (grad_region_mid + grad_norm_region).astype(jnp.bfloat16)[None]
    qkv_bias_grad = jnp.stack([triple_sums[:D], triple_sums[2 * D :]])
    (
        in_gain_grad,
        in_shift_grad,
        qkv_grad,
        qkv_bias_grad,
        out_grad,
        out_bias_grad,
        mlp_gain_grad,
        mlp_shift_grad,
        up_grad,
        up_bias_grad,
        down_grad,
        down_bias_grad,
    ) = lax.psum(
        (
            in_gain_grad,
            in_shift_grad,
            qkv_grad,
            qkv_bias_grad,
            out_grad,
            out_bias_grad,
            mlp_gain_grad,
            mlp_shift_grad,
            up_grad,
            up_bias_grad,
            down_grad,
            down_bias_grad,
        ),
        ("win", "dp"),
    )
    return (
        patch_out,
        region_out,
        patch_grad,
        region_grad,
        in_gain_grad,
        in_shift_grad,
        qkv_grad,
        qkv_bias_grad,
        out_grad,
        out_bias_grad,
        mlp_gain_grad,
        mlp_shift_grad,
        up_grad,
        up_bias_grad,
        down_grad,
        down_bias_grad,
    )


def solution(mesh):
    in_specs = (
        P("dp", "win", None, None),
        P("dp", "win", None),
        P("dp", None),
        P(),
        P(),
        P(),
        P(),
        P(),
        P(),
        P(),
        P(),
        P(),
        P(),
        P(),
        P(),
        P("dp", "win", None, None),
        P("dp", "win", None),
    )
    out_specs = (
        P("dp", "win", None, None),
        P("dp", "win", None),
        P("dp", "win", None, None),
        P("dp", "win", None),
        P(),
        P(),
        P(),
        P(),
        P(),
        P(),
        P(),
        P(),
        P(),
        P(),
        P(),
        P(),
    )
    return jax.shard_map(shards, mesh=mesh, in_specs=in_specs, out_specs=out_specs, check_vma=False)
```

profile of v0, /device:TPU:0, one launch (start us, length us, event | category | flops | bytes accessed | tf_op | source)
XLA Modules:
  0.0 869.2 jit_solution(7070396460106512676)
XLA Ops:
  14.0 11.0 %all_gather.7 = bf16[384,512]{1,0:T(8,128)(2,1)S(1)} all-gather(bf16[48,512]{1,0:T(8,128)(2,1)S(1)} %get-tuple-element.103), channel_id=1, replica_groups=mesh['win'=8,'dp'=4] {'win'}, dimensions={0}, use_global_device_ids=true | all-gather | bytes 442368 | tf_op jit(solution)/shard_map/all_gather | solution.py:103
  26.8 9.5 %all_gather.6 = bf16[384,512]{1,0:T(8,128)(2,1)S(1)} all-gather(bf16[48,512]{1,0:T(8,128)(2,1)S(1)} %get-tuple-element.105), channel_id=1, replica_groups=mesh['win'=8,'dp'=4] {'win'}, dimensions={0}, use_global_device_ids=true | all-gather | bytes 442368 | tf_op jit(solution)/shard_map/all_gather | solution.py:104
  74.9 32.3 %reshape.380 = bf16[48,50,3,16,32]{4,3,2,1,0:T(8,128)(2,1)} reshape(bf16[2400,1536]{1,0:T(8,128)(2,1)} %add_convert_fusion.1) | data formatting | bytes 14745600 | tf_op jit(solution)/shard_map/reshape | solution.py:122
  107.2 22.4 %fusion.89 = (bf16[48,50,1,16,32]{4,3,2,1,0:T(8,128)(2,1)}, bf16[48,50,1,16,32]{4,3,2,1,0:T(8,128)(2,1)}, bf16[48,50,1,16,32]{4,3,2,1,0:T(8,128)(2,1)}) fusion(bf16[48,50,3,16,32]{4,3,2,1,0:T(8,128)(2,1)} %reshape.380), kind=kLoop, calls=%fused_computation.159 | loop fusion | bytes 14745600 | tf_op jit(solution)/shard_map/slice | solution.py:53
  129.6 14.0 %copy.154 = bf16[48,50,1,16,32]{1,4,3,0,2:T(8,128)(2,1)} copy(bf16[48,50,1,16,32]{4,3,2,1,0:T(8,128)(2,1)} %get-tuple-element.98) | data formatting | bytes 4915200
  143.6 13.9 %copy.155 = bf16[48,50,1,16,32]{1,4,3,0,2:T(8,128)(2,1)} copy(bf16[48,50,1,16,32]{4,3,2,1,0:T(8,128)(2,1)} %get-tuple-element.100) | data formatting | bytes 4915200
  157.5 13.6 %fusion.14 = f32[48,16,50,50]{2,3,1,0:T(8,128)} fusion(bf16[48,50,1,16,32]{1,4,3,0,2:T(8,128)(2,1)} %copy.155, bf16[48,50,1,16,32]{1,4,3,0,2:T(8,128)(2,1)} %copy.154), kind=kOutput, calls=%fused_computation.36 | convolution fusion | flops 122880000 | bytes 12595200 | tf_op jit(solution)/shard_map/wqhe,wkhe->whqk/dot_general | solution.py:51
  171.1 27.0 %fusion.93 = (f32[48,16,50]{2,1,0:T(8,128)S(1)}, f32[48,16,50,50]{2,3,1,0:T(8,128)}) fusion(f32[48,16,50,50]{2,3,1,0:T(8,128)} %fusion.14), kind=kOutput, calls=%fused_computation.163 | output fusion | flops 7680049 | bytes 15513600 | tf_op jit(solution)/shard_map/sub | solution.py:59
  198.1 14.1 %copy.153 = bf16[48,50,1,16,32]{1,4,3,0,2:T(8,128)(2,1)} copy(bf16[48,50,1,16,32]{4,3,2,1,0:T(8,128)(2,1)} %get-tuple-element.99) | data formatting | bytes 4915200
  212.2 14.0 %convert_bitcast_fusion = bf16[48,50,16,32]{1,3,2,0:T(8,128)(2,1)} fusion(bf16[48,50,1,16,32]{1,4,3,0,2:T(8,128)(2,1)} %copy.153, f32[48,16,50,50]{2,3,1,0:T(8,128)} %get-tuple-element.115, f32[48,16,50]{2,1,0:T(8,128)S(1)} %get-tuple-element.114), kind=kOutput, calls=%fused_computation.45 | convolution fusion | flops 127948800 | bytes 12748800 | tf_op jit(solution)/shard_map/whqk,wkhe->wqhe/dot_general | solution.py:124
  226.2 9.5 %copy.119 = bf16[48,50,16,32]{1,0,3,2:T(8,128)(2,1)} copy(bf16[48,50,16,32]{1,3,2,0:T(8,128)(2,1)} %convert_bitcast_fusion) | data formatting | bytes 4915200 | tf_op jit(solution)/shard_map/convert_element_type | solution.py:127
  260.7 51.1 %multiply_convert_fusion.1 = (bf16[2400,2048]{1,0:T(8,128)(2,1)}, f32[2400,2048]{1,0:T(8,128)}, f32[2400,2048]{1,0:T(8,128)}) fusion(f32[2048]{0:T(1024)S(1)} %convert_element_type.221, bf16[512,2048]{1,0:T(8,128)(2,1)S(1)} %copy-done, f32[2400,512]{1,0:T(8,128)} %copy-done.3, f32[512]{0:T(512)S(1)} %convert_element_type.219, ...), kind=kOutput, calls=%fused_computation.11 | convolution fusion | flops 5363712000 | bytes 56195840 | tf_op jit(solution)/shard_map/dot_general | solution.py:134
  311.8 23.0 %convert_reduce_fusion.1 = (f32[2048]{0:T(1024)}, bf16[2400,2048]{1,0:T(8,128)(2,1)}) fusion(f32[2400,2048]{1,0:T(8,128)} %get-tuple-element.97, bf16[2400,512]{1,0:T(8,128)(2,1)S(1)} %copy-done.6, bf16[2048,512]{1,0:T(8,128)(2,1)} %param.30, f32[2400,2048]{1,0:T(8,128)} %get-tuple-element.118, f32[2048]{0:T(1024)S(1)} %convert_element_type.221), kind=kOutput, calls=%fused_computation.9 | convolution fusion | flops 5116721152 | bytes 53723136 | tf_op jit(solution)/shard_map/nd,fd->nf/dot_general | solution.py:148
  334.8 11.5 %multiply_reduce_fusion.2 = (f32[512]{0:T(512)}, f32[2400]{0:T(1024)S(1)}, f32[512]{0:T(512)}, f32[2400,512]{1,0:T(8,128)S(1)}) fusion(f32[2400,512]{1,0:T(8,128)S(1)} %copy-done.4, f32[2400]{0:T(1024)S(1)} %fusion.70, f32[2400]{0:T(1024)S(1)} %broadcast_multiply_fusion.1, f32[512]{0:T(512)S(1)} %convert_element_type.218, ...), kind=kOutput, calls=%fused_computation.53 | convolution fusion | flops 5042991616 | bytes 21792896 | tf_op jit(solution)/shard_map/nf,df->nd/dot_general | solution.py:152
  355.2 11.8 %reshape.381 = bf16[48,50,16,32]{3,2,1,0:T(8,128)(2,1)} reshape(bf16[2400,512]{1,0:T(8,128)(2,1)} %convolution_convert_fusion) | data formatting | bytes 4915200 | tf_op jit(solution)/shard_map/reshape | solution.py:165
  367.0 14.0 %copy.122 = bf16[48,50,16,32]{1,3,2,0:T(8,128)(2,1)} copy(bf16[48,50,16,32]{3,2,1,0:T(8,128)(2,1)} %reshape.381) | data formatting | bytes 4915200 | tf_op jit(solution)/shard_map/reshape | solution.py:165
  381.0 21.6 %multiply_reduce_fusion = (f32[48,16,50]{2,1,0:T(8,128)S(1)}, f32[48,16,50,50]{2,3,1,0:T(8,128)}) fusion(f32[48,16,50,50]{2,3,1,0:T(8,128)} %get-tuple-element.115, f32[48,16,50]{2,1,0:T(8,128)S(1)} %copy-done.24, bf16[48,50,16,32]{1,3,2,0:T(8,128)(2,1)} %copy.122, bf16[48,50,1,16,32]{1,4,3,0,2:T(8,128)(2,1)} %copy.153), kind=kOutput, calls=%fused_computation.6 | convolution fusion | flops 128601600 | bytes 20582400 | tf_op jit(solution)/shard_map/wqhe,wkhe->whqk/dot_general | solution.py:169
  402.6 18.6 %multiply_convert_fusion = bf16[48,16,50,50]{2,3,1,0:T(8,128)(2,1)} fusion(f32[48,16,50,50]{2,3,1,0:T(8,128)} %get-tuple-element.121, f32[48,16,50]{2,1,0:T(8,128)S(1)} %get-tuple-element.120, f32[48,16,50,50]{2,3,1,0:T(8,128)} %get-tuple-element.115, f32[48,16,50]{2,1,0:T(8,128)S(1)} %copy-done.24), kind=kLoop, calls=%fused_computation.5 | loop fusion | flops 7680000 | bytes 19507200 | tf_op jit(solution)/shard_map/convert_element_type | solution.py:178
  421.2 11.9 %multiply_bitcast_fusion.1 = bf16[48,50,1,16,32]{1,4,3,0,2:T(8,128)(2,1)} fusion(bf16[48,16,50,50]{2,3,1,0:T(8,128)(2,1)} %multiply_convert_fusion, bf16[48,50,1,16,32]{1,4,3,0,2:T(8,128)(2,1)} %copy.155), kind=kOutput, calls=%fused_computation.29 | convolution fusion | flops 125337600 | bytes 8755200 | tf_op jit(solution)/shard_map/whqk,wkhe->wqhe/dot_general | solution.py:180
  433.1 11.5 %multiply_bitcast_fusion = bf16[48,50,1,16,32]{1,4,3,0,2:T(8,128)(2,1)} fusion(bf16[48,16,50,50]{2,3,1,0:T(8,128)(2,1)} %multiply_convert_fusion, bf16[48,50,1,16,32]{1,4,3,0,2:T(8,128)(2,1)} %copy.154), kind=kOutput, calls=%fused_computation.28 | convolution fusion | flops 125337600 | bytes 8755200 | tf_op jit(solution)/shard_map/whqk,wqhe->wkhe/dot_general | solution.py:189
  444.5 13.8 %fusion.27 = bf16[48,50,1,16,32]{1,4,3,0,2:T(8,128)(2,1)} fusion(bf16[48,50,16,32]{1,3,2,0:T(8,128)(2,1)} %copy.122, f32[48,16,50,50]{2,3,1,0:T(8,128)} %get-tuple-element.115, f32[48,16,50]{2,1,0:T(8,128)S(1)} %copy-done.24), kind=kOutput, calls=%fused_computation.68 | convolution fusion | flops 126720000 | bytes 12748800 | tf_op jit(solution)/shard_map/whqk,wqhe->wkhe/dot_general | solution.py:197
  458.4 13.2 %convert_reduce_fusion = (f32[3,16,32]{2,1,0:T(8,128)}, bf16[48,50,3,16,32]{1,4,3,0,2:T(8,128)(2,1)S(1)}) fusion(bf16[48,50,1,16,32]{1,4,3,0,2:T(8,128)(2,1)} %fusion.27, bf16[48,50,1,16,32]{1,4,3,0,2:T(8,128)(2,1)} %multiply_bitcast_fusion, bf16[48,50,1,16,32]{1,4,3,0,2:T(8,128)(2,1)} %multiply_bitcast_fusion.1), kind=kLoop, calls=%fused_computation.3 | loop fusion | flops 14744064 | bytes 14751744 | tf_op jit(solution)/shard_map/reduce_sum | solution.py:63
  471.5 12.8 %copy.127 = bf16[48,50,3,16,32]{1,0,4,3,2:T(8,128)(2,1)} copy(bf16[48,50,3,16,32]{1,4,3,0,2:T(8,128)(2,1)S(1)} %get-tuple-element.91) | data formatting | bytes 14745600 | tf_op jit(solution)/shard_map/convert_element_type | solution.py:206
  484.3 25.4 %convert_element_type.231 = bf16[2400,1536]{0,1:T(8,128)(2,1)} reshape(bf16[48,50,3,16,32]{1,0,4,3,2:T(8,128)(2,1)} %copy.127) | data formatting | bytes 14745600 | tf_op jit(solution)/shard_map/convert_element_type | solution.py:206
  509.8 11.8 %multiply_reduce_fusion.3 = (f32[512]{0:T(512)}, f32[2400]{0:T(1024)S(1)}, f32[512]{0:T(512)}, f32[2400,512]{1,0:T(8,128)S(1)}) fusion(f32[2400,512]{1,0:T(8,128)} %reshape.366, f32[2400]{0:T(1024)S(1)} %copy-done.53, f32[2400]{0:T(1024)S(1)} %copy-done.55, f32[512]{0:T(512)S(1)} %copy-done.39, bf16[2400,1536]{0,1:T(8,128)(2,1)} %convert_element_type.231, ...), kind=kOutput, calls=%fused_computation.56 | convolution fusion | flops 3784700672 | bytes 18811008 | tf_op jit(solution)/shard_map/ne,de->nd/dot_general | solution.py:210
  542.4 13.2 %fusion.81 = f32[512,2048]{1,0:T(8,128)} fusion(bf16[2400,2048]{1,0:T(8,128)(2,1)} %get-tuple-element.127, f32[2400,512]{1,0:T(8,128)} %copy-done.3, f32[512]{0:T(512)S(1)} %copy-done.77, f32[512]{0:T(512)S(1)} %copy-done.69, f32[2400]{0:T(1024)S(1)} %copy-done.51, f32[2400]{0:T(1024)S(1)} %copy-done.42), kind=kOutput, calls=%fused_computation.153 | convolution fusion | flops 5039308800 | bytes 18963200 | tf_op jit(solution)/shard_map/nd,nf->df/dot_general | solution.py:150
  565.1 10.0 %fusion.95 = f32[512,1536]{1,0:T(8,128)} fusion(bf16[2400,512]{1,0:T(8,128)(2,1)} %convert_element_type.243, bf16[2400,1536]{0,1:T(8,128)(2,1)} %convert_element_type.231), kind=kOutput, calls=%fused_computation.165 | convolution fusion | flops 3774873600 | bytes 12976128 | tf_op jit(solution)/shard_map/nd,ne->de/dot_general | solution.py:208
  575.1 9.7 %fusion.97 = f32[2048,512]{1,0:T(8,128)} fusion(bf16[2400,2048]{1,0:T(8,128)(2,1)} %get-tuple-element.96, bf16[2400,512]{1,0:T(8,128)(2,1)S(1)} %copy-done.8), kind=kOutput, calls=%fused_computation.167 | convolution fusion | flops 5033164800 | bytes 16482304 | tf_op jit(solution)/shard_map/nf,nd->fd/dot_general | solution.py:146
  587.6 23.8 %reduce-scatter.9.cloned.1.call-done = bf16[48,512]{1,0:T(8,128)(2,1)} async-done(((bf16[384,512]{1,0:T(8,128)(2,1)}), bf16[48,512]{1,0:T(8,128)(2,1)}) %reduce-scatter.9.cloned.1.call-update) | async-done | bytes 49168 | tf_op jit(solution)/shard_map/reduce_scatter | solution.py:266
  622.6 11.8 %add_convert_fusion.3 = bf16[2400,512]{1,0:T(8,128)(2,1)} fusion(f32[2400,512]{1,0:T(8,128)S(1)} %bitcast.181, bf16[2400,2048]{1,0:T(8,128)(2,1)} %get-tuple-element.96, bf16[2048,512]{1,0:T(8,128)(2,1)S(1)} %copy-done.83, f32[512]{0:T(512)S(1)} %convert_element_type.223), kind=kOutput, calls=%fused_computation.61 | convolution fusion | flops 5036851200 | bytes 19302400 | tf_op jit(solution)/shard_map/dot_general | solution.py:139
  648.5 41.8 %all-reduce = (f32[512]{0:T(512)}, f32[512]{0:T(512)}, f32[2,512]{1,0:T(2,128)}, f32[512]{0:T(512)}, f32[512]{0:T(512)}, /*index=5*/f32[512]{0:T(512)}, f32[2048]{0:T(1024)}, f32[512]{0:T(512)}) all-reduce(f32[512]{0:T(512)S(1)} %add.216, f32[512]{0:T(512)S(1)} %add.217, ...), channel_id=1, replica_groups=mesh['win'=8,'dp'=4] {'win','dp'}, use_global_device_ids=true, to_apply=%region_22.23 | all-reduce | flops 6144 | bytes 49152 | tf_op jit(solution)/shard_map/psum | solution.py:300
  690.3 161.8 %all-reduce.4.cloned.1.call-done = (f32[512,1536]{1,0:T(8,128)}, f32[512,512]{1,0:T(8,128)}, f32[512,2048]{1,0:T(8,128)}, f32[2048,512]{1,0:T(8,128)}) async-done(((f32[512,1536]{1,0:T(8,128)}, f32[512,512]{1,0:T(8,128)}, f32[512,2048]{1,0:T(8,128)}, f32[2048,512]{1,0:T(8,128)}), (f32[512,1536]{1,0:T(8,128)}, f32[512,512]{1,0:T(8,128)}, f32[512,2048]{1,0:T(8,128)}, ...) | async-done | bytes 12582928 | tf_op jit(solution)/shard_map/psum | solution.py:300
  (283 shorter events, 148.4 us)
Async XLA Ops:
  7.2 253.5 %copy-start = (bf16[512,2048]{1,0:T(8,128)(2,1)S(1)}, bf16[512,2048]{1,0:T(8,128)(2,1)}, u32[]{:S(2)}) copy-start(bf16[512,2048]{1,0:T(8,128)(2,1)} %param.28) | copy-start | bytes 6291460
  7.2 580.4 %reduce-scatter.7.cloned.1.call-start = ((), (), s32[]{:S(2)}) async-start(), calls=%async_computation.2 | async-start | bytes 442368 | tf_op jit(solution)/shard_map/reduce_scatter | solution.py:263
  8.3 28.1 %copy-start.60 = (f32[48]{0:T(128)}, f32[48]{0:T(128)S(1)}, u32[]{:S(2)}) copy-start(f32[48]{0:T(128)S(1)} %broadcast_multiply_fusion.2) | copy-start | bytes 580
  10.6 55.6 %copy-start.38 = (f32[512]{0:T(512)}, f32[512]{0:T(512)S(1)}, u32[]{:S(2)}) copy-start(f32[512]{0:T(512)S(1)} %convert_element_type.200) | copy-start | bytes 6148
  12.0 54.1 %copy-start.56 = (f32[512]{0:T(512)}, f32[512]{0:T(512)S(1)}, u32[]{:S(2)}) copy-start(f32[512]{0:T(512)S(1)} %convert_element_type.201) | copy-start | bytes 6148
  25.2 19.0 %copy-start.25 = (bf16[384,512]{0,1:T(8,128)(2,1)}, bf16[384,512]{0,1:T(8,128)(2,1)S(1)}, u32[]{:S(2)}) copy-start(bf16[384,512]{0,1:T(8,128)(2,1)S(1)} %copy.109) | copy-start | bytes 1179652
  25.4 18.8 %copy-start.32 = (bf16[48,512]{0,1:T(8,128)(2,1)}, bf16[48,512]{0,1:T(8,128)(2,1)S(1)}, u32[]{:S(2)}) copy-start(bf16[48,512]{0,1:T(8,128)(2,1)S(1)} %copy.146) | copy-start | bytes 147460
  198.1 14.1 %copy-start.23 = (f32[48,16,50]{2,1,0:T(8,128)}, f32[48,16,50]{2,1,0:T(8,128)S(1)}, u32[]{:S(2)}) copy-start(f32[48,16,50]{2,1,0:T(8,128)S(1)} %get-tuple-element.114) | copy-start | bytes 460804
  249.8 96.5 %copy-start.41 = (f32[2400]{0:T(1024)}, f32[2400]{0:T(1024)S(1)}, u32[]{:S(2)}) copy-start(f32[2400]{0:T(1024)S(1)} %broadcast_multiply_fusion.1) | copy-start | bytes 28804
  250.8 95.5 %copy-start.50 = (f32[2400]{0:T(1024)}, f32[2400]{0:T(1024)S(1)}, u32[]{:S(2)}) copy-start(f32[2400]{0:T(1024)S(1)} %fusion.70) | copy-start | bytes 28804
  250.9 95.5 %copy-start.68 = (f32[512]{0:T(512)}, f32[512]{0:T(512)S(1)}, u32[]{:S(2)}) copy-start(f32[512]{0:T(512)S(1)} %convert_element_type.218) | copy-start | bytes 6148
  250.9 9.8 %copy-start.76 = (f32[512]{0:T(512)}, f32[512]{0:T(512)S(1)}, u32[]{:S(2)}) copy-start(f32[512]{0:T(512)S(1)} %convert_element_type.219) | copy-start | bytes 6148
  260.6 51.1 %copy-start.6 = (bf16[2400,512]{1,0:T(8,128)(2,1)S(1)}, bf16[2400,512]{1,0:T(8,128)(2,1)}, u32[]{:S(2)}) copy-start(bf16[2400,512]{1,0:T(8,128)(2,1)} %reshape.369) | copy-start | bytes 7372804
  311.7 23.0 %copy-start.4 = (f32[2400,512]{1,0:T(8,128)S(1)}, f32[2400,512]{1,0:T(8,128)}, u32[]{:S(2)}) copy-start(f32[2400,512]{1,0:T(8,128)} %copy-done.3) | copy-start | bytes 14745604
  334.8 11.5 %copy-start.46 = (f32[2400]{0:T(1024)S(1)}, f32[2400]{0:T(1024)}, u32[]{:S(2)}) copy-start(f32[2400]{0:T(1024)} %copy-done.45) | copy-start | bytes 28804
  367.0 14.0 %copy-start.24 = (f32[48,16,50]{2,1,0:T(8,128)S(1)}, f32[48,16,50]{2,1,0:T(8,128)}, u32[]{:S(2)}) copy-start(f32[48,16,50]{2,1,0:T(8,128)} %copy-done.23) | copy-start | bytes 460804
  484.3 25.4 %copy-start.12 = (bf16[512,1536]{1,0:T(8,128)(2,1)S(1)}, bf16[512,1536]{1,0:T(8,128)(2,1)}, u32[]{:S(2)}) copy-start(bf16[512,1536]{1,0:T(8,128)(2,1)} %param.22) | copy-start | bytes 4718596
  484.3 25.4 %copy-start.39 = (f32[512]{0:T(512)S(1)}, f32[512]{0:T(512)}, u32[]{:S(2)}) copy-start(f32[512]{0:T(512)} %copy-done.38) | copy-start | bytes 6148
  484.3 25.5 %copy-start.53 = (f32[2400]{0:T(1024)S(1)}, f32[2400]{0:T(1024)}, u32[]{:S(2)}) copy-start(f32[2400]{0:T(1024)} %copy-done.52) | copy-start | bytes 28804
  484.3 25.5 %copy-start.55 = (f32[2400]{0:T(1024)S(1)}, f32[2400]{0:T(1024)}, u32[]{:S(2)}) copy-start(f32[2400]{0:T(1024)} %copy-done.54) | copy-start | bytes 28804
  484.3 37.3 %slice-start = ((s8[4915200]{0:T(1024)(128)(4,1)}), s8[720896]{0:T(1024)(128)(4,1)S(1)}, s32[]{:S(2)}) async-start(s8[4915200]{0:T(1024)(128)(4,1)} %bitcast.178), calls=%async_computation.5 | async-start | bytes 1441792
  509.8 11.8 %copy-start.48 = (f32[2400]{0:T(1024)S(1)}, f32[2400]{0:T(1024)}, u32[]{:S(2)}) copy-start(f32[2400]{0:T(1024)} %copy-done.47) | copy-start | bytes 28804
  509.8 11.8 %slice-start.1 = ((s8[4915200]{0:T(1024)(128)(4,1)}), s8[4194304]{0:T(1024)(128)(4,1)S(1)}, s32[]{:S(2)}) async-start(s8[4915200]{0:T(1024)(128)(4,1)} %bitcast.178), calls=%async_computation.6 | async-start | bytes 8388608
  539.6 71.8 %reduce-scatter.9.cloned.1.call-start = ((), (), s32[]{:S(2)}) async-start(), calls=%async_computation.3 | async-start | bytes 442368 | tf_op jit(solution)/shard_map/reduce_scatter | solution.py:266
  542.1 310.1 %all-reduce.4.cloned.1.call-start = ((), (), s32[]{:S(2)}) async-start(), calls=%async_computation.4 | async-start | bytes 25165824 | tf_op jit(solution)/shard_map/psum | solution.py:300
  565.1 10.0 %copy-start.8 = (bf16[2400,512]{1,0:T(8,128)(2,1)S(1)}, bf16[2400,512]{1,0:T(8,128)(2,1)}, u32[]{:S(2)}) copy-start(bf16[2400,512]{1,0:T(8,128)(2,1)} %reshape.369) | copy-start | bytes 7372804
  575.1 9.7 %copy-start.22 = (bf16[2400,512]{1,0:T(8,128)(2,1)S(1)}, bf16[2400,512]{1,0:T(8,128)(2,1)}, u32[]{:S(2)}) copy-start(bf16[2400,512]{1,0:T(8,128)(2,1)} %copy-done.21) | copy-start | bytes 7372804
  584.8 26.6 %copy-start.20 = (bf16[1,48,512]{2,1,0:T(8,128)(2,1)S(1)}, bf16[1,48,512]{2,1,0:T(8,128)(2,1)}, u32[]{:S(2)}) copy-start(bf16[1,48,512]{2,1,0:T(8,128)(2,1)} %param.18) | copy-start | bytes 147460
  584.8 26.6 %copy-start.40 = (f32[512]{0:T(512)S(1)}, f32[512]{0:T(512)}, u32[]{:S(2)}) copy-start(f32[512]{0:T(512)} %copy-done.38) | copy-start | bytes 6148
  584.8 26.6 %copy-start.57 = (f32[512]{0:T(512)S(1)}, f32[512]{0:T(512)}, u32[]{:S(2)}) copy-start(f32[512]{0:T(512)} %copy-done.56) | copy-start | bytes 6148
  584.8 26.6 %copy-start.61 = (f32[48]{0:T(128)S(1)}, f32[48]{0:T(128)}, u32[]{:S(2)}) copy-start(f32[48]{0:T(128)} %copy-done.60) | copy-start | bytes 580
  584.8 26.6 %copy-start.66 = (f32[48]{0:T(128)S(1)}, f32[48]{0:T(128)}, u32[]{:S(2)}) copy-start(f32[48]{0:T(128)} %copy-done.65) | copy-start | bytes 580
  (59 other events, 265.7 us)
Sparse Core Ops, SparseCore 0:
  539.7 34.1 reduce-scatter.6
  577.5 33.8 reduce-scatter.8
  618.9 233.1 all-reduce.3
where the time goes:
time: 877 us; the launch traced here: 869 us
  matrix products  262 us (30%)
  local copies, waits for them, and re-layouts  252 us (29%)
  waiting for transfers between devices  186 us (21%)
  other arithmetic  91.2 us (10%)
  blocking collectives  62.4 us (7%)
  between operations  15.4 us (2%)
    psum x1, waiting for transfers between devices, shards(): lax.psum((in_gain_grad, in_shift_grad, qkv_grad, qkv_bias_grad, out_grad,...  162 us
    unnamed x188, local copies, waits for them, and re-layouts  65 us
    dot_general x1, matrix products, shards(): jnp.dot(mlp_in, w_up, preferred_element_type=jnp.float32)  51.1 us
    psum x1, blocking collectives, shards(): lax.psum((in_gain_grad, in_shift_grad, qkv_grad, qkv_bias_grad, out_grad,...  41.8 us
    convert_element_type x2, local copies, waits for them, and re-layouts, shards(): grad_triple = jnp.stack([grad_query, grad_keys, grad_values], axis=2).res...  38.2 us
    reshape x1, local copies, waits for them, and re-layouts, shards(): project(local_in, w_qkv, bias_row)  32.3 us
    sub x1, other arithmetic, local_probs_of(): return jax.nn.softmax(scores, axis=-1)  27 us
    reshape x2, local copies, waits for them, and re-layouts, shards(): grad_local_merged.astype(jnp.bfloat16)  25.8 us
  transfers between devices with their start and end apart: 3, of which 2 were waited for; matrix products, arithmetic and copies ran while one was open for 9% of the time, Pallas kernels for 0%

commit v1 on v0

v1 whole, which is shorter than its diff:
```python
import functools

import jax
import jax.numpy as jnp
from jax import lax
from jax.experimental import pallas as pl
from jax.experimental.pallas import tpu as pltpu
from jax.sharding import PartitionSpec as P

D = 512
HEADS = 16
HD = 32
FF = 2048
EPSILON = 1e-06
MASKED_SCORE = -1e30
SCALING = HD ** (-0.5)
LOG2E = 1.4426950408889634
TP = 64
WC = 16
f32 = jnp.float32
bf16 = jnp.bfloat16
VMEM_LIMIT = 60 * 2**20
MESH = pl.DeviceIdType.MESH


def nn(a, b):
    return lax.dot_general(a, b, (((1,), (0,)), ((), ())), preferred_element_type=f32)


def nt(a, b):
    return lax.dot_general(a, b, (((1,), (1,)), ((), ())), preferred_element_type=f32)


def tn(a, b):
    return lax.dot_general(a, b, (((0,), (0,)), ((), ())), preferred_element_type=f32)


def call(body, grid, ins, outs, scratch=(), name=None, collective_id=None):
    def spec(block, index):
        if block is None:
            return pl.BlockSpec(memory_space=pl.ANY)
        if index is None:
            return pl.BlockSpec(block, lambda *_: (0,) * len(block), pipeline_mode=pl.Buffered(1))
        return pl.BlockSpec(block, index)

    return pl.pallas_call(
        body,
        grid=grid,
        in_specs=[spec(b, i) for _, b, i in ins],
        out_specs=[spec(b, i) for _, b, i in outs],
        out_shape=[jax.ShapeDtypeStruct(s, d) for (s, d), _, _ in outs],
        scratch_shapes=list(scratch),
        compiler_params=pltpu.CompilerParams(
            vmem_limit_bytes=VMEM_LIMIT, collective_id=collective_id, has_side_effects=collective_id is not None
        ),
        name=name,
    )(*[a for a, _, _ in ins])


def whole(a):
    return (a, a.shape, None)


def whole_out(shape, dtype):
    return ((shape, dtype), shape, lambda *_: (0,) * len(shape))


def left(a):
    return (a, None, None)


def left_out(shape, dtype):
    return ((shape, dtype), None, None)


def norm_stats(rows):
    average = jnp.mean(rows, axis=-1, keepdims=True)
    centred = rows - average
    spread = jnp.mean(centred * centred, axis=-1, keepdims=True)
    inverse = lax.rsqrt(spread + EPSILON)
    return centred * inverse, inverse


def norm_back(vhat, inverse, gain, grad_out):
    scaled = grad_out * gain
    first = jnp.mean(scaled, axis=-1, keepdims=True)
    second = jnp.mean(scaled * vhat, axis=-1, keepdims=True)
    return inverse * (scaled - first - vhat * second)


def col(x):
    return jnp.sum(x, axis=0, keepdims=True)


class Place:
    def __init__(self, wins, dps):
        self.wins, self.dps = wins, dps
        self.win = lax.axis_index("win")
        self.dp = lax.axis_index("dp")
        self.core = lax.rem(self.win, 2)
        self.chip = self.win // 2
        self.chips = wins // 2

    def other_core(self):
        return {"win": self.chip * 2 + 1 - self.core}

    def at_chip(self, j):
        chip = lax.rem(self.chip + j, self.chips)
        return chip, {"win": chip * 2 + self.core}

    def at_dp(self, j):
        dp = lax.rem(self.dp + j, self.dps)
        return dp, {"dp": dp}

    def greet(self, all_wins=False):
        barrier = pltpu.get_barrier_semaphore()
        if all_wins:
            for j in range(1, self.wins):
                pl.semaphore_signal(barrier, inc=1, device_id={"win": lax.rem(self.win + j, self.wins)}, device_id_type=MESH)
        else:
            pl.semaphore_signal(barrier, inc=1, device_id=self.other_core(), device_id_type=MESH)
            for j in range(1, self.chips):
                pl.semaphore_signal(barrier, inc=1, device_id=self.at_chip(j)[1], device_id_type=MESH)
        for j in range(1, self.dps):
            pl.semaphore_signal(barrier, inc=1, device_id=self.at_dp(j)[1], device_id_type=MESH)

    def greeted(self, all_wins=False):
        near = self.wins - 1 if all_wins else self.chips
        pl.semaphore_wait(pltpu.get_barrier_semaphore(), near + self.dps - 1)


def rows_of(wins, dps):
    half = D // 2
    piece = half // (wins // 2)
    last = piece // dps if piece % (16 * dps) == 0 else piece
    return half, piece, last


def stream_scratch(wins, dps, columns):
    half, piece, last = rows_of(wins, dps)
    chips = wins // 2
    return [
        pltpu.VMEM((half, columns), bf16),
        pltpu.VMEM((half, columns), bf16),
        pltpu.VMEM((max(chips - 1, 1), piece, columns), bf16),
        pltpu.VMEM((piece, columns), bf16),
        pltpu.VMEM((max(dps - 1, 1), last, columns), bf16),
        pltpu.VMEM((piece, columns), bf16),
        pltpu.SemaphoreType.DMA((6 + 4 * chips + 4 * dps,)),
    ]


class Stream:
    PARTS = 7

    def __init__(self, place, source, final, refs, first=None):
        self.p = place
        self.source, self.final = source, final
        self.own, self.r1, self.r2, self.s, self.r3, self.s2, self.sem = refs
        self.half, self.piece, self.last = rows_of(place.wins, place.dps)
        self.split = self.last != self.piece
        self.slabs = self.half // 16
        self.columns = self.own.shape[1]

    def rows(self, start, size):
        return pl.ds(pl.multiple_of(start, 16), size)

    def remote(self, src, dst, to, k):
        return pltpu.make_async_remote_copy(
            src_ref=src, dst_ref=dst, send_sem=self.sem.at[2 * k], recv_sem=self.sem.at[2 * k + 1],
            device_id=to, device_id_type=MESH,
        )

    def _own(self):
        mine = self.rows(self.p.core * self.half, self.half)
        return pltpu.make_async_copy(self.source.at[mine], self.own, self.sem.at[0])

    def _put(self):
        mine = self.rows(self.p.core * self.half + self.p.chip * self.piece, self.piece)
        return pltpu.make_async_copy(self.s2, self.final.at[mine], self.sem.at[1])

    def _cores(self):
        other = self.rows((1 - self.p.core) * self.half, self.half)
        return [self.remote(self.source.at[other], self.r1, self.p.other_core(), 1)]

    def _chips(self):
        out = []
        for j in range(1, self.p.chips):
            chip, to = self.p.at_chip(j)
            out.append(self.remote(self.own.at[self.rows(chip * self.piece, self.piece)], self.r2.at[j - 1], to, 2 + j))
        return out

    def _dps(self):
        out = []
        for j in range(1, self.p.dps):
            dp, to = self.p.at_dp(j)
            src = self.s.at[self.rows(dp * self.last, self.last)] if self.split else self.s
            out.append(self.remote(src, self.r3.at[j - 1], to, 2 + self.p.chips + j))
        return out

    def _dps_back(self):
        out = []
        if self.split:
            for j in range(1, self.p.dps):
                mine = self.s2.at[self.rows(self.p.dp * self.last, self.last)]
                out.append(self.remote(mine, mine, self.p.at_dp(j)[1], 2 + self.p.chips + self.p.dps + j))
        return out

    def _chips_back(self):
        out = []
        for j in range(1, self.p.chips):
            mine = self.final.at[self.rows(self.p.core * self.half + self.p.chip * self.piece, self.piece)]
            out.append(self.remote(self.s2, mine, self.p.at_chip(j)[1], 2 + self.p.chips + 2 * self.p.dps + j))
        return out

    def _cores_back(self):
        mine = self.final.at[self.rows(self.p.core * self.half, self.half)]
        return [self.remote(mine, mine, self.p.other_core(), 2)]

    def start(self, copies):
        for c in copies:
            c.start()

    def wait(self, copies):
        for c in copies:
            c.wait()

    def load(self):
        self._own().start()

    def send_cores(self):
        self.start(self._cores())

    def send_chips(self):
        self._own().wait()
        self.wait(self._cores())

        def add(i, carry):
            at = self.rows(i * 16, 16)
            self.own[at] = (self.own[at].astype(f32) + self.r1[at].astype(f32)).astype(bf16)
            return carry

        lax.fori_loop(0, self.half // 16, add, 0)
        self.start(self._chips())

    def send_dps(self):
        self.wait(self._chips())

        def add(i, carry):
            at = self.rows(i * 16, 16)
            total = self.own[self.rows(self.p.chip * self.piece + i * 16, 16)].astype(f32)
            for j in range(self.p.chips - 1):
                total += self.r2[j, at].astype(f32)
            self.s[at] = total.astype(bf16)
            return carry

        lax.fori_loop(0, self.piece // 16, add, 0)
        self.start(self._dps())

    def send_dps_back(self):
        self.wait(self._dps())

        def add(i, carry):
            mine = self.rows((self.p.dp * self.last if self.split else 0) + i * 16, 16)
            total = self.s[mine].astype(f32)
            for j in range(self.p.dps - 1):
                total += self.r3[j, self.rows(i * 16, 16)].astype(f32)
            self.s2[mine] = total.astype(bf16)
            return carry

        lax.fori_loop(0, self.last // 16, add, 0)
        self.start(self._dps_back())

    def send_chips_back(self):
        self.wait(self._dps_back())
        self._put().start()
        self.start(self._chips_back())

    def send_cores_back(self):
        self._put().wait()
        self.wait(self._chips_back())
        self.start(self._cores_back())

    def finish(self):
        self.wait(self._cores_back())


def region_in_kernel(regional, gain, shift, w_qkv, bias, region_in, triple):
    vhat, _ = norm_stats(regional[...].astype(f32))
    normed = (vhat * gain[...] + shift[...]).astype(bf16)
    region_in[...] = normed
    triple[...] = (nn(normed, w_qkv[...]) + bias[...]).astype(bf16)


def patch_proj_kernel(patches, gain, shift, w_qkv, bias, triple):
    rows = patches.shape[0] * patches.shape[1]
    vhat, _ = norm_stats(patches[...].reshape(rows, D).astype(f32))
    normed = (vhat * gain[...] + shift[...]).astype(bf16)
    out = (nn(normed, w_qkv[...]) + bias[...]).astype(bf16)
    triple[...] = out.reshape(triple.shape)


def expand_group(x, heads):
    lane = lax.broadcasted_iota(jnp.int32, (1, x.shape[1]), 1) // HD
    return jnp.concatenate([jnp.where(lane == i, x, jnp.zeros_like(x)) for i in range(heads)], axis=0)


def fold_group(y, heads):
    rows = y.shape[0] // heads
    lane = lax.broadcasted_iota(jnp.int32, (1, y.shape[1]), 1) // HD
    total = y[(heads - 1) * rows :]
    for i in range(heads - 2, -1, -1):
        total = jnp.where(lane == i, y[i * rows : (i + 1) * rows], total)
    return total


def region_attn_kernel(
    triple, gathered, image_col, image_row, regional, gain, shift, w_qkv, bias, w_out, out_bias,
    probs, merged, region_mid, triple0,
):
    count = triple.shape[0]
    width = 8 * count
    for g in range(2):
        lanes = slice(256 * g, 256 * g + 256)
        queries = expand_group(triple[:, lanes], 8)
        scores = nt(gathered[:, lanes], queries)
        same = image_col[...] == image_row[:, g * width : (g + 1) * width]
        scores = jnp.where(same, scores * SCALING, MASKED_SCORE)
        top = jnp.max(scores, axis=0, keepdims=True)
        exps = jnp.exp2((scores - top) * LOG2E)
        low = (exps * (1.0 / col(exps))).astype(bf16)
        probs[g] = low
        merged[:, lanes] = fold_group(tn(low, gathered[:, D + 256 * g : D + 256 * g + 256]), 8).astype(bf16)
    mid = regional[...].astype(f32) + nn(merged[...], w_out[...]) + out_bias[...]
    region_mid[...] = mid
    vhat, _ = norm_stats(mid)
    normed = (vhat * gain[...] + shift[...]).astype(bf16)
    triple0[...] = (nn(normed, w_qkv[...]) + bias[...]).astype(bf16)


def expand(x):
    lane = lax.broadcasted_iota(jnp.int32, (1, 128), 1) // HD
    return jnp.concatenate([jnp.where(lane == i, x, jnp.zeros_like(x)) for i in range(4)], axis=0)


def query_side(rows, weights):
    lane = lax.broadcasted_iota(jnp.int32, (1, 128), 1) // HD
    out = tn(rows, weights)
    pairs = jnp.concatenate([out[0:64, 0:128], out[64:128, 128:256]], axis=0).T
    return jnp.where(lane % 2 == 0, pairs[0:64], pairs[64:128])


def load_triple(t, triple, triple0, patch):
    for b in range(12):
        lanes = slice(128 * b, 128 * b + 128)
        t[b, 0 : patch * WC] = triple[:, :, lanes].reshape(patch * WC, 128).astype(f32)
        t[b, patch * WC : (patch + 1) * WC] = triple0[:, lanes].astype(f32)
        t[b, (patch + 1) * WC :] = jnp.zeros(((TP - patch - 1) * WC, 128), f32)


def local_fwd_kernel(triple, triple0, merged, probs, t, m):
    patch = triple.shape[0]
    load_triple(t, triple, triple0, patch)
    row = lax.broadcasted_iota(jnp.int32, (TP, 1), 0)

    def one(w):
        for b in range(4):
            q = t[b, pl.ds(w, TP, stride=WC), :].astype(bf16)
            k = t[4 + b, pl.ds(w, TP, stride=WC), :].astype(bf16)
            v = t[8 + b, pl.ds(w, TP, stride=WC), :].astype(bf16)
            scores = nt(k, expand(q))
            scores = jnp.where(row <= patch, scores, MASKED_SCORE)
            top = jnp.max(scores, axis=0, keepdims=True)
            exps = jnp.exp2((scores - top) * (SCALING * LOG2E))
            low = (exps * (1.0 / col(exps))).astype(bf16)
            probs[w, :, 256 * b : 256 * b + 256] = low
            m[b, pl.ds(w, TP, stride=WC), :] = query_side(v, low)

    def body(i, carry):
        for u in range(4):
            one(i * 4 + u)
        return carry

    lax.fori_loop(0, WC // 4, body, 0)
    for b in range(4):
        merged[:, :, 128 * b : 128 * b + 128] = m[b, 0 : (patch + 1) * WC].astype(bf16).reshape(patch + 1, WC, 128)


def local_bwd_step(w, probs, t, d):
    at = pl.ds(w, TP, stride=WC)
    for b in range(4):
        q = t[b, at, :].astype(bf16)
        k = t[4 + b, at, :].astype(bf16)
        v = t[8 + b, at, :].astype(bf16)
        g = t[12 + b, at, :].astype(bf16)
        qx = expand(q)
        gx = expand(g)
        low = probs[w, :, 256 * b : 256 * b + 256]
        high = low.astype(f32)
        scaled = high * nt(v, gx)
        back = (scaled - high * col(scaled)).astype(bf16)
        d[4 + b, at, :] = nn(back, qx) * SCALING
        d[8 + b, at, :] = nn(low, gx)
        d[b, at, :] = query_side(k, back) * SCALING


def back_kernel(
    wins, dps,
    triple, triple0, probs, grad_merged,
    region_triple, gathered, probs_r, merged_r, region_mid, grad_middle0, gain, w_qkv, w_out, out_local,
    up_source, down_source,
    grad_triple, up_sum, down_sum, terms, grad_query, out_grad, sums, out_bias_part, grad_mid,
    t, d, d0, *streams,
):
    step = pl.program_id(0)
    place = Place(wins, dps)
    up = Stream(place, up_source, up_sum, streams[: Stream.PARTS])
    down = Stream(place, down_source, down_sum, streams[Stream.PARTS :])

    @pl.when(step == 0)
    def _():
        place.greet()
        up.load()
        down.load()

    patch = triple.shape[0]
    load_triple(t, triple, triple0, patch)
    rows = (patch + 1) * WC
    for b in range(4):
        t[12 + b, 0:rows] = grad_merged[:, :, 128 * b : 128 * b + 128].reshape(rows, 128).astype(f32)
        t[12 + b, rows:] = jnp.zeros((TP * WC - rows, 128), f32)

    hooks = {
        0: (place.greeted, up.send_cores, down.send_cores),
        1: (up.send_chips,),
        2: (down.send_chips,),
        5: (up.send_dps,),
        8: (up.send_dps_back, down.send_dps),
        11: (up.send_chips_back, down.send_dps_back),
    }

    def body(i, carry):
        for u in range(4):
            local_bwd_step(i * 4 + u, probs, t, d)
        for when, todo in hooks.items():

            @pl.when(step * (WC // 4) + i == when)
            def _(todo=todo):
                for act in todo:
                    act()

        return carry

    lax.fori_loop(0, WC // 4, body, 0)
    at = pl.ds(pl.multiple_of(step * WC, WC), WC)
    for b in range(12):
        lanes = slice(128 * b, 128 * b + 128)
        low = d[b, 0:rows].astype(bf16)
        grad_triple[:, :, lanes] = low.reshape(patch + 1, WC, 128)
        d0[at, lanes] = low[rows - WC :]

    @pl.when(step == pl.num_programs(0) - 1)
    def _():
        vhat, inverse = norm_stats(region_mid[...])
        mid = grad_middle0[0].astype(f32) + norm_back(vhat, inverse, gain[...], nt(d0[...], w_qkv[...]))
        grad_mid[...] = mid
        grad_attn = mid.astype(bf16)
        out_grad[...] = (out_local[...] + tn(merged_r[...], grad_attn)).astype(bf16)
        out_bias_part[...] = col(grad_attn.astype(f32))
        grad_merged_r = nt(grad_attn, w_out[...]).astype(bf16)
        for g in range(2):
            lanes = slice(256 * g, 256 * g + 256)
            value_lanes = slice(D + 256 * g, D + 256 * g + 256)
            qx = expand_group(region_triple[:, lanes], 8)
            gx = expand_group(grad_merged_r[:, lanes], 8)
            low = probs_r[g]
            high = low.astype(f32)
            scaled = high * nt(gathered[:, value_lanes], gx)
            back = (scaled - high * col(scaled)).astype(bf16)
            terms[:, lanes] = (nn(back, qx) * SCALING).astype(bf16)
            terms[:, value_lanes] = nn(low, gx).astype(bf16)
            grad_query[:, lanes] = (fold_group(tn(back, gathered[:, lanes]), 8) * SCALING).astype(bf16)
            if g == 0:
                down.send_chips_back()
        sums[:, :D] = col(grad_query[...].astype(f32))
        sums[:, D:] = col(terms[...].astype(f32))
        up.send_cores_back()
        down.send_cores_back()
        up.finish()
        down.finish()


def gelu_both(v):
    e = jnp.exp2(v * v * (-0.5 * LOG2E))
    cdf = 0.5 + 0.5 * lax.erf(v * (0.5**0.5))
    return v * cdf, cdf + v * e * 0.3989422804014327


def with_region(block, region, last):
    tokens, count, width = block.shape
    head = block[0 : tokens - 1].reshape((tokens - 1) * count, width)
    tail = jnp.where(last, region, block[tokens - 1])
    return jnp.concatenate([head, tail], axis=0)


def mlp_kernel(
    patches, region_mid, merged, patch_cot, region_cot, w_out, out_bias, gain, shift, w_up, up_bias, w_down, down_bias,
    patch_out, region_out, grad_middle, grad_merged, up_grad, down_grad_t, out_grad, vec512, up_bias_grad,
    up_acc, down_acc,
):
    step = pl.program_id(0)
    last = step == pl.num_programs(0) - 1
    tokens, count, _ = patches.shape
    rows = tokens * count

    @pl.when(step == 0)
    def _():
        up_acc[...] = jnp.zeros_like(up_acc)
        down_acc[...] = jnp.zeros_like(down_acc)
        out_grad[...] = jnp.zeros_like(out_grad)
        vec512[...] = jnp.zeros_like(vec512)
        up_bias_grad[...] = jnp.zeros_like(up_bias_grad)

    x = with_region(patches[...].astype(f32), region_mid[...], last)
    grad_result = with_region(patch_cot[...], region_cot[...], last)
    low_merged = merged[...].reshape(rows, D)
    middle = x + nn(low_merged, w_out[...]) + out_bias[...]
    vhat, inverse = norm_stats(middle)
    mlp_in = (vhat * gain[...] + shift[...]).astype(bf16)
    mlp_in_t = mlp_in.T
    grad_result_t = grad_result.T
    result = middle + down_bias[...]
    grad_in = jnp.zeros((rows, D), f32)
    for f in range(FF // 512):
        at = slice(512 * f, 512 * f + 512)
        hidden = nn(mlp_in, w_up[:, at]) + up_bias[:, at]
        active, slope = gelu_both(hidden)
        active = active.astype(bf16)
        grad_hidden = (nt(grad_result, w_down[at, :]) * slope).astype(bf16)
        result += nn(active, w_down[at, :])
        grad_in += nt(grad_hidden, w_up[:, at])
        up_acc[:, at] += nn(mlp_in_t, grad_hidden)
        down_acc[:, at] += nn(grad_result_t, active)
        up_bias_grad[:, at] += col(grad_hidden.astype(f32))
    shown = result.astype(bf16)
    patch_out[...] = shown.reshape(tokens, count, D)
    region_out[...] = shown[rows - count :]
    gm = grad_result.astype(f32) + norm_back(vhat, inverse, gain[...], grad_in)
    low_gm = gm.astype(bf16)
    grad_middle[...] = low_gm.reshape(tokens, count, D)
    out_grad[...] += nn(low_merged.T, low_gm)
    grad_merged[...] = nt(low_gm, w_out[...]).astype(bf16).reshape(tokens, count, D)
    vec512[0:1] += col(grad_in * vhat)
    vec512[1:2] += col(grad_in)
    vec512[2:3] += col(low_gm.astype(f32))
    vec512[3:4] += col(grad_result.astype(f32))

    @pl.when(last)
    def _():
        up_grad[...] = up_acc[...].astype(bf16)
        down_grad_t[...] = down_acc[...].astype(bf16)


def tail_kernel(
    wins, dps,
    patches, grad_triple, grad_middle, region_mid, gain, shift, w_qkv, region_in, region_in_all, terms, grad_query,
    regional, grad_mid, vec_mlp, up_bias_grad, sums, out_bias_part, out_source,
    patch_grad, region_grad, small_sum, out_sum, query_sum, key_sum, value_sum,
    qkv_acc, qkv_low, triple_sums, vec, pieces, piece_sem, pack, near, near_sem, total, far, far_sem, *streams,
):
    step = pl.program_id(0)
    half = pl.num_programs(0) // 2
    tokens, count, _ = patches.shape
    rows = tokens * count
    place = Place(wins, dps)
    parts = [streams[Stream.PARTS * b : Stream.PARTS * (b + 1)] for b in range(4)]
    out = Stream(place, out_source, out_sum, parts[0])
    blocks = [Stream(place, qkv_low.at[b], (query_sum, key_sum, value_sum)[b], parts[b + 1]) for b in range(3)]

    def to_owners():
        copies = []
        for j in range(1, wins):
            win = lax.rem(place.win + j, wins)
            copies.append(pltpu.make_async_remote_copy(
                src_ref=terms.at[pl.ds(pl.multiple_of(win * count, 16), count)], dst_ref=pieces.at[j - 1],
                send_sem=piece_sem.at[2 * j - 2], recv_sem=piece_sem.at[2 * j - 1],
                device_id={"win": win}, device_id_type=MESH,
            ))
        return copies

    def to_near():
        return [pltpu.make_async_remote_copy(
            src_ref=pack, dst_ref=near.at[j - 1], send_sem=near_sem.at[2 * j - 2], recv_sem=near_sem.at[2 * j - 1],
            device_id={"win": lax.rem(place.win + j, wins)}, device_id_type=MESH,
        ) for j in range(1, wins)]

    def to_far():
        return [pltpu.make_async_remote_copy(
            src_ref=total, dst_ref=far.at[j - 1], send_sem=far_sem.at[2 * j - 2], recv_sem=far_sem.at[2 * j - 1],
            device_id=place.at_dp(j)[1], device_id_type=MESH,
        ) for j in range(1, dps)]

    def begin():
        place.greeted(all_wins=True)
        for c in to_owners():
            c.start()
        out.load()
        out.send_cores()

    def region_end():
        for c in to_owners():
            c.wait()
        key_value = terms[pl.ds(pl.multiple_of(place.win * count, 16), count)].astype(f32)
        for j in range(wins - 1):
            key_value += pieces[j].astype(f32)
        vhat, inverse = norm_stats(regional[...].astype(f32))
        grad_in = nt(grad_query[...], w_qkv[:, :D]) + nt(key_value.astype(bf16), w_qkv[:, D:])
        region_grad[...] = (grad_mid[...] + norm_back(vhat, inverse, gain[...], grad_in)).astype(bf16)
        vec[0:1] += col(grad_in * vhat)
        vec[1:2] += col(grad_in)

    def qkv_end():
        qkv_low[0] = (qkv_acc[:, :D] + tn(region_in[...], grad_query[...])).astype(bf16)
        for b in range(1, 3):
            lanes = slice(D * (b - 1), D * b)
            qkv_low[b] = (qkv_acc[:, D * b : D * (b + 1)] + tn(region_in_all[...], terms[:, lanes])).astype(bf16)
        for s in blocks:
            s.load()
            s.send_cores()

    def small_begin():
        pack[0:2] = vec[0:2]
        pack[2:3] = triple_sums[:, :D] + sums[:, :D]
        pack[3:4] = triple_sums[:, 2 * D :] + sums[:, 2 * D :]
        pack[4:5] = vec_mlp[2:3] + out_bias_part[...]
        pack[5:7] = vec_mlp[0:2]
        pack[7:8] = vec_mlp[3:4]
        for b in range(4):
            pack[8 + b : 9 + b] = up_bias_grad[:, D * b : D * (b + 1)]
        pack[12:16] = jnp.zeros((4, D), f32)
        for c in to_near():
            c.start()

    def small_middle():
        for c in to_near():
            c.wait()
        part = pack[...]
        for j in range(wins - 1):
            part += near[j]
        total[...] = part
        for c in to_far():
            c.start()

    def small_end():
        for c in to_far():
            c.wait()
        part = total[...]
        for j in range(dps - 1):
            part += far[j]
        small_sum[...] = part

    @pl.when(step == 0)
    def _():
        place.greet(all_wins=True)
        qkv_acc[...] = jnp.zeros_like(qkv_acc)
        triple_sums[...] = jnp.zeros_like(triple_sums)
        vec[...] = jnp.zeros_like(vec)

    x = with_region(patches[...].astype(f32), region_mid[...], lax.rem(step, half) == half - 1)
    vhat, inverse = norm_stats(x)
    low = grad_triple[...].reshape(rows, 3 * D)

    @pl.when(step < half)
    def _():
        local_in = (vhat * gain[...] + shift[...]).astype(bf16)
        qkv_acc[...] += nn(local_in.T, low)
        triple_sums[...] += col(low.astype(f32))

    @pl.when(step >= half)
    def _():
        grad_in = nt(low, w_qkv[...])
        vec[0:1] += col(grad_in * vhat)
        vec[1:2] += col(grad_in)
        total_rows = grad_middle[...].reshape(rows, D).astype(f32) + norm_back(vhat, inverse, gain[...], grad_in)
        patch_grad[...] = total_rows.astype(bf16).reshape(tokens, count, D)

    query, key, value = blocks
    hooks = {
        0: (begin,),
        1: (out.send_chips,),
        2: (region_end,),
        3: (out.send_dps,),
        half - 1: (qkv_end, out.send_dps_back),
        half: (query.send_chips, key.send_chips),
        half + 1: (value.send_chips, out.send_chips_back),
        half + 2: (query.send_dps, out.send_cores_back),
        half + 3: (key.send_dps,),
        half + 4: (
            small_begin, out.finish, value.send_dps, query.send_dps_back, small_middle, key.send_dps_back,
            value.send_dps_back, query.send_chips_back, small_end, key.send_chips_back, value.send_chips_back,
            query.send_cores_back, key.send_cores_back, value.send_cores_back, query.finish, key.finish, value.finish,
        ),
    }
    for when, todo in hooks.items():

        @pl.when(step == when)
        def _(todo=todo):
            for act in todo:
                act()


def shards(
    wins, dps,
    patches, regional, window_image, in_gain, in_shift, w_qkv, qkv_bias, w_out, out_bias,
    mlp_gain, mlp_shift, w_up, up_bias, w_down, down_bias, patch_cot, region_cot,
):
    _, count, patch, _ = patches.shape
    group = window_image.shape[1]
    row = lambda v: v.astype(f32).reshape(1, -1)
    gain1, shift1, gain2, shift2 = row(in_gain), row(in_shift), row(mlp_gain), row(mlp_shift)
    bias_row = row(jnp.concatenate([qkv_bias[0], jnp.zeros_like(qkv_bias[0]), qkv_bias[1]]))
    out_row, up_row, down_row = row(out_bias), row(up_bias), row(down_bias)
    images = window_image[0]
    own = lax.dynamic_slice_in_dim(images, lax.axis_index("win") * count, count)
    image_row = jnp.tile(own, HEADS)[None]
    image_col = images[:, None]
    x = patches[0].transpose(1, 0, 2)
    cot = patch_cot[0].transpose(1, 0, 2)
    reg = regional[0]
    rcot = region_cot[0]

    region_in, region_triple = call(
        region_in_kernel, (1,), [whole(a) for a in (reg, gain1, shift1, w_qkv, bias_row)],
        [whole_out((count, D), bf16), whole_out((count, 3 * D), bf16)], name="region_in",
    )
    packed = jnp.concatenate([region_triple[:, D:], region_in], axis=1)
    gathered = lax.all_gather(packed, "win", axis=0, tiled=True)
    block = lambda a, n: (a, (n,) + a.shape[1:], lambda i: (i, 0, 0))
    block_out = lambda shape, n, dtype=bf16: ((shape, dtype), (n,) + shape[1:], lambda i: (i, 0, 0))
    (triple,) = call(
        patch_proj_kernel, (pl.cdiv(patch, 7),),
        [block(x, 7)] + [whole(a) for a in (gain1, shift1, w_qkv, bias_row)],
        [block_out((patch, count, 3 * D), 7)], name="patch_proj",
    )
    probs_r, merged_r, region_mid, triple0 = call(
        region_attn_kernel, (1,),
        [whole(a) for a in (region_triple, gathered, image_col, image_row, reg, gain1, shift1, w_qkv, bias_row, w_out, out_row)],
        [whole_out((2, group, 8 * count), bf16), whole_out((count, D), bf16),
         whole_out((count, D), f32), whole_out((count, 3 * D), bf16)], name="region_attn",
    )
    steps = (count // WC,)
    mid = lambda a: (a, (a.shape[0], WC, a.shape[2]), lambda i: (0, i, 0))
    mid_out = lambda shape, dtype=bf16: ((shape, dtype), (shape[0], WC, shape[2]), lambda i: (0, i, 0))
    tail = lambda a: (a, (WC, a.shape[1]), lambda i: (i, 0))
    merged, probs = call(
        local_fwd_kernel, steps, [mid(triple), tail(triple0)],
        [mid_out((patch + 1, count, D)), ((((count, TP, HEADS * TP)), bf16), (WC, TP, HEADS * TP), lambda i: (i, 0, 0))],
        [pltpu.VMEM((12, TP * WC, 128), f32), pltpu.VMEM((4, TP * WC, 128), f32)], name="local_fwd",
    )
    n = 10
    rows_grid = ((patch + 1) // n,)
    patch_out, region_out, grad_middle, grad_merged, up_grad, down_grad_t, out_local, vec_mlp, up_bias_grad = call(
        mlp_kernel, rows_grid,
        [block(x, n), whole(region_mid), block(merged, n), block(cot, n)]
        + [whole(a) for a in (rcot, w_out, out_row, gain2, shift2, w_up, up_row, w_down, down_row)],
        [block_out((patch, count, D), n), whole_out((count, D), bf16),
         block_out((patch + 1, count, D), n), block_out((patch + 1, count, D), n),
         whole_out((D, FF), bf16), whole_out((D, FF), bf16), whole_out((D, D), f32),
         whole_out((8, D), f32), whole_out((1, FF), f32)],
        [pltpu.VMEM((D, FF), f32), pltpu.VMEM((D, FF), f32)], name="mlp",
    )
    const = lambda *arrays: [whole(a) for a in arrays]
    grad_triple, up_sum, down_sum, terms, grad_query, out_grad, sums, out_bias_part, grad_mid = call(
        functools.partial(back_kernel, wins, dps), steps,
        [mid(triple), tail(triple0), (probs, (WC, TP, HEADS * TP), lambda i: (i, 0, 0)), mid(grad_merged)]
        + const(region_triple, gathered, probs_r, merged_r, region_mid)
        + [(grad_middle, (1, count, D), lambda i: (patch, 0, 0))]
        + const(gain1, w_qkv, w_out, out_local) + [left(up_grad), left(down_grad_t)],
        [mid_out((patch + 1, count, 3 * D)), left_out((D, FF), bf16), left_out((D, FF), bf16),
         whole_out((group, 2 * D), bf16), whole_out((count, D), bf16), whole_out((D, D), bf16),
         whole_out((1, 3 * D), f32), whole_out((1, D), f32), whole_out((count, D), f32)],
        [pltpu.VMEM((16, TP * WC, 128), f32), pltpu.VMEM((12, TP * WC, 128), f32), pltpu.VMEM((count, 3 * D), bf16)]
        + stream_scratch(wins, dps, FF) * 2,
        name="back", collective_id=0,
    )
    half = rows_grid[0]
    again = lambda a: (a, (n,) + a.shape[1:], lambda i: (lax.rem(i, half), 0, 0))
    second = lambda a: (a, (n,) + a.shape[1:], lambda i: (lax.max(i - half, 0), 0, 0))
    patch_grad, region_grad, small, out_sum, query_sum, key_sum, value_sum = call(
        functools.partial(tail_kernel, wins, dps), (2 * half,),
        [again(x), again(grad_triple), second(grad_middle)]
        + const(region_mid, gain1, shift1, w_qkv, region_in)
        + [(gathered, (group, D), lambda i: (0, 2))]
        + const(terms, grad_query, reg, grad_mid, vec_mlp, up_bias_grad, sums, out_bias_part) + [left(out_grad)],
        [(((patch, count, D), bf16), (n, count, D), lambda i: (lax.max(i - half, 0), 0, 0)),
         whole_out((count, D), bf16), whole_out((16, D), f32)] + [left_out((D, D), bf16)] * 4,
        [pltpu.VMEM((D, 3 * D), f32), pltpu.VMEM((3, D, D), bf16), pltpu.VMEM((1, 3 * D), f32), pltpu.VMEM((8, D), f32),
         pltpu.VMEM((wins - 1, count, 2 * D), bf16), pltpu.SemaphoreType.DMA((2 * wins,)),
         pltpu.VMEM((16, D), f32), pltpu.VMEM((wins - 1, 16, D), f32), pltpu.SemaphoreType.DMA((2 * wins,)),
         pltpu.VMEM((16, D), f32), pltpu.VMEM((max(dps - 1, 1), 16, D), f32), pltpu.SemaphoreType.DMA((2 * dps,))]
        + stream_scratch(wins, dps, D) * 4,
        name="tail", collective_id=1,
    )
    return (
        patch_out.transpose(1, 0, 2)[None],
        region_out[None],
        patch_grad.transpose(1, 0, 2)[None],
        region_grad[None],
        small[0],
        small[1],
        jnp.concatenate([query_sum, key_sum, value_sum], axis=1).astype(f32),
        small[2:4],
        out_sum.astype(f32),
        small[4],
        small[5],
        small[6],
        up_sum.astype(f32),
        small[8:12].reshape(-1),
        down_sum.T.astype(f32),
        small[7],
    )


def solution(mesh):
    wide = P("dp", "win", None, None)
    narrow = P("dp", "win", None)
    in_specs = (wide, narrow, P("dp", None)) + (P(),) * 12 + (wide, narrow)
    out_specs = (wide, narrow, wide, narrow) + (P(),) * 12
    return jax.shard_map(functools.partial(shards, mesh.shape["win"], mesh.shape["dp"]), mesh=mesh, in_specs=in_specs, out_specs=out_specs, check_vma=False)
```

time: 877 us -> 283 us (0.32)
  matrix products: 262 us -> 0 us
  local copies, waits for them, and re-layouts: 252 us -> 16.6 us
  Pallas kernels: 0 us -> 223 us
  waiting for transfers between devices: 186 us -> 7.65 us
  other arithmetic: 91.2 us -> 20.2 us
  blocking collectives: 62.4 us -> 0 us
    dot_general x29 -> x0, matrix products: 260 us -> none  [the longest x1 51.1 us: shards(): jnp.dot(mlp_in, w_up, preferred_element_type=jnp.float32)]
    pallas_call x0 -> x7, Pallas kernels: none -> 223 us  [call(): pl.pallas_call(body, grid=grid, in_specs=[spec(b, i) for _, b, i in ins],...]
    psum x1 -> x0, waiting for transfers between devices: 162 us -> none  [shards(): lax.psum((in_gain_grad, in_shift_grad, qkv_grad, qkv_bias_grad, out_grad,...]
    reshape x9 -> x0, local copies, waits for them, and re-layouts: 73.6 us -> none  [the longest x1 32.3 us: shards(): project(local_in, w_qkv, bias_row)]
    convert_element_type x6 -> x0, local copies, waits for them, and re-layouts: 66 us -> none  [the longest x2 38.2 us: shards(): grad_triple = jnp.stack([grad_query, grad_keys, grad_values], axis=2).res...]
    unnamed x188 -> x19, local copies, waits for them, and re-layouts: 65 us -> 9.11 us
    psum x1 -> x0, blocking collectives: 41.8 us -> none  [shards(): lax.psum((in_gain_grad, in_shift_grad, qkv_grad, qkv_bias_grad, out_grad,...]
    reduce_sum x13 -> x0, other arithmetic: 28.1 us -> none  [the longest x5 16.5 us: column_sums(): return jnp.sum(matrix.astype(jnp.float32), axis=0)]
  transfers between devices with their start and end apart: 3 -> 1, of which waited for: 2 -> 1; matrix products, arithmetic and copies ran while one was open for 9% -> 3% of each run, Pallas kernels for 0% -> 4%
where the time goes in v1:
time: 283 us; the launch traced here: 282 us
  Pallas kernels  223 us (79%)
  other arithmetic  20.2 us (7%)
  local copies, waits for them, and re-layouts  16.6 us (6%)
  between operations  14.1 us (5%)
  waiting for transfers between devices  7.65 us (3%)
    pallas_call x7, Pallas kernels, call(): pl.pallas_call(body, grid=grid, in_specs=[spec(b, i) for _, b, i in ins],...  223 us
    unnamed x19, local copies, waits for them, and re-layouts  9.11 us
    reshape x7, other arithmetic, shards(): row = lambda v: v.astype(f32).reshape(1, -1)  8.83 us
    all_gather x1, waiting for transfers between devices, shards(): gathered = lax.all_gather(packed, 'win', axis=0, tiled=True)  7.63 us
  transfers between devices with their start and end apart: 1, of which 1 were waited for; matrix products, arithmetic and copies ran while one was open for 3% of the time, Pallas kernels for 4%

profile of v1, /device:TPU:0, one launch (start us, length us, event | category | flops | bytes accessed | tf_op | source)
XLA Modules:
  0.0 281.8 jit_solution(2741234945861106679)
XLA Ops:
  7.2 1.3 reshape.120
  8.5 1.3 reshape.122
  9.7 0.8 fusion.3
  10.5 0.6 fusion.1.bias
  11.1 2.6 region_in.1
  13.8 0.9 slice.35
  14.7 1.5 pad_maximum_fusion
  16.2 1.3 reshape.124
  17.4 1.3 reshape.126
  18.7 1.3 reshape.128
  19.9 1.3 reshape.132
  21.2 0.8 dynamic-slice_bitcast_fusion
  21.9 0.7 broadcast_in_dim_tile.3.image_row
  22.6 1.3 reshape.130
  23.9 1.5 copy.34.image_col
  25.4 10.0 %patch_proj.1.triple = bf16[49,48,1536]{2,1,0:T(8,128)(2,1)} custom-call(bf16[49,48,512]{2,1,0:T(8,128)(2,1)} %bitcast.37, f32[1,512]{1,0:T(1,128)} %bitcast.46, f32[1,512]{1,0:T(1,128)} %bitcast.51, bf16[512,1536]{1,0:T(8,128)(2,1)} %w_qkv.9, f32[1,1536]{1,0:T(1,128)} %fusion.1.bias), custom_call_target="tpu_custom_call" | custom-call | tf_op jit(solution)/shard_map/patch_proj/pallas_call | solution.py:46
  35.4 7.6 %all-gather.2.cloned.1.call-done.gathered.region_in_all = bf16[384,1536]{1,0:T(8,128)(2,1)} async-done(((bf16[48,1536]{1,0:T(8,128)(2,1)}), bf16[384,1536]{1,0:T(8,128)(2,1)}) %all-gather.2.cloned.1.call-update) | async-done | bytes 1179664 | tf_op jit(solution)/shard_map/all_gather | solution.py:737
  43.1 4.5 %region_attn.1 = (bf16[2,384,384]{2,1,0:T(8,128)(2,1)}, bf16[48,512]{1,0:T(8,128)(2,1)}, f32[48,512]{1,0:T(8,128)}, bf16[48,1536]{1,0:T(8,128)(2,1)}) custom-call(bf16[48,1536]{1,0:T(8,128)(2,1)} %get-tuple-element.49.triple.region_triple, bf16[384,1536]{1,0:T(8,128)(2,1)} %all-gather.2.cloned.1.call-done.gathered.region_in_all, s32[384,1]{1,0:T(8,128)} %copy.34.image_col, ...), custom_call_target="tpu_custom_call" | custom-call | tf_op jit(solution)/shard_map/region_attn/pallas_call | solution.py:46
  47.5 21.9 %local_fwd.1 = (bf16[50,48,512]{2,1,0:T(8,128)(2,1)}, bf16[48,64,1024]{2,1,0:T(8,128)(2,1)}) custom-call(bf16[49,48,1536]{2,1,0:T(8,128)(2,1)} %patch_proj.1.triple, bf16[48,1536]{1,0:T(8,128)(2,1)} %get-tuple-element.52.triple0), custom_call_target="tpu_custom_call" | custom-call | tf_op jit(solution)/shard_map/local_fwd/pallas_call | solution.py:46
  69.5 50.2 %mlp.1 = (bf16[49,48,512]{2,1,0:T(8,128)(2,1)}, bf16[48,512]{1,0:T(8,128)(2,1)}, bf16[50,48,512]{2,1,0:T(8,128)(2,1)}, bf16[50,48,512]{2,1,0:T(8,128)(2,1)}, bf1...) custom-call(bf16[49,48,512]{2,1,0:T(8,128)(2,1)} %bitcast.38, ...), custom_call_target="tpu_custom_call" | custom-call | tf_op jit(solution)/shard_map/mlp/pallas_call | solution.py:46
  119.7 71.5 %back.1 = (bf16[50,48,1536]{2,1,0:T(8,128)(2,1)}, bf16[512,2048]{1,0:T(8,128)(2,1)}, bf16[512,2048]{1,0:T(8,128)(2,1)}, bf16[384,1024]{1,0:T(8,128)(2,1)}, bf16[...) custom-call(bf16[49,48,1536]{2,1,0:T(8,128)(2,1)} %patch_proj.1.trip, ...), custom_call_target="tpu_custom_call" | custom-call | tf_op jit(solution)/shard_map/back/pallas_call | solution.py:46
  191.3 62.5 %tail.1 = (bf16[49,48,512]{2,1,0:T(8,128)(2,1)}, bf16[48,512]{1,0:T(8,128)(2,1)}, f32[16,512]{1,0:T(8,128)}, bf16[512,512]{1,0:T(8,128)(2,1)}, bf16[512,512]{1,0...) custom-call(bf16[49,48,512]{2,1,0:T(8,128)(2,1)} %bitcast.39, ...), custom_call_target="tpu_custom_call" | custom-call | tf_op jit(solution)/shard_map/tail/pallas_call | solution.py:46
  253.7 1.3 slice.38
  255.0 0.7 slice_bitcast_fusion
  255.7 1.5 fusion.2
  257.9 2.1 convert_element_type.34
  260.0 2.5 convert_element_type.35
  262.6 2.5 convert_bitcast_fusion
  265.1 5.5 %copy.35 = f32[2048,512]{1,0:T(8,128)} copy(f32[2048,512]{0,1:T(8,128)} %convert_bitcast_fusion) | data formatting | bytes 8388608
  270.6 2.1 maximum_convert_fusion
  272.9 1.4 copy.39
  274.3 0.6 copy.40
  (20 shorter events, 1.0 us)
Async XLA Ops:
  7.2 35.9 %all-gather.2.cloned.1.call-start = ((), (), s32[]{:S(2)}) async-start(), calls=%async_computation | async-start | bytes 1327104 | tf_op jit(solution)/shard_map/all_gather | solution.py:737
  191.2 68.8 %copy-start.2 = (bf16[512,2048]{1,0:T(8,128)(2,1)S(1)}, bf16[512,2048]{1,0:T(8,128)(2,1)}, u32[]{:S(2)}) copy-start(bf16[512,2048]{1,0:T(8,128)(2,1)} %get-tuple-element.80) | copy-start | bytes 6291460
  260.0 2.5 copy-start.1
  265.1 5.5 %copy-start.3 = (bf16[512,512]{1,0:T(8,128)(2,1)S(1)}, bf16[512,512]{1,0:T(8,128)(2,1)}, u32[]{:S(2)}) copy-start(bf16[512,512]{1,0:T(8,128)(2,1)} %get-tuple-element.76) | copy-start | bytes 1572868
  265.1 5.5 %copy-start.4 = (bf16[512,512]{1,0:T(8,128)(2,1)S(1)}, bf16[512,512]{1,0:T(8,128)(2,1)}, u32[]{:S(2)}) copy-start(bf16[512,512]{1,0:T(8,128)(2,1)} %get-tuple-element.77) | copy-start | bytes 1572868
  265.1 5.5 %copy-start.5 = (bf16[512,512]{1,0:T(8,128)(2,1)S(1)}, bf16[512,512]{1,0:T(8,128)(2,1)}, u32[]{:S(2)}) copy-start(bf16[512,512]{1,0:T(8,128)(2,1)} %get-tuple-element.78) | copy-start | bytes 1572868
  270.5 2.4 copy-start
  272.6 1.7 copy-start.6
Sparse Core Ops, SparseCore 0:
  16.3 26.7 all-gather.1

commit v2 on v1

--- a/solution.py
+++ b/solution.py
@@ -100,9 +100,18 @@
         self.core = lax.rem(self.win, 2)
         self.chip = self.win // 2
         self.chips = wins // 2
+        self.square = self.chips == 4
+        self.a = self.chip // 2
+        self.b = lax.rem(self.chip, 2)
 
     def other_core(self):
         return {"win": self.chip * 2 + 1 - self.core}
+
+    def other_a(self):
+        return {"win": ((1 - self.a) * 2 + self.b) * 2 + self.core}
+
+    def other_b(self):
+        return {"win": (self.a * 2 + 1 - self.b) * 2 + self.core}
 
     def at_chip(self, j):
         chip = lax.rem(self.chip + j, self.chips)
@@ -112,55 +121,60 @@
         dp = lax.rem(self.dp + j, self.dps)
         return dp, {"dp": dp}
 
-    def greet(self, all_wins=False):
+    def near(self, all_wins):
+        if all_wins:
+            return [{"win": lax.rem(self.win + j, self.wins)} for j in range(1, self.wins)]
+        if self.square:
+            return [self.other_core(), self.other_a(), self.other_b()]
+        return [self.other_core()] + [self.at_chip(j)[1] for j in range(1, self.chips)]
+
+    def partners(self, all_wins, along):
+        return self.near(all_wins) + [self.at_dp(j)[1] for j in range(1, self.dps if along else 1)]
+
+    def greet(self, all_wins=False, along=True):
         barrier = pltpu.get_barrier_semaphore()
-        if all_wins:
-            for j in range(1, self.wins):
-                pl.semaphore_signal(barrier, inc=1, device_id={"win": lax.rem(self.win + j, self.wins)}, device_id_type=MESH)
-        else:
-            pl.semaphore_signal(barrier, inc=1, device_id=self.other_core(), device_id_type=MESH)
-            for j in range(1, self.chips):
-                pl.semaphore_signal(barrier, inc=1, device_id=self.at_chip(j)[1], device_id_type=MESH)
-        for j in range(1, self.dps):
-            pl.semaphore_signal(barrier, inc=1, device_id=self.at_dp(j)[1], device_id_type=MESH)
-
-    def greeted(self, all_wins=False):
-        near = self.wins - 1 if all_wins else self.chips
-        pl.semaphore_wait(pltpu.get_barrier_semaphore(), near + self.dps - 1)
+        for to in self.partners(all_wins, along):
+            pl.semaphore_signal(barrier, inc=1, device_id=to, device_id_type=MESH)
+
+    def greeted(self, all_wins=False, along=True):
+        pl.semaphore_wait(pltpu.get_barrier_semaphore(), len(self.partners(all_wins, along)))
 
 
 def rows_of(wins, dps):
-    half = D // 2
-    piece = half // (wins // 2)
-    last = piece // dps if piece % (16 * dps) == 0 else piece
-    return half, piece, last
+    piece = D // wins
+    return piece, piece // dps if piece % (16 * dps) == 0 else piece
+
+
+def stream_shape(wins, columns):
+    return (2, wins // 2, D // wins, columns)
 
 
 def stream_scratch(wins, dps, columns):
-    half, piece, last = rows_of(wins, dps)
+    piece, last = rows_of(wins, dps)
     chips = wins // 2
+    landing = (4, 2, piece, columns // 2) if chips == 4 else (max(chips - 1, 1), piece, columns)
     return [
-        pltpu.VMEM((half, columns), bf16),
-        pltpu.VMEM((half, columns), bf16),
-        pltpu.VMEM((max(chips - 1, 1), piece, columns), bf16),
+        pltpu.VMEM((chips, piece, columns), bf16),
+        pltpu.VMEM((chips, piece, columns), bf16),
+        pltpu.VMEM(landing, bf16),
         pltpu.VMEM((piece, columns), bf16),
         pltpu.VMEM((max(dps - 1, 1), last, columns), bf16),
         pltpu.VMEM((piece, columns), bf16),
-        pltpu.SemaphoreType.DMA((6 + 4 * chips + 4 * dps,)),
+        pltpu.SemaphoreType.DMA((20 + 4 * chips + 4 * dps,)),
     ]
 
 
 class Stream:
     PARTS = 7
 
-    def __init__(self, place, source, final, refs, first=None):
+    def __init__(self, place, source, final, refs):
         self.p = place
         self.source, self.final = source, final
         self.own, self.r1, self.r2, self.s, self.r3, self.s2, self.sem = refs
-        self.half, self.piece, self.last = rows_of(place.wins, place.dps)
+        self.piece, self.last = rows_of(place.wins, place.dps)
         self.split = self.last != self.piece
-        self.slabs = self.half // 16
-        self.columns = self.own.shape[1]
+        columns = self.own.shape[2]
+        self.left, self.right = pl.ds(0, columns // 2), pl.ds(columns // 2, columns // 2)
 
     def rows(self, start, size):
         return pl.ds(pl.multiple_of(start, 16), size)
@@ -172,22 +186,57 @@
         )
 
     def _own(self):
-        mine = self.rows(self.p.core * self.half, self.half)
-        return pltpu.make_async_copy(self.source.at[mine], self.own, self.sem.at[0])
+        return pltpu.make_async_copy(self.source.at[self.p.core], self.own, self.sem.at[0])
 
     def _put(self):
-        mine = self.rows(self.p.core * self.half + self.p.chip * self.piece, self.piece)
-        return pltpu.make_async_copy(self.s2, self.final.at[mine], self.sem.at[1])
+        return pltpu.make_async_copy(self.r1, self.final.at[self.p.core], self.sem.at[1])
 
     def _cores(self):
-        other = self.rows((1 - self.p.core) * self.half, self.half)
-        return [self.remote(self.source.at[other], self.r1, self.p.other_core(), 1)]
+        return [self.remote(self.source.at[1 - self.p.core], self.r1, self.p.other_core(), 1)]
+
+    def _cores_back(self):
+        return [self.remote(self.r1, self.final.at[self.p.core], self.p.other_core(), 2)]
+
+    def _chips_left(self, k):
+        p = self.p
+        if k == 0:
+            return [self.remote(self.own.at[c * 2 + 1 - p.b, :, self.left], self.r2.at[0, c], p.other_b(), 3 + c) for c in range(2)]
+        return [self.remote(self.own.at[(1 - p.a) * 2 + p.b, :, self.left], self.r2.at[2, 0], p.other_a(), 5)]
+
+    def _chips_right(self, k):
+        p = self.p
+        if k == 0:
+            return [self.remote(self.own.at[(1 - p.a) * 2 + c, :, self.right], self.r2.at[1, c], p.other_a(), 6 + c) for c in range(2)]
+        return [self.remote(self.own.at[p.a * 2 + 1 - p.b, :, self.right], self.r2.at[3, 0], p.other_b(), 8)]
+
+    def _back_left(self, k):
+        p = self.p
+        mine = self.r1
+        if k == 0:
+            return [self.remote(self.s2.at[:, self.left], mine.at[p.chip, :, self.left], p.other_a(), 9)]
+        rows = [mine.at[c * 2 + p.b, :, self.left] for c in range(2)]
+        return [self.remote(rows[c], rows[c], p.other_b(), 10 + c) for c in range(2)]
+
+    def _back_right(self, k):
+        p = self.p
+        mine = self.r1
+        if k == 0:
+            return [self.remote(self.s2.at[:, self.right], mine.at[p.chip, :, self.right], p.other_b(), 12)]
+        rows = [mine.at[p.a * 2 + c, :, self.right] for c in range(2)]
+        return [self.remote(rows[c], rows[c], p.other_a(), 13 + c) for c in range(2)]
 
     def _chips(self):
         out = []
         for j in range(1, self.p.chips):
             chip, to = self.p.at_chip(j)
-            out.append(self.remote(self.own.at[self.rows(chip * self.piece, self.piece)], self.r2.at[j - 1], to, 2 + j))
+            out.append(self.remote(self.own.at[chip], self.r2.at[j - 1], to, 2 + j))
+        return out
+
+    def _chips_back(self):
+        out = []
+        for j in range(1, self.p.chips):
+            mine = self.r1.at[self.p.chip]
+            out.append(self.remote(self.s2, mine, self.p.at_chip(j)[1], 2 + self.p.chips + j))
         return out
 
     def _dps(self):
@@ -195,7 +244,7 @@
         for j in range(1, self.p.dps):
             dp, to = self.p.at_dp(j)
             src = self.s.at[self.rows(dp * self.last, self.last)] if self.split else self.s
-            out.append(self.remote(src, self.r3.at[j - 1], to, 2 + self.p.chips + j))
+            out.append(self.remote(src, self.r3.at[j - 1], to, 8 + 2 * self.p.chips + j))
         return out
 
     def _dps_back(self):
@@ -203,19 +252,8 @@
         if self.split:
             for j in range(1, self.p.dps):
                 mine = self.s2.at[self.rows(self.p.dp * self.last, self.last)]
-                out.append(self.remote(mine, mine, self.p.at_dp(j)[1], 2 + self.p.chips + self.p.dps + j))
+                out.append(self.remote(mine, mine, self.p.at_dp(j)[1], 8 + 2 * self.p.chips + self.p.dps + j))
         return out
-
-    def _chips_back(self):
-        out = []
-        for j in range(1, self.p.chips):
-            mine = self.final.at[self.rows(self.p.core * self.half + self.p.chip * self.piece, self.piece)]
-            out.append(self.remote(self.s2, mine, self.p.at_chip(j)[1], 2 + self.p.chips + 2 * self.p.dps + j))
-        return out
-
-    def _cores_back(self):
-        mine = self.final.at[self.rows(self.p.core * self.half, self.half)]
-        return [self.remote(mine, mine, self.p.other_core(), 2)]
 
     def start(self, copies):
         for c in copies:
@@ -236,68 +274,91 @@
         self.wait(self._cores())
 
         def add(i, carry):
-            at = self.rows(i * 16, 16)
-            self.own[at] = (self.own[at].astype(f32) + self.r1[at].astype(f32)).astype(bf16)
+            self.own[i] = (self.own[i].astype(f32) + self.r1[i].astype(f32)).astype(bf16)
             return carry
 
-        lax.fori_loop(0, self.half // 16, add, 0)
-        self.start(self._chips())
+        lax.fori_loop(0, self.p.chips, add, 0)
+        if self.p.square:
+            self.start(self._chips_left(0))
+            self.start(self._chips_right(0))
+        else:
+            self.start(self._chips())
+
+    def add_square(self, chip, lanes, slot, c):
+        self.own[chip, :, lanes] = (self.own[chip, :, lanes].astype(f32) + self.r2[slot, c].astype(f32)).astype(bf16)
+
+    def send_chips_again(self):
+        p = self.p
+        if p.square:
+            self.wait(self._chips_left(0))
+            for c in range(2):
+                self.add_square(c * 2 + p.b, self.left, 0, c)
+            self.start(self._chips_left(1))
+            self.wait(self._chips_right(0))
+            for c in range(2):
+                self.add_square(p.a * 2 + c, self.right, 1, c)
+            self.start(self._chips_right(1))
 
     def send_dps(self):
-        self.wait(self._chips())
-
-        def add(i, carry):
-            at = self.rows(i * 16, 16)
-            total = self.own[self.rows(self.p.chip * self.piece + i * 16, 16)].astype(f32)
-            for j in range(self.p.chips - 1):
-                total += self.r2[j, at].astype(f32)
-            self.s[at] = total.astype(bf16)
-            return carry
-
-        lax.fori_loop(0, self.piece // 16, add, 0)
+        p = self.p
+        if p.square:
+            for lanes, slot, copies in ((self.left, 2, self._chips_left(1)), (self.right, 3, self._chips_right(1))):
+                self.wait(copies)
+                self.s[:, lanes] = (self.own[p.chip, :, lanes].astype(f32) + self.r2[slot, 0].astype(f32)).astype(bf16)
+        else:
+            self.wait(self._chips())
+            total = self.own[p.chip].astype(f32)
+            for j in range(p.chips - 1):
+                total += self.r2[j].astype(f32)
+            self.s[...] = total.astype(bf16)
         self.start(self._dps())
 
     def send_dps_back(self):
         self.wait(self._dps())
-
-        def add(i, carry):
-            mine = self.rows((self.p.dp * self.last if self.split else 0) + i * 16, 16)
-            total = self.s[mine].astype(f32)
-            for j in range(self.p.dps - 1):
-                total += self.r3[j, self.rows(i * 16, 16)].astype(f32)
-            self.s2[mine] = total.astype(bf16)
-            return carry
-
-        lax.fori_loop(0, self.last // 16, add, 0)
+        mine = self.rows(self.p.dp * self.last if self.split else 0, self.last)
+        total = self.s[mine].astype(f32)
+        for j in range(self.p.dps - 1):
+            total += self.r3[j].astype(f32)
+        self.s2[mine] = total.astype(bf16)
         self.start(self._dps_back())
 
     def send_chips_back(self):
         self.wait(self._dps_back())
+        self.r1[self.p.chip] = self.s2[...]
+        if self.p.square:
+            self.start(self._back_left(0))
+            self.start(self._back_right(0))
+        else:
+            self.start(self._chips_back())
+
+    def send_chips_back_again(self):
+        if self.p.square:
+            self.wait(self._back_left(0))
+            self.start(self._back_left(1))
+            self.wait(self._back_right(0))
+            self.start(self._back_right(1))
+        else:
+            self.wait(self._chips_back())
+
+    def send_cores_back(self):
+        if self.p.square:
+            self.wait(self._back_left(1))
+            self.wait(self._back_right(1))
+        self.start(self._cores_back())
         self._put().start()
-        self.start(self._chips_back())
-
-    def send_cores_back(self):
-        self._put().wait()
-        self.wait(self._chips_back())
-        self.start(self._cores_back())
 
     def finish(self):
         self.wait(self._cores_back())
-
-
-def region_in_kernel(regional, gain, shift, w_qkv, bias, region_in, triple):
-    vhat, _ = norm_stats(regional[...].astype(f32))
-    normed = (vhat * gain[...] + shift[...]).astype(bf16)
-    region_in[...] = normed
-    triple[...] = (nn(normed, w_qkv[...]) + bias[...]).astype(bf16)
-
-
-def patch_proj_kernel(patches, gain, shift, w_qkv, bias, triple):
-    rows = patches.shape[0] * patches.shape[1]
-    vhat, _ = norm_stats(patches[...].reshape(rows, D).astype(f32))
-    normed = (vhat * gain[...] + shift[...]).astype(bf16)
-    out = (nn(normed, w_qkv[...]) + bias[...]).astype(bf16)
-    triple[...] = out.reshape(triple.shape)
+        self._put().wait()
+
+    STEPS = (
+        "send_cores", "send_chips", "send_chips_again", "send_dps", "send_dps_back",
+        "send_chips_back", "send_chips_back_again", "send_cores_back", "finish",
+    )
+
+    def step(self, k):
+        if 0 <= k < len(self.STEPS):
+            getattr(self, self.STEPS[k])()
 
 
 def expand_group(x, heads):
@@ -314,28 +375,96 @@
     return total
 
 
-def region_attn_kernel(
-    triple, gathered, image_col, image_row, regional, gain, shift, w_qkv, bias, w_out, out_bias,
-    probs, merged, region_mid, triple0,
+GAIN1, SHIFT1, GAIN2, SHIFT2, OUT_BIAS, DOWN_BIAS, QUERY_BIAS, KEY_BIAS, VALUE_BIAS, UP_BIAS = range(10)
+
+
+def row(vecs, at):
+    return vecs[at : at + 1]
+
+
+def normed_low(vhat, vecs, gain, shift):
+    return (vhat * row(vecs, gain) + row(vecs, shift)).astype(bf16)
+
+
+def front_kernel(
+    wins, dps,
+    patches, regional, images, in_gain, in_shift, w_qkv, qkv_bias, w_out, out_bias, mlp_gain, mlp_shift, up_bias, down_bias,
+    triple, vecs, region_triple, gathered_out, probs, merged, region_mid, triple0,
+    gathered, packed, image_col, sem,
 ):
-    count = triple.shape[0]
-    width = 8 * count
-    for g in range(2):
-        lanes = slice(256 * g, 256 * g + 256)
-        queries = expand_group(triple[:, lanes], 8)
-        scores = nt(gathered[:, lanes], queries)
-        same = image_col[...] == image_row[:, g * width : (g + 1) * width]
-        scores = jnp.where(same, scores * SCALING, MASKED_SCORE)
-        top = jnp.max(scores, axis=0, keepdims=True)
-        exps = jnp.exp2((scores - top) * LOG2E)
-        low = (exps * (1.0 / col(exps))).astype(bf16)
-        probs[g] = low
-        merged[:, lanes] = fold_group(tn(low, gathered[:, D + 256 * g : D + 256 * g + 256]), 8).astype(bf16)
-    mid = regional[...].astype(f32) + nn(merged[...], w_out[...]) + out_bias[...]
-    region_mid[...] = mid
-    vhat, _ = norm_stats(mid)
-    normed = (vhat * gain[...] + shift[...]).astype(bf16)
-    triple0[...] = (nn(normed, w_qkv[...]) + bias[...]).astype(bf16)
+    step = pl.program_id(0)
+    place = Place(wins, dps)
+    count = regional.shape[0]
+    group = gathered.shape[0]
+    mine = pl.ds(pl.multiple_of(place.win * count, 16), count)
+
+    def project(normed):
+        out = nn(normed, w_qkv[...])
+        return jnp.concatenate(
+            [out[:, :D] + row(vecs, QUERY_BIAS), out[:, D : 2 * D], out[:, 2 * D :] + row(vecs, VALUE_BIAS)], axis=1
+        ).astype(bf16)
+
+    def sends():
+        copies = []
+        for j in range(1, wins):
+            copies.append(pltpu.make_async_remote_copy(
+                src_ref=packed, dst_ref=gathered.at[mine], send_sem=sem.at[2 * j - 2], recv_sem=sem.at[2 * j - 1],
+                device_id={"win": lax.rem(place.win + j, wins)}, device_id_type=MESH,
+            ))
+        return copies
+
+    @pl.when(step == 0)
+    def _():
+        place.greet(all_wins=True, along=False)
+        for at, v in (
+            (GAIN1, in_gain), (SHIFT1, in_shift), (GAIN2, mlp_gain), (SHIFT2, mlp_shift), (OUT_BIAS, out_bias), (DOWN_BIAS, down_bias),
+        ):
+            vecs[at : at + 1] = v[...].astype(f32).reshape(1, D)
+        vecs[QUERY_BIAS : QUERY_BIAS + 1] = qkv_bias[0:1].astype(f32)
+        vecs[KEY_BIAS : KEY_BIAS + 1] = jnp.zeros((1, D), f32)
+        vecs[VALUE_BIAS : VALUE_BIAS + 1] = qkv_bias[1:2].astype(f32)
+        up = up_bias[...].astype(f32).reshape(1, FF)
+        for b in range(FF // D):
+            vecs[UP_BIAS + b : UP_BIAS + b + 1] = up[:, D * b : D * (b + 1)]
+        vecs[UP_BIAS + FF // D : 16] = jnp.zeros((16 - UP_BIAS - FF // D, D), f32)
+        vhat, _ = norm_stats(regional[...].astype(f32))
+        normed = normed_low(vhat, vecs, GAIN1, SHIFT1)
+        own = project(normed)
+        region_triple[...] = own
+        packed[:, : 2 * D] = own[:, D:]
+        packed[:, 2 * D :] = normed
+        gathered[mine] = packed[...]
+        place.greeted(all_wins=True, along=False)
+        for c in sends():
+            c.start()
+        ids = images[...].astype(f32)
+        image_col[...] = jnp.broadcast_to(ids, (128, group)).T
+
+    rows = patches.shape[0] * count
+    vhat, _ = norm_stats(patches[...].reshape(rows, D).astype(f32))
+    triple[...] = project(normed_low(vhat, vecs, GAIN1, SHIFT1)).reshape(triple.shape)
+
+    @pl.when(step == pl.num_programs(0) - 1)
+    def _():
+        for c in sends():
+            c.wait()
+        gathered_out[...] = gathered[...]
+        own_ids = image_col[mine]
+        own_row = jnp.concatenate([own_ids] * 8, axis=0).T[0:1]
+        same = image_col[:, 0:1] == own_row
+        for g in range(2):
+            lanes = slice(256 * g, 256 * g + 256)
+            scores = nt(gathered[:, lanes], expand_group(region_triple[:, lanes], 8))
+            scores = jnp.where(same, scores * SCALING, MASKED_SCORE)
+            top = jnp.max(scores, axis=0, keepdims=True)
+            exps = jnp.exp2((scores - top) * LOG2E)
+            low = (exps * (1.0 / col(exps))).astype(bf16)
+            probs[g] = low
+            merged[:, lanes] = fold_group(tn(low, gathered[:, D + 256 * g : D + 256 * g + 256]), 8).astype(bf16)
+        mid = regional[...].astype(f32) + nn(merged[...], w_out[...]) + row(vecs, OUT_BIAS)
+        region_mid[...] = mid
+        vhat_mid, _ = norm_stats(mid)
+        triple0[...] = project(normed_low(vhat_mid, vecs, GAIN1, SHIFT1))
 
 
 def expand(x):
@@ -407,7 +536,7 @@
 def back_kernel(
     wins, dps,
     triple, triple0, probs, grad_merged,
-    region_triple, gathered, probs_r, merged_r, region_mid, grad_middle0, gain, w_qkv, w_out, out_local,
+    region_triple, gathered, probs_r, merged_r, region_mid, grad_middle0, vecs, w_qkv, w_out, out_local,
     up_source, down_source,
     grad_triple, up_sum, down_sum, terms, grad_query, out_grad, sums, out_bias_part, grad_mid,
     t, d, d0, *streams,
@@ -430,24 +559,20 @@
         t[12 + b, 0:rows] = grad_merged[:, :, 128 * b : 128 * b + 128].reshape(rows, 128).astype(f32)
         t[12 + b, rows:] = jnp.zeros((TP * WC - rows, 128), f32)
 
-    hooks = {
-        0: (place.greeted, up.send_cores, down.send_cores),
-        1: (up.send_chips,),
-        2: (down.send_chips,),
-        5: (up.send_dps,),
-        8: (up.send_dps_back, down.send_dps),
-        11: (up.send_chips_back, down.send_dps_back),
-    }
+    def slot(k):
+        if k == 0:
+            place.greeted()
+        up.step(k)
+        down.step(k - 1)
 
     def body(i, carry):
         for u in range(4):
             local_bwd_step(i * 4 + u, probs, t, d)
-        for when, todo in hooks.items():
-
-            @pl.when(step * (WC // 4) + i == when)
-            def _(todo=todo):
-                for act in todo:
-                    act()
+        for k in range(6):
+
+            @pl.when(step * (WC // 4) + i == 2 * k)
+            def _(k=k):
+                slot(k)
 
         return carry
 
@@ -462,7 +587,7 @@
     @pl.when(step == pl.num_programs(0) - 1)
     def _():
         vhat, inverse = norm_stats(region_mid[...])
-        mid = grad_middle0[0].astype(f32) + norm_back(vhat, inverse, gain[...], nt(d0[...], w_qkv[...]))
+        mid = grad_middle0[0].astype(f32) + norm_back(vhat, inverse, row(vecs, GAIN1), nt(d0[...], w_qkv[...]))
         grad_mid[...] = mid
         grad_attn = mid.astype(bf16)
         out_grad[...] = (out_local[...] + tn(merged_r[...], grad_attn)).astype(bf16)
@@ -480,14 +605,11 @@
             terms[:, lanes] = (nn(back, qx) * SCALING).astype(bf16)
             terms[:, value_lanes] = nn(low, gx).astype(bf16)
             grad_query[:, lanes] = (fold_group(tn(back, gathered[:, lanes]), 8) * SCALING).astype(bf16)
-            if g == 0:
-                down.send_chips_back()
+            slot(6 + g)
         sums[:, :D] = col(grad_query[...].astype(f32))
         sums[:, D:] = col(terms[...].astype(f32))
-        up.send_cores_back()
-        down.send_cores_back()
-        up.finish()
-        down.finish()
+        slot(8)
+        slot(9)
 
 
 def gelu_both(v):
@@ -504,7 +626,7 @@
 
 
 def mlp_kernel(
-    patches, region_mid, merged, patch_cot, region_cot, w_out, out_bias, gain, shift, w_up, up_bias, w_down, down_bias,
+    patches, region_mid, merged, patch_cot, region_cot, vecs, w_out, w_up, w_down,
     patch_out, region_out, grad_middle, grad_merged, up_grad, down_grad_t, out_grad, vec512, up_bias_grad,
     up_acc, down_acc,
 ):
@@ -524,16 +646,16 @@
     x = with_region(patches[...].astype(f32), region_mid[...], last)
     grad_result = with_region(patch_cot[...], region_cot[...], last)
     low_merged = merged[...].reshape(rows, D)
-    middle = x + nn(low_merged, w_out[...]) + out_bias[...]
+    middle = x + nn(low_merged, w_out[...]) + row(vecs, OUT_BIAS)
     vhat, inverse = norm_stats(middle)
-    mlp_in = (vhat * gain[...] + shift[...]).astype(bf16)
+    mlp_in = normed_low(vhat, vecs, GAIN2, SHIFT2)
     mlp_in_t = mlp_in.T
     grad_result_t = grad_result.T
-    result = middle + down_bias[...]
+    result = middle + row(vecs, DOWN_BIAS)
     grad_in = jnp.zeros((rows, D), f32)
     for f in range(FF // 512):
         at = slice(512 * f, 512 * f + 512)
-        hidden = nn(mlp_in, w_up[:, at]) + up_bias[:, at]
+        hidden = nn(mlp_in, w_up[:, at]) + row(vecs, UP_BIAS + f)
         active, slope = gelu_both(hidden)
         active = active.astype(bf16)
         grad_hidden = (nt(grad_result, w_down[at, :]) * slope).astype(bf16)
@@ -545,7 +667,7 @@
     shown = result.astype(bf16)
     patch_out[...] = shown.reshape(tokens, count, D)
     region_out[...] = shown[rows - count :]
-    gm = grad_result.astype(f32) + norm_back(vhat, inverse, gain[...], grad_in)
+    gm = grad_result.astype(f32) + norm_back(vhat, inverse, row(vecs, GAIN2), grad_in)
     low_gm = gm.astype(bf16)
     grad_middle[...] = low_gm.reshape(tokens, count, D)
     out_grad[...] += nn(low_merged.T, low_gm)
@@ -563,7 +685,7 @@
 
 def tail_kernel(
     wins, dps,
-    patches, grad_triple, grad_middle, region_mid, gain, shift, w_qkv, region_in, region_in_all, terms, grad_query,
+    patches, grad_triple, grad_middle, region_mid, vecs, w_qkv, region_in_all, terms, grad_query,
     regional, grad_mid, vec_mlp, up_bias_grad, sums, out_bias_part, out_source,
     patch_grad, region_grad, small_sum, out_sum, query_sum, key_sum, value_sum,
     qkv_acc, qkv_low, triple_sums, vec, pieces, piece_sem, pack, near, near_sem, total, far, far_sem, *streams,
@@ -615,15 +737,16 @@
             key_value += pieces[j].astype(f32)
         vhat, inverse = norm_stats(regional[...].astype(f32))
         grad_in = nt(grad_query[...], w_qkv[:, :D]) + nt(key_value.astype(bf16), w_qkv[:, D:])
-        region_grad[...] = (grad_mid[...] + norm_back(vhat, inverse, gain[...], grad_in)).astype(bf16)
+        region_grad[...] = (grad_mid[...] + norm_back(vhat, inverse, row(vecs, GAIN1), grad_in)).astype(bf16)
         vec[0:1] += col(grad_in * vhat)
         vec[1:2] += col(grad_in)
 
     def qkv_end():
-        qkv_low[0] = (qkv_acc[:, :D] + tn(region_in[...], grad_query[...])).astype(bf16)
+        shape = qkv_low.shape[1:]
+        qkv_low[0] = (qkv_acc[:, :D] + tn(region_in_all[pl.ds(pl.multiple_of(place.win * count, 16), count)], grad_query[...])).astype(bf16).reshape(shape)
         for b in range(1, 3):
             lanes = slice(D * (b - 1), D * b)
-            qkv_low[b] = (qkv_acc[:, D * b : D * (b + 1)] + tn(region_in_all[...], terms[:, lanes])).astype(bf16)
+            qkv_low[b] = (qkv_acc[:, D * b : D * (b + 1)] + tn(region_in_all[...], terms[:, lanes])).astype(bf16).reshape(shape)
         for s in blocks:
             s.load()
             s.send_cores()
@@ -672,7 +795,7 @@
 
     @pl.when(step < half)
     def _():
-        local_in = (vhat * gain[...] + shift[...]).astype(bf16)
+        local_in = normed_low(vhat, vecs, GAIN1, SHIFT1)
         qkv_acc[...] += nn(local_in.T, low)
         triple_sums[...] += col(low.astype(f32))
 
@@ -681,25 +804,36 @@
         grad_in = nt(low, w_qkv[...])
         vec[0:1] += col(grad_in * vhat)
         vec[1:2] += col(grad_in)
-        total_rows = grad_middle[...].reshape(rows, D).astype(f32) + norm_back(vhat, inverse, gain[...], grad_in)
+        total_rows = grad_middle[...].reshape(rows, D).astype(f32) + norm_back(vhat, inverse, row(vecs, GAIN1), grad_in)
         patch_grad[...] = total_rows.astype(bf16).reshape(tokens, count, D)
 
-    query, key, value = blocks
+    def slot(k):
+        out.step(k)
+
+    def block_slot(k):
+        for s in blocks:
+            s.step(k)
+
+    def end():
+        small_begin()
+        for k in range(5, 7):
+            block_slot(k)
+        small_middle()
+        block_slot(7)
+        small_end()
+        block_slot(8)
+
     hooks = {
         0: (begin,),
-        1: (out.send_chips,),
-        2: (region_end,),
-        3: (out.send_dps,),
-        half - 1: (qkv_end, out.send_dps_back),
-        half: (query.send_chips, key.send_chips),
-        half + 1: (value.send_chips, out.send_chips_back),
-        half + 2: (query.send_dps, out.send_cores_back),
-        half + 3: (key.send_dps,),
-        half + 4: (
-            small_begin, out.finish, value.send_dps, query.send_dps_back, small_middle, key.send_dps_back,
-            value.send_dps_back, query.send_chips_back, small_end, key.send_chips_back, value.send_chips_back,
-            query.send_cores_back, key.send_cores_back, value.send_cores_back, query.finish, key.finish, value.finish,
-        ),
+        1: (lambda: slot(1),),
+        2: (lambda: slot(2), region_end),
+        3: (lambda: slot(3),),
+        half - 1: (qkv_end, lambda: slot(4)),
+        half: (lambda: block_slot(1), lambda: slot(5)),
+        half + 1: (lambda: block_slot(2), lambda: slot(6)),
+        half + 2: (lambda: block_slot(3), lambda: slot(7)),
+        half + 3: (lambda: block_slot(4), lambda: slot(8)),
+        half + 4: (end,),
     }
     for when, todo in hooks.items():
 
@@ -707,6 +841,27 @@
         def _(todo=todo):
             for act in todo:
                 act()
+
+
+def last_kernel(
+    up, down_t, out, query, key, value, small, patch_in, region_in,
+    patch_grad, region_grad, in_gain, in_shift, qkv, qkv_bias, out_grad, out_bias, mlp_gain, mlp_shift,
+    up_grad, up_bias, down_grad, down_bias,
+):
+    up_grad[...] = up[...].astype(f32)
+    down_grad[...] = down_t[...].T.astype(f32)
+    out_grad[...] = out[...].astype(f32)
+    for b, part in enumerate((query, key, value)):
+        qkv[:, D * b : D * (b + 1)] = part[...].astype(f32)
+    patch_grad[...] = patch_in[...]
+
+    @pl.when(pl.program_id(0) == 0)
+    def _():
+        region_grad[...] = region_in[...]
+        for at, v in ((0, in_gain), (1, in_shift), (4, out_bias), (5, mlp_gain), (6, mlp_shift), (7, down_bias)):
+            v[...] = small[at : at + 1].reshape(D)
+        qkv_bias[...] = small[2:4]
+        up_bias[...] = jnp.concatenate([small[8 + b : 9 + b] for b in range(FF // D)], axis=1).reshape(FF)
 
 
 def shards(
@@ -716,37 +871,23 @@
 ):
     _, count, patch, _ = patches.shape
     group = window_image.shape[1]
-    row = lambda v: v.astype(f32).reshape(1, -1)
-    gain1, shift1, gain2, shift2 = row(in_gain), row(in_shift), row(mlp_gain), row(mlp_shift)
-    bias_row = row(jnp.concatenate([qkv_bias[0], jnp.zeros_like(qkv_bias[0]), qkv_bias[1]]))
-    out_row, up_row, down_row = row(out_bias), row(up_bias), row(down_bias)
-    images = window_image[0]
-    own = lax.dynamic_slice_in_dim(images, lax.axis_index("win") * count, count)
-    image_row = jnp.tile(own, HEADS)[None]
-    image_col = images[:, None]
     x = patches[0].transpose(1, 0, 2)
     cot = patch_cot[0].transpose(1, 0, 2)
     reg = regional[0]
     rcot = region_cot[0]
-
-    region_in, region_triple = call(
-        region_in_kernel, (1,), [whole(a) for a in (reg, gain1, shift1, w_qkv, bias_row)],
-        [whole_out((count, D), bf16), whole_out((count, 3 * D), bf16)], name="region_in",
-    )
-    packed = jnp.concatenate([region_triple[:, D:], region_in], axis=1)
-    gathered = lax.all_gather(packed, "win", axis=0, tiled=True)
+    const = lambda *arrays: [whole(a) for a in arrays]
     block = lambda a, n: (a, (n,) + a.shape[1:], lambda i: (i, 0, 0))
     block_out = lambda shape, n, dtype=bf16: ((shape, dtype), (n,) + shape[1:], lambda i: (i, 0, 0))
-    (triple,) = call(
-        patch_proj_kernel, (pl.cdiv(patch, 7),),
-        [block(x, 7)] + [whole(a) for a in (gain1, shift1, w_qkv, bias_row)],
-        [block_out((patch, count, 3 * D), 7)], name="patch_proj",
-    )
-    probs_r, merged_r, region_mid, triple0 = call(
-        region_attn_kernel, (1,),
-        [whole(a) for a in (region_triple, gathered, image_col, image_row, reg, gain1, shift1, w_qkv, bias_row, w_out, out_row)],
-        [whole_out((2, group, 8 * count), bf16), whole_out((count, D), bf16),
-         whole_out((count, D), f32), whole_out((count, 3 * D), bf16)], name="region_attn",
+    triple, vecs, region_triple, gathered, probs_r, merged_r, region_mid, triple0 = call(
+        functools.partial(front_kernel, wins, dps), (pl.cdiv(patch, 7),),
+        [block(x, 7)]
+        + const(reg, window_image, in_gain, in_shift, w_qkv, qkv_bias, w_out, out_bias, mlp_gain, mlp_shift, up_bias, down_bias),
+        [block_out((patch, count, 3 * D), 7), whole_out((16, D), f32), whole_out((count, 3 * D), bf16),
+         whole_out((group, 3 * D), bf16), whole_out((2, group, 8 * count), bf16), whole_out((count, D), bf16),
+         whole_out((count, D), f32), whole_out((count, 3 * D), bf16)],
+        [pltpu.VMEM((group, 3 * D), bf16), pltpu.VMEM((count, 3 * D), bf16), pltpu.VMEM((group, 128), f32),
+         pltpu.SemaphoreType.DMA((2 * wins,))],
+        name="front", collective_id=2,
     )
     steps = (count // WC,)
     mid = lambda a: (a, (a.shape[0], WC, a.shape[2]), lambda i: (0, i, 0))
@@ -762,21 +903,20 @@
     patch_out, region_out, grad_middle, grad_merged, up_grad, down_grad_t, out_local, vec_mlp, up_bias_grad = call(
         mlp_kernel, rows_grid,
         [block(x, n), whole(region_mid), block(merged, n), block(cot, n)]
-        + [whole(a) for a in (rcot, w_out, out_row, gain2, shift2, w_up, up_row, w_down, down_row)],
+        + const(rcot, vecs, w_out, w_up, w_down),
         [block_out((patch, count, D), n), whole_out((count, D), bf16),
          block_out((patch + 1, count, D), n), block_out((patch + 1, count, D), n),
          whole_out((D, FF), bf16), whole_out((D, FF), bf16), whole_out((D, D), f32),
          whole_out((8, D), f32), whole_out((1, FF), f32)],
         [pltpu.VMEM((D, FF), f32), pltpu.VMEM((D, FF), f32)], name="mlp",
     )
-    const = lambda *arrays: [whole(a) for a in arrays]
     grad_triple, up_sum, down_sum, terms, grad_query, out_grad, sums, out_bias_part, grad_mid = call(
         functools.partial(back_kernel, wins, dps), steps,
         [mid(triple), tail(triple0), (probs, (WC, TP, HEADS * TP), lambda i: (i, 0, 0)), mid(grad_merged)]
         + const(region_triple, gathered, probs_r, merged_r, region_mid)
         + [(grad_middle, (1, count, D), lambda i: (patch, 0, 0))]
-        + const(gain1, w_qkv, w_out, out_local) + [left(up_grad), left(down_grad_t)],
-        [mid_out((patch + 1, count, 3 * D)), left_out((D, FF), bf16), left_out((D, FF), bf16),
+        + const(vecs, w_qkv, w_out, out_local) + [left(a.reshape(stream_shape(wins, FF))) for a in (up_grad, down_grad_t)],
+        [mid_out((patch + 1, count, 3 * D)), left_out(stream_shape(wins, FF), bf16), left_out(stream_shape(wins, FF), bf16),
          whole_out((group, 2 * D), bf16), whole_out((count, D), bf16), whole_out((D, D), bf16),
          whole_out((1, 3 * D), f32), whole_out((1, D), f32), whole_out((count, D), f32)],
         [pltpu.VMEM((16, TP * WC, 128), f32), pltpu.VMEM((12, TP * WC, 128), f32), pltpu.VMEM((count, 3 * D), bf16)]
@@ -789,35 +929,42 @@
     patch_grad, region_grad, small, out_sum, query_sum, key_sum, value_sum = call(
         functools.partial(tail_kernel, wins, dps), (2 * half,),
         [again(x), again(grad_triple), second(grad_middle)]
-        + const(region_mid, gain1, shift1, w_qkv, region_in)
+        + const(region_mid, vecs, w_qkv)
         + [(gathered, (group, D), lambda i: (0, 2))]
-        + const(terms, grad_query, reg, grad_mid, vec_mlp, up_bias_grad, sums, out_bias_part) + [left(out_grad)],
+        + const(terms, grad_query, reg, grad_mid, vec_mlp, up_bias_grad, sums, out_bias_part) + [left(out_grad.reshape(stream_shape(wins, D)))],
         [(((patch, count, D), bf16), (n, count, D), lambda i: (lax.max(i - half, 0), 0, 0)),
-         whole_out((count, D), bf16), whole_out((16, D), f32)] + [left_out((D, D), bf16)] * 4,
-        [pltpu.VMEM((D, 3 * D), f32), pltpu.VMEM((3, D, D), bf16), pltpu.VMEM((1, 3 * D), f32), pltpu.VMEM((8, D), f32),
+         whole_out((count, D), bf16), whole_out((16, D), f32)] + [left_out(stream_shape(wins, D), bf16)] * 4,
+        [pltpu.VMEM((D, 3 * D), f32), pltpu.VMEM((3,) + stream_shape(wins, D), bf16), pltpu.VMEM((1, 3 * D), f32), pltpu.VMEM((8, D), f32),
          pltpu.VMEM((wins - 1, count, 2 * D), bf16), pltpu.SemaphoreType.DMA((2 * wins,)),
          pltpu.VMEM((16, D), f32), pltpu.VMEM((wins - 1, 16, D), f32), pltpu.SemaphoreType.DMA((2 * wins,)),
          pltpu.VMEM((16, D), f32), pltpu.VMEM((max(dps - 1, 1), 16, D), f32), pltpu.SemaphoreType.DMA((2 * dps,))]
         + stream_scratch(wins, dps, D) * 4,
         name="tail", collective_id=1,
     )
+    up_sum, down_sum = up_sum.reshape(D, FF), down_sum.reshape(D, FF)
+    out_sum, query_sum, key_sum, value_sum = (a.reshape(D, D) for a in (out_sum, query_sum, key_sum, value_sum))
+    n = 8
+    down = lambda i: (i, 0)
+    vector = lambda size: ((((size,), f32)), (size,), lambda i: (0,))
+    token = -(-patch // n)
+    tokens = lambda i: (lax.min(i, (patch - 1) // token), 0, 0)
+    (
+        patch_grad, region_grad, in_gain_grad, in_shift_grad, qkv_grad, qkv_bias_grad, out_grad, out_bias_grad,
+        mlp_gain_grad, mlp_shift_grad, up_grad, up_bias_grad, down_grad, down_bias_grad,
+    ) = call(
+        last_kernel, (n,),
+        [(up_sum, (D // n, FF), down), (down_sum, (D, FF // n), lambda i: (0, i))]
+        + [(a, (D // n, D), down) for a in (out_sum, query_sum, key_sum, value_sum)]
+        + [whole(small), (patch_grad, (token, count, D), tokens), whole(region_grad)],
+        [(((patch, count, D), bf16), (token, count, D), tokens), whole_out((count, D), bf16), vector(D), vector(D),
+         (((D, 3 * D), f32), (D // n, 3 * D), down), whole_out((2, D), f32), (((D, D), f32), (D // n, D), down), vector(D),
+         vector(D), vector(D), (((D, FF), f32), (D // n, FF), down), vector(FF), (((FF, D), f32), (FF // n, D), down), vector(D)],
+        name="last",
+    )
     return (
-        patch_out.transpose(1, 0, 2)[None],
-        region_out[None],
-        patch_grad.transpose(1, 0, 2)[None],
-        region_grad[None],
-        small[0],
-        small[1],
-        jnp.concatenate([query_sum, key_sum, value_sum], axis=1).astype(f32),
-        small[2:4],
-        out_sum.astype(f32),
-        small[4],
-        small[5],
-        small[6],
-        up_sum.astype(f32),
-        small[8:12].reshape(-1),
-        down_sum.T.astype(f32),
-        small[7],
+        patch_out.transpose(1, 0, 2)[None], region_out[None], patch_grad.transpose(1, 0, 2)[None], region_grad[None],
+        in_gain_grad, in_shift_grad, qkv_grad, qkv_bias_grad, out_grad, out_bias_grad,
+        mlp_gain_grad, mlp_shift_grad, up_grad, up_bias_grad, down_grad, down_bias_grad,
     )
 
 

time: 283 us -> 237 us (0.84)
  other arithmetic: 20.2 us -> 0 us
  local copies, waits for them, and re-layouts: 16.6 us -> 0 us
  between operations: 14.1 us -> 0.86 us
  Pallas kernels: 223 us -> 236 us
  waiting for transfers between devices: 7.65 us -> 0 us
    pallas_call x7 -> x6, Pallas kernels: 223 us -> 236 us  [call(): pl.pallas_call(body, grid=grid, in_specs=[spec(b, i) for _, b, i in ins],...]
    convert_element_type x5 -> x0, other arithmetic: 9.85 us -> none  [the longest x1 2.54 us: shards(): up_sum.astype(f32)]
    unnamed x19 -> x0, local copies, waits for them, and re-layouts: 9.11 us -> none
    reshape x7 -> x0, other arithmetic: 8.83 us -> none  [shards(): row = lambda v: v.astype(f32).reshape(1, -1)]
    all_gather x1 -> x0, waiting for transfers between devices: 7.63 us -> none  [shards(): gathered = lax.all_gather(packed, 'win', axis=0, tiled=True)]
    slice x4 -> x0, local copies, waits for them, and re-layouts: 4.51 us -> none  [the longest x1 1.54 us: shards(): small[7]]
    another operation x4 -> x0, local copies, waits for them, and re-layouts: 2.92 us -> none  [the longest x1 1.5 us: shards(): image_col = images[:, None]]
  transfers between devices with their start and end apart: 1 -> 0, of which waited for: 1 -> 0; matrix products, arithmetic and copies ran while one was open for 3% -> 0% of each run, Pallas kernels for 4% -> 0%
where the time goes in v2:
time: 237 us
  Pallas kernels  236 us (100%)
    pallas_call x6, Pallas kernels, call(): pl.pallas_call(body, grid=grid, in_specs=[spec(b, i) for _, b, i in ins],...  236 us

profile of v2, /device:TPU:0, one launch (start us, length us, event | category | flops | bytes accessed | tf_op | source)
XLA Modules:
  0.0 236.9 jit_solution(6531153231912173942)
XLA Ops:
  0.6 22.7 %front.1 = (bf16[49,48,1536]{2,1,0:T(8,128)(2,1)}, f32[16,512]{1,0:T(8,128)}, bf16[48,1536]{1,0:T(8,128)(2,1)}, bf16[384,1536]{1,0:T(8,128)(2,1)}, bf16[2,384,38...) custom-call(bf16[49,48,512]{2,1,0:T(8,128)(2,1)} %bitcast.25, ...), custom_call_target="tpu_custom_call" | custom-call | tf_op jit(solution)/shard_map/front/pallas_call | solution.py:46
  23.3 21.9 %local_fwd.1 = (bf16[50,48,512]{2,1,0:T(8,128)(2,1)}, bf16[48,64,1024]{2,1,0:T(8,128)(2,1)}) custom-call(bf16[49,48,1536]{2,1,0:T(8,128)(2,1)} %get-tuple-element.66.triple, bf16[48,1536]{1,0:T(8,128)(2,1)} %get-tuple-element.67.triple0), custom_call_target="tpu_custom_call" | custom-call | tf_op jit(solution)/shard_map/local_fwd/pallas_call | solution.py:46
  45.3 50.2 %mlp.1 = (bf16[49,48,512]{2,1,0:T(8,128)(2,1)}, bf16[48,512]{1,0:T(8,128)(2,1)}, bf16[50,48,512]{2,1,0:T(8,128)(2,1)}, bf16[50,48,512]{2,1,0:T(8,128)(2,1)}, bf1...) custom-call(bf16[49,48,512]{2,1,0:T(8,128)(2,1)} %bitcast.26, ...), custom_call_target="tpu_custom_call" | custom-call | tf_op jit(solution)/shard_map/mlp/pallas_call | solution.py:46
  95.4 72.3 %back.1 = (bf16[50,48,1536]{2,1,0:T(8,128)(2,1)}, bf16[2,4,64,2048]{3,2,1,0:T(8,128)(2,1)}, bf16[2,4,64,2048]{3,2,1,0:T(8,128)(2,1)}, bf16[384,1024]{1,0:T(8,128...) custom-call(bf16[49,48,1536]{2,1,0:T(8,128)(2,1)} %get-tuple-element, ...), custom_call_target="tpu_custom_call" | custom-call | tf_op jit(solution)/shard_map/back/pallas_call | solution.py:46
  167.7 58.4 %tail.1 = (bf16[49,48,512]{2,1,0:T(8,128)(2,1)}, bf16[48,512]{1,0:T(8,128)(2,1)}, f32[16,512]{1,0:T(8,128)}, bf16[2,4,64,512]{3,2,1,0:T(8,128)(2,1)}, bf16[2,4,6...) custom-call(bf16[49,48,512]{2,1,0:T(8,128)(2,1)} %bitcast.27, ...), custom_call_target="tpu_custom_call" | custom-call | tf_op jit(solution)/shard_map/tail/pallas_call | solution.py:46
  226.1 10.6 %last.1 = (bf16[49,48,512]{2,1,0:T(8,128)(2,1)}, bf16[48,512]{1,0:T(8,128)(2,1)}, f32[512]{0:T(512)}, f32[512]{0:T(512)}, f32[512,1536]{1,0:T(8,128)}, /*index=5...) custom-call(bf16[512,2048]{1,0:T(8,128)(2,1)} %bitcast.29, ...), custom_call_target="tpu_custom_call" | custom-call | tf_op jit(solution)/shard_map/last/pallas_call | solution.py:46

commit v3 on v2

--- a/solution.py
+++ b/solution.py
@@ -21,6 +21,7 @@
 bf16 = jnp.bfloat16
 VMEM_LIMIT = 60 * 2**20
 MESH = pl.DeviceIdType.MESH
+BACK_SLOTS = (0, 1, 5, 8)
 
 
 def nn(a, b):
@@ -36,17 +37,17 @@
 
 
 def call(body, grid, ins, outs, scratch=(), name=None, collective_id=None):
-    def spec(block, index):
+    def spec(block, index, *single):
         if block is None:
             return pl.BlockSpec(memory_space=pl.ANY)
         if index is None:
             return pl.BlockSpec(block, lambda *_: (0,) * len(block), pipeline_mode=pl.Buffered(1))
-        return pl.BlockSpec(block, index)
+        return pl.BlockSpec(block, index, pipeline_mode=pl.Buffered(1) if any(single) else None)
 
     return pl.pallas_call(
         body,
         grid=grid,
-        in_specs=[spec(b, i) for _, b, i in ins],
+        in_specs=[spec(*entry[1:]) for entry in ins],
         out_specs=[spec(b, i) for _, b, i in outs],
         out_shape=[jax.ShapeDtypeStruct(s, d) for (s, d), _, _ in outs],
         scratch_shapes=list(scratch),
@@ -54,7 +55,7 @@
             vmem_limit_bytes=VMEM_LIMIT, collective_id=collective_id, has_side_effects=collective_id is not None
         ),
         name=name,
-    )(*[a for a, _, _ in ins])
+    )(*[entry[0] for entry in ins])
 
 
 def whole(a):
@@ -62,7 +63,7 @@
 
 
 def whole_out(shape, dtype):
-    return ((shape, dtype), shape, lambda *_: (0,) * len(shape))
+    return ((shape, dtype), shape, None)
 
 
 def left(a):
@@ -149,19 +150,25 @@
     return (2, wins // 2, D // wins, columns)
 
 
-def stream_scratch(wins, dps, columns):
+def stream_scratch(wins, dps, columns, kind="whole"):
     piece, last = rows_of(wins, dps)
     chips = wins // 2
     landing = (4, 2, piece, columns // 2) if chips == 4 else (max(chips - 1, 1), piece, columns)
+    half, part, some = pltpu.VMEM((chips, piece, columns), bf16), pltpu.VMEM((piece, columns), bf16), pltpu.VMEM((16, 128), bf16)
+    down = kind != "back"
     return [
-        pltpu.VMEM((chips, piece, columns), bf16),
-        pltpu.VMEM((chips, piece, columns), bf16),
-        pltpu.VMEM(landing, bf16),
-        pltpu.VMEM((piece, columns), bf16),
-        pltpu.VMEM((max(dps - 1, 1), last, columns), bf16),
-        pltpu.VMEM((piece, columns), bf16),
+        half if down else some,
+        half,
+        pltpu.VMEM(landing, bf16) if down else some,
+        part if down else some,
+        pltpu.VMEM((max(dps - 1, 1), last, columns), bf16) if down else some,
+        some if kind == "down" else part,
         pltpu.SemaphoreType.DMA((20 + 4 * chips + 4 * dps,)),
     ]
+
+
+def columns_of(refs):
+    return refs[1].shape[2]
 
 
 class Stream:
@@ -173,7 +180,7 @@
         self.own, self.r1, self.r2, self.s, self.r3, self.s2, self.sem = refs
         self.piece, self.last = rows_of(place.wins, place.dps)
         self.split = self.last != self.piece
-        columns = self.own.shape[2]
+        columns = columns_of(refs)
         self.left, self.right = pl.ds(0, columns // 2), pl.ds(columns // 2, columns // 2)
 
     def rows(self, start, size):
@@ -313,17 +320,33 @@
             self.s[...] = total.astype(bf16)
         self.start(self._dps())
 
-    def send_dps_back(self):
+    def sum_dps(self, out, at):
         self.wait(self._dps())
-        mine = self.rows(self.p.dp * self.last if self.split else 0, self.last)
+        mine = self.part()
         total = self.s[mine].astype(f32)
         for j in range(self.p.dps - 1):
             total += self.r3[j].astype(f32)
-        self.s2[mine] = total.astype(bf16)
+        out[at] = total.astype(bf16)
+
+    def part(self):
+        return self.rows(self.p.dp * self.last if self.split else 0, self.last)
+
+    def send_dps_back(self):
+        self.sum_dps(self.s2, self.part())
         self.start(self._dps_back())
 
+    def end_dps_back(self):
+        self.wait(self._dps_back())
+
+    def begin_back(self, part):
+        self.s2[self.part()] = part[...]
+        self.start(self._dps_back())
+
     def send_chips_back(self):
-        self.wait(self._dps_back())
+        self.end_dps_back()
+        self.start_chips_back()
+
+    def start_chips_back(self):
         self.r1[self.p.chip] = self.s2[...]
         if self.p.square:
             self.start(self._back_left(0))
@@ -389,7 +412,7 @@
 def front_kernel(
     wins, dps,
     patches, regional, images, in_gain, in_shift, w_qkv, qkv_bias, w_out, out_bias, mlp_gain, mlp_shift, up_bias, down_bias,
-    triple, vecs, region_triple, gathered_out, probs, merged, region_mid, triple0,
+    triple, local_in, vecs, region_triple, gathered_out, probs, merged, region_mid, triple0, local_in0,
     gathered, packed, image_col, sem,
 ):
     step = pl.program_id(0)
@@ -442,7 +465,9 @@
 
     rows = patches.shape[0] * count
     vhat, _ = norm_stats(patches[...].reshape(rows, D).astype(f32))
-    triple[...] = project(normed_low(vhat, vecs, GAIN1, SHIFT1)).reshape(triple.shape)
+    normed_rows = normed_low(vhat, vecs, GAIN1, SHIFT1)
+    local_in[...] = normed_rows.reshape(local_in.shape)
+    triple[...] = project(normed_rows).reshape(triple.shape)
 
     @pl.when(step == pl.num_programs(0) - 1)
     def _():
@@ -464,7 +489,9 @@
         mid = regional[...].astype(f32) + nn(merged[...], w_out[...]) + row(vecs, OUT_BIAS)
         region_mid[...] = mid
         vhat_mid, _ = norm_stats(mid)
-        triple0[...] = project(normed_low(vhat_mid, vecs, GAIN1, SHIFT1))
+        normed_mid = normed_low(vhat_mid, vecs, GAIN1, SHIFT1)
+        local_in0[...] = normed_mid
+        triple0[...] = project(normed_mid)
 
 
 def expand(x):
@@ -535,22 +562,24 @@
 
 def back_kernel(
     wins, dps,
-    triple, triple0, probs, grad_merged,
+    triple, triple0, probs, grad_merged, local_in, local_in0,
     region_triple, gathered, probs_r, merged_r, region_mid, grad_middle0, vecs, w_qkv, w_out, out_local,
     up_source, down_source,
-    grad_triple, up_sum, down_sum, terms, grad_query, out_grad, sums, out_bias_part, grad_mid,
-    t, d, d0, *streams,
+    grad_triple, up_part, down_part, terms, grad_query, low_first, low_second, sums, out_bias_part, grad_mid,
+    t, d, d0, qkv_acc, grad_merged_s, *streams,
 ):
     step = pl.program_id(0)
     place = Place(wins, dps)
-    up = Stream(place, up_source, up_sum, streams[: Stream.PARTS])
-    down = Stream(place, down_source, down_sum, streams[Stream.PARTS :])
+    up = Stream(place, up_source, None, streams[: Stream.PARTS])
+    down = Stream(place, down_source, None, streams[Stream.PARTS :])
 
     @pl.when(step == 0)
     def _():
         place.greet()
         up.load()
         down.load()
+        qkv_acc[...] = jnp.zeros_like(qkv_acc)
+        sums[...] = jnp.zeros_like(sums)
 
     patch = triple.shape[0]
     load_triple(t, triple, triple0, patch)
@@ -562,15 +591,18 @@
     def slot(k):
         if k == 0:
             place.greeted()
-        up.step(k)
-        down.step(k - 1)
+        for s in (up, down):
+            if k < 4:
+                s.step(k)
+            else:
+                s.sum_dps(up_part if s is up else down_part, slice(None))
 
     def body(i, carry):
         for u in range(4):
             local_bwd_step(i * 4 + u, probs, t, d)
-        for k in range(6):
-
-            @pl.when(step * (WC // 4) + i == 2 * k)
+        for k, when in enumerate(BACK_SLOTS):
+
+            @pl.when(step * (WC // 4) + i == when)
             def _(k=k):
                 slot(k)
 
@@ -583,6 +615,11 @@
         low = d[b, 0:rows].astype(bf16)
         grad_triple[:, :, lanes] = low.reshape(patch + 1, WC, 128)
         d0[at, lanes] = low[rows - WC :]
+        sums[:, lanes] += col(low.astype(f32))
+    normed = jnp.concatenate([local_in[...].reshape(patch * WC, D), local_in0[...]], axis=0).T
+    for b in range(3):
+        lanes = slice(D * b, D * (b + 1))
+        qkv_acc[:, lanes] += nn(normed, grad_triple[:, :, lanes].reshape(rows, D))
 
     @pl.when(step == pl.num_programs(0) - 1)
     def _():
@@ -590,26 +627,62 @@
         mid = grad_middle0[0].astype(f32) + norm_back(vhat, inverse, row(vecs, GAIN1), nt(d0[...], w_qkv[...]))
         grad_mid[...] = mid
         grad_attn = mid.astype(bf16)
-        out_grad[...] = (out_local[...] + tn(merged_r[...], grad_attn)).astype(bf16)
+        out_low = (out_local[...] + tn(merged_r[...], grad_attn)).astype(bf16)
         out_bias_part[...] = col(grad_attn.astype(f32))
         grad_merged_r = nt(grad_attn, w_out[...]).astype(bf16)
-        for g in range(2):
-            lanes = slice(256 * g, 256 * g + 256)
-            value_lanes = slice(D + 256 * g, D + 256 * g + 256)
+        grad_merged_s[...] = grad_merged_r
+
+        keys = gathered.shape[0]
+        width = 8 * region_triple.shape[0]
+        blocks = max(keys // width, 1) if keys % width == 0 else 1
+        size = keys // blocks
+
+        def group_half(g, carry):
+            lanes = pl.ds(pl.multiple_of(256 * g, 256), 256)
+            value_lanes = pl.ds(pl.multiple_of(D + 256 * g, 256), 256)
             qx = expand_group(region_triple[:, lanes], 8)
-            gx = expand_group(grad_merged_r[:, lanes], 8)
-            low = probs_r[g]
-            high = low.astype(f32)
-            scaled = high * nt(gathered[:, value_lanes], gx)
-            back = (scaled - high * col(scaled)).astype(bf16)
-            terms[:, lanes] = (nn(back, qx) * SCALING).astype(bf16)
-            terms[:, value_lanes] = nn(low, gx).astype(bf16)
-            grad_query[:, lanes] = (fold_group(tn(back, gathered[:, lanes]), 8) * SCALING).astype(bf16)
-            slot(6 + g)
-        sums[:, :D] = col(grad_query[...].astype(f32))
-        sums[:, D:] = col(terms[...].astype(f32))
-        slot(8)
-        slot(9)
+            gx = expand_group(grad_merged_s[:, lanes], 8)
+
+            def scaled_at(at):
+                high = probs_r[g, at].astype(f32)
+                return high, high * nt(gathered[at, value_lanes], gx)
+
+            def finish(at, row_terms, scaled=None):
+                high, scaled = scaled_at(at) if scaled is None else scaled
+                back = (scaled - high * row_terms).astype(bf16)
+                terms[at, lanes] = (nn(back, qx) * SCALING).astype(bf16)
+                terms[at, value_lanes] = nn(probs_r[g, at], gx).astype(bf16)
+                return tn(back, gathered[at, lanes])
+
+            if blocks == 1:
+                both = scaled_at(pl.ds(0, keys))
+                total = finish(pl.ds(0, keys), col(both[1]), both)
+            else:
+                at = lambda i: pl.ds(pl.multiple_of(i * size, 16), size)
+                row_terms = lax.fori_loop(
+                    0, blocks, lambda i, r: r + col(scaled_at(at(i))[1]), jnp.zeros((1, width), f32)
+                )
+                total = lax.fori_loop(
+                    0, blocks, lambda i, q: q + finish(at(i), row_terms), jnp.zeros((width, 256), f32)
+                )
+            grad_query[:, lanes] = (fold_group(total, 8) * SCALING).astype(bf16)
+            return carry
+
+        if blocks == 1:
+            group_half(0, 0)
+            group_half(1, 0)
+        else:
+            lax.fori_loop(0, 2, group_half, 0)
+        sums[:, :D] += col(grad_query[...].astype(f32))
+        sums[:, D:] += col(terms[...].astype(f32))
+        region_in_all = gathered[:, 2 * D :]
+        own_in = gathered[pl.ds(pl.multiple_of(place.win * region_triple.shape[0], 16), region_triple.shape[0]), 2 * D :]
+        shape = low_first.shape[:3] + (D,)
+        low_first[:, :, :, :D] = (qkv_acc[:, :D] + tn(own_in, grad_query[...])).astype(bf16).reshape(shape)
+        low_first[:, :, :, D:] = (qkv_acc[:, D : 2 * D] + tn(region_in_all, terms[:, :D])).astype(bf16).reshape(shape)
+        low_second[:, :, :, :D] = (qkv_acc[:, 2 * D :] + tn(region_in_all, terms[:, D:])).astype(bf16).reshape(shape)
+        low_second[:, :, :, D:] = out_low.reshape(shape)
+        slot(4)
 
 
 def gelu_both(v):
@@ -685,28 +758,36 @@
 
 def tail_kernel(
     wins, dps,
-    patches, grad_triple, grad_middle, region_mid, vecs, w_qkv, region_in_all, terms, grad_query,
-    regional, grad_mid, vec_mlp, up_bias_grad, sums, out_bias_part, out_source,
-    patch_grad, region_grad, small_sum, out_sum, query_sum, key_sum, value_sum,
-    qkv_acc, qkv_low, triple_sums, vec, pieces, piece_sem, pack, near, near_sem, total, far, far_sem, *streams,
+    patches, grad_triple, grad_middle, region_mid, vecs, w_qkv, terms, grad_query,
+    regional, grad_mid, vec_mlp, up_bias_grad, sums, out_bias_part, up_part, down_part, first_source, second_source,
+    patch_grad, region_grad, small_sum, up_sum, down_sum, first_sum, second_sum,
+    vec, halves, half_sem, summed, pieces, piece_sem, pack, near, near_sem, total, far, far_sem, *streams,
 ):
     step = pl.program_id(0)
-    half = pl.num_programs(0) // 2
     tokens, count, _ = patches.shape
     rows = tokens * count
     place = Place(wins, dps)
     parts = [streams[Stream.PARTS * b : Stream.PARTS * (b + 1)] for b in range(4)]
-    out = Stream(place, out_source, out_sum, parts[0])
-    blocks = [Stream(place, qkv_low.at[b], (query_sum, key_sum, value_sum)[b], parts[b + 1]) for b in range(3)]
+    late = (Stream(place, first_source, first_sum, parts[0]), Stream(place, second_source, second_sum, parts[1]))
+    early = (Stream(place, None, up_sum, parts[2]), Stream(place, None, down_sum, parts[3]))
+
+    def window_rows(chip, core):
+        return pl.ds(pl.multiple_of((chip * 2 + core) * count, 16), count)
+
+    def to_core():
+        return [pltpu.make_async_remote_copy(
+            src_ref=terms.at[window_rows(chip, 1 - place.core)], dst_ref=halves.at[chip],
+            send_sem=half_sem.at[2 * chip], recv_sem=half_sem.at[2 * chip + 1],
+            device_id=place.other_core(), device_id_type=MESH,
+        ) for chip in range(place.chips)]
 
     def to_owners():
         copies = []
-        for j in range(1, wins):
-            win = lax.rem(place.win + j, wins)
+        for j in range(1, place.chips):
+            chip, to = place.at_chip(j)
             copies.append(pltpu.make_async_remote_copy(
-                src_ref=terms.at[pl.ds(pl.multiple_of(win * count, 16), count)], dst_ref=pieces.at[j - 1],
-                send_sem=piece_sem.at[2 * j - 2], recv_sem=piece_sem.at[2 * j - 1],
-                device_id={"win": win}, device_id_type=MESH,
+                src_ref=summed.at[chip], dst_ref=pieces.at[j - 1],
+                send_sem=piece_sem.at[2 * j - 2], recv_sem=piece_sem.at[2 * j - 1], device_id=to, device_id_type=MESH,
             ))
         return copies
 
@@ -722,18 +803,40 @@
             device_id=place.at_dp(j)[1], device_id_type=MESH,
         ) for j in range(1, dps)]
 
+    def late_step(k):
+        for s in late:
+            s.step(k)
+
+    def early_step(k):
+        for s in early:
+            s.step(k)
+
     def begin():
         place.greeted(all_wins=True)
+        late_step(0)
+        for c in to_core():
+            c.start()
+        for s, part in zip(early, (up_part, down_part)):
+            s.begin_back(part)
+
+    def owners_begin():
+        for c in to_core():
+            c.wait()
+
+        def add(chip, carry):
+            own = terms[window_rows(chip, place.core)].astype(f32)
+            summed[chip] = (own + halves[chip].astype(f32)).astype(bf16)
+            return carry
+
+        lax.fori_loop(0, place.chips, add, 0)
         for c in to_owners():
             c.start()
-        out.load()
-        out.send_cores()
 
     def region_end():
         for c in to_owners():
             c.wait()
-        key_value = terms[pl.ds(pl.multiple_of(place.win * count, 16), count)].astype(f32)
-        for j in range(wins - 1):
+        key_value = summed[place.chip].astype(f32)
+        for j in range(place.chips - 1):
             key_value += pieces[j].astype(f32)
         vhat, inverse = norm_stats(regional[...].astype(f32))
         grad_in = nt(grad_query[...], w_qkv[:, :D]) + nt(key_value.astype(bf16), w_qkv[:, D:])
@@ -741,20 +844,10 @@
         vec[0:1] += col(grad_in * vhat)
         vec[1:2] += col(grad_in)
 
-    def qkv_end():
-        shape = qkv_low.shape[1:]
-        qkv_low[0] = (qkv_acc[:, :D] + tn(region_in_all[pl.ds(pl.multiple_of(place.win * count, 16), count)], grad_query[...])).astype(bf16).reshape(shape)
-        for b in range(1, 3):
-            lanes = slice(D * (b - 1), D * b)
-            qkv_low[b] = (qkv_acc[:, D * b : D * (b + 1)] + tn(region_in_all[...], terms[:, lanes])).astype(bf16).reshape(shape)
-        for s in blocks:
-            s.load()
-            s.send_cores()
-
     def small_begin():
         pack[0:2] = vec[0:2]
-        pack[2:3] = triple_sums[:, :D] + sums[:, :D]
-        pack[3:4] = triple_sums[:, 2 * D :] + sums[:, 2 * D :]
+        pack[2:3] = sums[:, :D]
+        pack[3:4] = sums[:, 2 * D :]
         pack[4:5] = vec_mlp[2:3] + out_bias_part[...]
         pack[5:7] = vec_mlp[0:2]
         pack[7:8] = vec_mlp[3:4]
@@ -785,74 +878,55 @@
     @pl.when(step == 0)
     def _():
         place.greet(all_wins=True)
-        qkv_acc[...] = jnp.zeros_like(qkv_acc)
-        triple_sums[...] = jnp.zeros_like(triple_sums)
+        for s in late:
+            s.load()
         vec[...] = jnp.zeros_like(vec)
-
-    x = with_region(patches[...].astype(f32), region_mid[...], lax.rem(step, half) == half - 1)
+        begin()
+
+    x = with_region(patches[...].astype(f32), region_mid[...], step == pl.num_programs(0) - 1)
     vhat, inverse = norm_stats(x)
-    low = grad_triple[...].reshape(rows, 3 * D)
-
-    @pl.when(step < half)
-    def _():
-        local_in = normed_low(vhat, vecs, GAIN1, SHIFT1)
-        qkv_acc[...] += nn(local_in.T, low)
-        triple_sums[...] += col(low.astype(f32))
-
-    @pl.when(step >= half)
-    def _():
-        grad_in = nt(low, w_qkv[...])
-        vec[0:1] += col(grad_in * vhat)
-        vec[1:2] += col(grad_in)
-        total_rows = grad_middle[...].reshape(rows, D).astype(f32) + norm_back(vhat, inverse, row(vecs, GAIN1), grad_in)
-        patch_grad[...] = total_rows.astype(bf16).reshape(tokens, count, D)
-
-    def slot(k):
-        out.step(k)
-
-    def block_slot(k):
-        for s in blocks:
-            s.step(k)
+    grad_in = nt(grad_triple[...].reshape(rows, 3 * D), w_qkv[...])
+    vec[0:1] += col(grad_in * vhat)
+    vec[1:2] += col(grad_in)
+    total_rows = grad_middle[...].reshape(rows, D).astype(f32) + norm_back(vhat, inverse, row(vecs, GAIN1), grad_in)
+    patch_grad[...] = total_rows.astype(bf16).reshape(tokens, count, D)
 
     def end():
+        late_step(3)
+        owners_begin()
+        early_step(5)
+        late_step(4)
+        early_step(6)
+        region_end()
         small_begin()
-        for k in range(5, 7):
-            block_slot(k)
+        late_step(5)
         small_middle()
-        block_slot(7)
+        late_step(6)
+        early_step(7)
         small_end()
-        block_slot(8)
+        late_step(7)
+        early_step(8)
+        late_step(8)
 
     hooks = {
-        0: (begin,),
-        1: (lambda: slot(1),),
-        2: (lambda: slot(2), region_end),
-        3: (lambda: slot(3),),
-        half - 1: (qkv_end, lambda: slot(4)),
-        half: (lambda: block_slot(1), lambda: slot(5)),
-        half + 1: (lambda: block_slot(2), lambda: slot(6)),
-        half + 2: (lambda: block_slot(3), lambda: slot(7)),
-        half + 3: (lambda: block_slot(4), lambda: slot(8)),
-        half + 4: (end,),
+        0: lambda: late_step(1),
+        3: lambda: late_step(2),
+        4: end,
     }
     for when, todo in hooks.items():
-
-        @pl.when(step == when)
-        def _(todo=todo):
-            for act in todo:
-                act()
+        pl.when(step == when)(todo)
 
 
 def last_kernel(
-    up, down_t, out, query, key, value, small, patch_in, region_in,
+    up, down_t, first, second, small, patch_in, region_in,
     patch_grad, region_grad, in_gain, in_shift, qkv, qkv_bias, out_grad, out_bias, mlp_gain, mlp_shift,
     up_grad, up_bias, down_grad, down_bias,
 ):
     up_grad[...] = up[...].astype(f32)
     down_grad[...] = down_t[...].T.astype(f32)
-    out_grad[...] = out[...].astype(f32)
-    for b, part in enumerate((query, key, value)):
-        qkv[:, D * b : D * (b + 1)] = part[...].astype(f32)
+    qkv[:, : 2 * D] = first[...].astype(f32)
+    qkv[:, 2 * D :] = second[:, :D].astype(f32)
+    out_grad[...] = second[:, D:].astype(f32)
     patch_grad[...] = patch_in[...]
 
     @pl.when(pl.program_id(0) == 0)
@@ -878,13 +952,13 @@
     const = lambda *arrays: [whole(a) for a in arrays]
     block = lambda a, n: (a, (n,) + a.shape[1:], lambda i: (i, 0, 0))
     block_out = lambda shape, n, dtype=bf16: ((shape, dtype), (n,) + shape[1:], lambda i: (i, 0, 0))
-    triple, vecs, region_triple, gathered, probs_r, merged_r, region_mid, triple0 = call(
+    triple, local_in, vecs, region_triple, gathered, probs_r, merged_r, region_mid, triple0, local_in0 = call(
         functools.partial(front_kernel, wins, dps), (pl.cdiv(patch, 7),),
         [block(x, 7)]
         + const(reg, window_image, in_gain, in_shift, w_qkv, qkv_bias, w_out, out_bias, mlp_gain, mlp_shift, up_bias, down_bias),
-        [block_out((patch, count, 3 * D), 7), whole_out((16, D), f32), whole_out((count, 3 * D), bf16),
+        [block_out((patch, count, 3 * D), 7), block_out((patch, count, D), 7), whole_out((16, D), f32), whole_out((count, 3 * D), bf16),
          whole_out((group, 3 * D), bf16), whole_out((2, group, 8 * count), bf16), whole_out((count, D), bf16),
-         whole_out((count, D), f32), whole_out((count, 3 * D), bf16)],
+         whole_out((count, D), f32), whole_out((count, 3 * D), bf16), whole_out((count, D), bf16)],
         [pltpu.VMEM((group, 3 * D), bf16), pltpu.VMEM((count, 3 * D), bf16), pltpu.VMEM((group, 128), f32),
          pltpu.SemaphoreType.DMA((2 * wins,))],
         name="front", collective_id=2,
@@ -910,39 +984,39 @@
          whole_out((8, D), f32), whole_out((1, FF), f32)],
         [pltpu.VMEM((D, FF), f32), pltpu.VMEM((D, FF), f32)], name="mlp",
     )
-    grad_triple, up_sum, down_sum, terms, grad_query, out_grad, sums, out_bias_part, grad_mid = call(
+    last_rows = rows_of(wins, dps)[1]
+    grad_triple, up_part, down_part, terms, grad_query, low_first, low_second, sums, out_bias_part, grad_mid = call(
         functools.partial(back_kernel, wins, dps), steps,
-        [mid(triple), tail(triple0), (probs, (WC, TP, HEADS * TP), lambda i: (i, 0, 0)), mid(grad_merged)]
+        [mid(triple), tail(triple0), (probs, (WC, TP, HEADS * TP), lambda i: (i, 0, 0), group > 512), mid(grad_merged), mid(local_in), tail(local_in0)]
         + const(region_triple, gathered, probs_r, merged_r, region_mid)
         + [(grad_middle, (1, count, D), lambda i: (patch, 0, 0))]
         + const(vecs, w_qkv, w_out, out_local) + [left(a.reshape(stream_shape(wins, FF))) for a in (up_grad, down_grad_t)],
-        [mid_out((patch + 1, count, 3 * D)), left_out(stream_shape(wins, FF), bf16), left_out(stream_shape(wins, FF), bf16),
-         whole_out((group, 2 * D), bf16), whole_out((count, D), bf16), whole_out((D, D), bf16),
+        [mid_out((patch + 1, count, 3 * D)), whole_out((last_rows, FF), bf16), whole_out((last_rows, FF), bf16),
+         whole_out((group, 2 * D), bf16), whole_out((count, D), bf16), whole_out(stream_shape(wins, 2 * D), bf16),
+         whole_out(stream_shape(wins, 2 * D), bf16),
          whole_out((1, 3 * D), f32), whole_out((1, D), f32), whole_out((count, D), f32)],
-        [pltpu.VMEM((16, TP * WC, 128), f32), pltpu.VMEM((12, TP * WC, 128), f32), pltpu.VMEM((count, 3 * D), bf16)]
-        + stream_scratch(wins, dps, FF) * 2,
+        [pltpu.VMEM((16, TP * WC, 128), f32), pltpu.VMEM((12, TP * WC, 128), f32), pltpu.VMEM((count, 3 * D), bf16),
+         pltpu.VMEM((D, 3 * D), f32), pltpu.VMEM((count, D), bf16)]
+        + stream_scratch(wins, dps, FF, "down") * 2,
         name="back", collective_id=0,
     )
-    half = rows_grid[0]
-    again = lambda a: (a, (n,) + a.shape[1:], lambda i: (lax.rem(i, half), 0, 0))
-    second = lambda a: (a, (n,) + a.shape[1:], lambda i: (lax.max(i - half, 0), 0, 0))
-    patch_grad, region_grad, small, out_sum, query_sum, key_sum, value_sum = call(
-        functools.partial(tail_kernel, wins, dps), (2 * half,),
-        [again(x), again(grad_triple), second(grad_middle)]
-        + const(region_mid, vecs, w_qkv)
-        + [(gathered, (group, D), lambda i: (0, 2))]
-        + const(terms, grad_query, reg, grad_mid, vec_mlp, up_bias_grad, sums, out_bias_part) + [left(out_grad.reshape(stream_shape(wins, D)))],
-        [(((patch, count, D), bf16), (n, count, D), lambda i: (lax.max(i - half, 0), 0, 0)),
-         whole_out((count, D), bf16), whole_out((16, D), f32)] + [left_out(stream_shape(wins, D), bf16)] * 4,
-        [pltpu.VMEM((D, 3 * D), f32), pltpu.VMEM((3,) + stream_shape(wins, D), bf16), pltpu.VMEM((1, 3 * D), f32), pltpu.VMEM((8, D), f32),
-         pltpu.VMEM((wins - 1, count, 2 * D), bf16), pltpu.SemaphoreType.DMA((2 * wins,)),
+    patch_grad, region_grad, small, up_sum, down_sum, first_sum, second_sum = call(
+        functools.partial(tail_kernel, wins, dps), rows_grid,
+        [block(x, n), block(grad_triple, n), block(grad_middle, n)]
+        + const(region_mid, vecs, w_qkv, terms, grad_query, reg, grad_mid, vec_mlp, up_bias_grad, sums, out_bias_part, up_part, down_part)
+        + [left(low_first), left(low_second)],
+        [block_out((patch, count, D), n), whole_out((count, D), bf16), whole_out((16, D), f32)]
+        + [left_out(stream_shape(wins, FF), bf16)] * 2 + [left_out(stream_shape(wins, 2 * D), bf16)] * 2,
+        [pltpu.VMEM((8, D), f32),
+         pltpu.VMEM((wins // 2, count, 2 * D), bf16), pltpu.SemaphoreType.DMA((wins,)), pltpu.VMEM((wins // 2, count, 2 * D), bf16),
+         pltpu.VMEM((wins // 2, count, 2 * D), bf16), pltpu.SemaphoreType.DMA((wins,)),
          pltpu.VMEM((16, D), f32), pltpu.VMEM((wins - 1, 16, D), f32), pltpu.SemaphoreType.DMA((2 * wins,)),
          pltpu.VMEM((16, D), f32), pltpu.VMEM((max(dps - 1, 1), 16, D), f32), pltpu.SemaphoreType.DMA((2 * dps,))]
-        + stream_scratch(wins, dps, D) * 4,
+        + stream_scratch(wins, dps, 2 * D) * 2 + stream_scratch(wins, dps, FF, "back") * 2,
         name="tail", collective_id=1,
     )
     up_sum, down_sum = up_sum.reshape(D, FF), down_sum.reshape(D, FF)
-    out_sum, query_sum, key_sum, value_sum = (a.reshape(D, D) for a in (out_sum, query_sum, key_sum, value_sum))
+    first_sum, second_sum = first_sum.reshape(D, 2 * D), second_sum.reshape(D, 2 * D)
     n = 8
     down = lambda i: (i, 0)
     vector = lambda size: ((((size,), f32)), (size,), lambda i: (0,))
@@ -954,7 +1028,7 @@
     ) = call(
         last_kernel, (n,),
         [(up_sum, (D // n, FF), down), (down_sum, (D, FF // n), lambda i: (0, i))]
-        + [(a, (D // n, D), down) for a in (out_sum, query_sum, key_sum, value_sum)]
+        + [(a, (D // n, 2 * D), down) for a in (first_sum, second_sum)]
         + [whole(small), (patch_grad, (token, count, D), tokens), whole(region_grad)],
         [(((patch, count, D), bf16), (token, count, D), tokens), whole_out((count, D), bf16), vector(D), vector(D),
          (((D, 3 * D), f32), (D // n, 3 * D), down), whole_out((2, D), f32), (((D, D), f32), (D // n, D), down), vector(D),

time: 237 us -> 214 us (0.903)
  Pallas kernels: 236 us -> 213 us
    pallas_call x6, Pallas kernels: 236 us -> 213 us  [call(): pl.pallas_call(body, grid=grid, in_specs=[spec(*entry[1:]) for entry in i...]
where the time goes in v3:
time: 214 us
  Pallas kernels  213 us (100%)
    pallas_call x6, Pallas kernels, call(): pl.pallas_call(body, grid=grid, in_specs=[spec(*entry[1:]) for entry in i...  213 us

profile of v3, /device:TPU:0, one launch (start us, length us, event | category | flops | bytes accessed | tf_op | source)
XLA Modules:
  0.0 213.9 jit_solution(12412863370137138666)
XLA Ops:
  0.6 22.8 %front.1 = (bf16[49,48,1536]{2,1,0:T(8,128)(2,1)}, bf16[49,48,512]{2,1,0:T(8,128)(2,1)}, f32[16,512]{1,0:T(8,128)}, bf16[48,1536]{1,0:T(8,128)(2,1)}, bf16[384,1...) custom-call(bf16[49,48,512]{2,1,0:T(8,128)(2,1)} %bitcast.22, ...), custom_call_target="tpu_custom_call" | custom-call | tf_op jit(solution)/shard_map/front/pallas_call | solution.py:47
  23.5 21.9 %local_fwd.1 = (bf16[50,48,512]{2,1,0:T(8,128)(2,1)}, bf16[48,64,1024]{2,1,0:T(8,128)(2,1)}) custom-call(bf16[49,48,1536]{2,1,0:T(8,128)(2,1)} %get-tuple-element.69.triple, bf16[48,1536]{1,0:T(8,128)(2,1)} %get-tuple-element.70.triple0), custom_call_target="tpu_custom_call" | custom-call | tf_op jit(solution)/shard_map/local_fwd/pallas_call | solution.py:47
  45.4 50.1 %mlp.1 = (bf16[49,48,512]{2,1,0:T(8,128)(2,1)}, bf16[48,512]{1,0:T(8,128)(2,1)}, bf16[50,48,512]{2,1,0:T(8,128)(2,1)}, bf16[50,48,512]{2,1,0:T(8,128)(2,1)}, bf1...) custom-call(bf16[49,48,512]{2,1,0:T(8,128)(2,1)} %bitcast.23, ...), custom_call_target="tpu_custom_call" | custom-call | tf_op jit(solution)/shard_map/mlp/pallas_call | solution.py:47
  95.5 49.9 %back.1 = (bf16[50,48,1536]{2,1,0:T(8,128)(2,1)}, bf16[16,2048]{1,0:T(8,128)(2,1)}, bf16[16,2048]{1,0:T(8,128)(2,1)}, bf16[384,1024]{1,0:T(8,128)(2,1)}, bf16[48...) custom-call(bf16[49,48,1536]{2,1,0:T(8,128)(2,1)} %get-tuple-element, ...), custom_call_target="tpu_custom_call" | custom-call | tf_op jit(solution)/shard_map/back/pallas_call | solution.py:47
  145.5 57.6 %tail.1 = (bf16[49,48,512]{2,1,0:T(8,128)(2,1)}, bf16[48,512]{1,0:T(8,128)(2,1)}, f32[16,512]{1,0:T(8,128)}, bf16[2,4,64,2048]{3,2,1,0:T(8,128)(2,1)}, bf16[2,4,...) custom-call(bf16[49,48,512]{2,1,0:T(8,128)(2,1)} %bitcast.24, ...), custom_call_target="tpu_custom_call" | custom-call | tf_op jit(solution)/shard_map/tail/pallas_call | solution.py:47
  203.1 10.6 %last.1 = (bf16[49,48,512]{2,1,0:T(8,128)(2,1)}, bf16[48,512]{1,0:T(8,128)(2,1)}, f32[512]{0:T(512)}, f32[512]{0:T(512)}, f32[512,1536]{1,0:T(8,128)}, /*index=5...) custom-call(bf16[512,2048]{1,0:T(8,128)(2,1)} %bitcast.26, ...), custom_call_target="tpu_custom_call" | custom-call | tf_op jit(solution)/shard_map/last/pallas_call | solution.py:47

commit v4 on v3

--- a/solution.py
+++ b/solution.py
@@ -16,12 +16,15 @@
 SCALING = HD ** (-0.5)
 LOG2E = 1.4426950408889634
 TP = 64
+FB = 2048
 WC = 16
 f32 = jnp.float32
 bf16 = jnp.bfloat16
 VMEM_LIMIT = 60 * 2**20
 MESH = pl.DeviceIdType.MESH
-BACK_SLOTS = (0, 1, 5, 8)
+BACK_SLOTS = (
+    (0, 0, (0,), (0,)), (0, 6, (1,), ()), (0, 16, (), (1,)), (1, 7, (2,), ()), (1, 16, (3,), (2,)), (2, 7, (), (3,)),
+)
 
 
 def nn(a, b):
@@ -36,7 +39,7 @@
     return lax.dot_general(a, b, (((0,), (0,)), ((), ())), preferred_element_type=f32)
 
 
-def call(body, grid, ins, outs, scratch=(), name=None, collective_id=None):
+def call(body, grid, ins, outs, scratch=(), name=None, collective_id=None, limit=VMEM_LIMIT):
     def spec(block, index, *single):
         if block is None:
             return pl.BlockSpec(memory_space=pl.ANY)
@@ -52,7 +55,7 @@
         out_shape=[jax.ShapeDtypeStruct(s, d) for (s, d), _, _ in outs],
         scratch_shapes=list(scratch),
         compiler_params=pltpu.CompilerParams(
-            vmem_limit_bytes=VMEM_LIMIT, collective_id=collective_id, has_side_effects=collective_id is not None
+            vmem_limit_bytes=limit, collective_id=collective_id, has_side_effects=collective_id is not None
         ),
         name=name,
     )(*[entry[0] for entry in ins])
@@ -532,12 +535,8 @@
             probs[w, :, 256 * b : 256 * b + 256] = low
             m[b, pl.ds(w, TP, stride=WC), :] = query_side(v, low)
 
-    def body(i, carry):
-        for u in range(4):
-            one(i * 4 + u)
-        return carry
-
-    lax.fori_loop(0, WC // 4, body, 0)
+    for w in range(WC):
+        one(w)
     for b in range(4):
         merged[:, :, 128 * b : 128 * b + 128] = m[b, 0 : (patch + 1) * WC].astype(bf16).reshape(patch + 1, WC, 128)
 
@@ -588,27 +587,26 @@
         t[12 + b, 0:rows] = grad_merged[:, :, 128 * b : 128 * b + 128].reshape(rows, 128).astype(f32)
         t[12 + b, rows:] = jnp.zeros((TP * WC - rows, 128), f32)
 
-    def slot(k):
-        if k == 0:
-            place.greeted()
-        for s in (up, down):
-            if k < 4:
-                s.step(k)
-            else:
-                s.sum_dps(up_part if s is up else down_part, slice(None))
-
-    def body(i, carry):
-        for u in range(4):
-            local_bwd_step(i * 4 + u, probs, t, d)
-        for k, when in enumerate(BACK_SLOTS):
-
-            @pl.when(step * (WC // 4) + i == when)
-            def _(k=k):
-                slot(k)
-
-        return carry
-
-    lax.fori_loop(0, WC // 4, body, 0)
+    def end():
+        for s, part in ((up, up_part), (down, down_part)):
+            s.sum_dps(part, slice(None))
+
+    def reached(w):
+        if w == 0:
+            pl.when(step == 0)(place.greeted)
+        for when, after, ups, downs in BACK_SLOTS:
+            if after == w:
+
+                @pl.when(step == when)
+                def _(ups=ups, downs=downs):
+                    for k in ups:
+                        up.step(k)
+                    for k in downs:
+                        down.step(k)
+
+    for w in range(WC):
+        local_bwd_step(w, probs, t, d)
+        reached(w)
     at = pl.ds(pl.multiple_of(step * WC, WC), WC)
     for b in range(12):
         lanes = slice(128 * b, 128 * b + 128)
@@ -620,6 +618,8 @@
     for b in range(3):
         lanes = slice(D * b, D * (b + 1))
         qkv_acc[:, lanes] += nn(normed, grad_triple[:, :, lanes].reshape(rows, D))
+
+    reached(WC)
 
     @pl.when(step == pl.num_programs(0) - 1)
     def _():
@@ -682,7 +682,7 @@
         low_first[:, :, :, D:] = (qkv_acc[:, D : 2 * D] + tn(region_in_all, terms[:, :D])).astype(bf16).reshape(shape)
         low_second[:, :, :, :D] = (qkv_acc[:, 2 * D :] + tn(region_in_all, terms[:, D:])).astype(bf16).reshape(shape)
         low_second[:, :, :, D:] = out_low.reshape(shape)
-        slot(4)
+        end()
 
 
 def gelu_both(v):
@@ -726,9 +726,10 @@
     grad_result_t = grad_result.T
     result = middle + row(vecs, DOWN_BIAS)
     grad_in = jnp.zeros((rows, D), f32)
-    for f in range(FF // 512):
-        at = slice(512 * f, 512 * f + 512)
-        hidden = nn(mlp_in, w_up[:, at]) + row(vecs, UP_BIAS + f)
+    up_row = jnp.concatenate([row(vecs, UP_BIAS + b) for b in range(FF // D)], axis=1)
+    for f in range(FF // FB):
+        at = slice(FB * f, FB * f + FB)
+        hidden = nn(mlp_in, w_up[:, at]) + up_row[:, at]
         active, slope = gelu_both(hidden)
         active = active.astype(bf16)
         grad_hidden = (nt(grad_result, w_down[at, :]) * slope).astype(bf16)
@@ -1017,7 +1018,7 @@
     )
     up_sum, down_sum = up_sum.reshape(D, FF), down_sum.reshape(D, FF)
     first_sum, second_sum = first_sum.reshape(D, 2 * D), second_sum.reshape(D, 2 * D)
-    n = 8
+    n = 4
     down = lambda i: (i, 0)
     vector = lambda size: ((((size,), f32)), (size,), lambda i: (0,))
     token = -(-patch // n)

time: 214 us -> 201 us (0.939)
  Pallas kernels: 213 us -> 200 us
    pallas_call x6, Pallas kernels: 213 us -> 200 us  [call(): pl.pallas_call(body, grid=grid, in_specs=[spec(*entry[1:]) for entry in i...]
where the time goes in v4:
time: 201 us
  Pallas kernels  200 us (100%)
    pallas_call x6, Pallas kernels, call(): pl.pallas_call(body, grid=grid, in_specs=[spec(*entry[1:]) for entry in i...  200 us

profile of v4, /device:TPU:0, one launch (start us, length us, event | category | flops | bytes accessed | tf_op | source)
XLA Modules:
  0.0 201.0 jit_solution(14946606636946053888)
XLA Ops:
  0.6 22.8 %front.1 = (bf16[49,48,1536]{2,1,0:T(8,128)(2,1)}, bf16[49,48,512]{2,1,0:T(8,128)(2,1)}, f32[16,512]{1,0:T(8,128)}, bf16[48,1536]{1,0:T(8,128)(2,1)}, bf16[384,1...) custom-call(bf16[49,48,512]{2,1,0:T(8,128)(2,1)} %bitcast.22, ...), custom_call_target="tpu_custom_call" | custom-call | tf_op jit(solution)/shard_map/front/pallas_call | solution.py:50
  23.5 17.2 %local_fwd.1 = (bf16[50,48,512]{2,1,0:T(8,128)(2,1)}, bf16[48,64,1024]{2,1,0:T(8,128)(2,1)}) custom-call(bf16[49,48,1536]{2,1,0:T(8,128)(2,1)} %get-tuple-element.69.triple, bf16[48,1536]{1,0:T(8,128)(2,1)} %get-tuple-element.70.triple0), custom_call_target="tpu_custom_call" | custom-call | tf_op jit(solution)/shard_map/local_fwd/pallas_call | solution.py:50
  40.7 48.3 %mlp.1 = (bf16[49,48,512]{2,1,0:T(8,128)(2,1)}, bf16[48,512]{1,0:T(8,128)(2,1)}, bf16[50,48,512]{2,1,0:T(8,128)(2,1)}, bf16[50,48,512]{2,1,0:T(8,128)(2,1)}, bf1...) custom-call(bf16[49,48,512]{2,1,0:T(8,128)(2,1)} %bitcast.23, ...), custom_call_target="tpu_custom_call" | custom-call | tf_op jit(solution)/shard_map/mlp/pallas_call | solution.py:50
  89.0 44.7 %back.1 = (bf16[50,48,1536]{2,1,0:T(8,128)(2,1)}, bf16[16,2048]{1,0:T(8,128)(2,1)}, bf16[16,2048]{1,0:T(8,128)(2,1)}, bf16[384,1024]{1,0:T(8,128)(2,1)}, bf16[48...) custom-call(bf16[49,48,1536]{2,1,0:T(8,128)(2,1)} %get-tuple-element, ...), custom_call_target="tpu_custom_call" | custom-call | tf_op jit(solution)/shard_map/back/pallas_call | solution.py:50
  133.7 57.5 %tail.1 = (bf16[49,48,512]{2,1,0:T(8,128)(2,1)}, bf16[48,512]{1,0:T(8,128)(2,1)}, f32[16,512]{1,0:T(8,128)}, bf16[2,4,64,2048]{3,2,1,0:T(8,128)(2,1)}, bf16[2,4,...) custom-call(bf16[49,48,512]{2,1,0:T(8,128)(2,1)} %bitcast.24, ...), custom_call_target="tpu_custom_call" | custom-call | tf_op jit(solution)/shard_map/tail/pallas_call | solution.py:50
  191.1 9.7 %last.1 = (bf16[49,48,512]{2,1,0:T(8,128)(2,1)}, bf16[48,512]{1,0:T(8,128)(2,1)}, f32[512]{0:T(512)}, f32[512]{0:T(512)}, f32[512,1536]{1,0:T(8,128)}, /*index=5...) custom-call(bf16[512,2048]{1,0:T(8,128)(2,1)} %bitcast.26, ...), custom_call_target="tpu_custom_call" | custom-call | tf_op jit(solution)/shard_map/last/pallas_call | solution.py:50

commit v5 on v4

--- a/solution.py
+++ b/solution.py
@@ -22,6 +22,7 @@
 bf16 = jnp.bfloat16
 VMEM_LIMIT = 60 * 2**20
 MESH = pl.DeviceIdType.MESH
+FRONT_SLOTS = (5, 6)
 BACK_SLOTS = (
     (0, 0, (0,), (0,)), (0, 6, (1,), ()), (0, 16, (), (1,)), (1, 7, (2,), ()), (1, 16, (3,), (2,)), (2, 7, (), (3,)),
 )
@@ -125,23 +126,23 @@
         dp = lax.rem(self.dp + j, self.dps)
         return dp, {"dp": dp}
 
-    def near(self, all_wins):
+    def near(self, all_wins, around=False):
         if all_wins:
             return [{"win": lax.rem(self.win + j, self.wins)} for j in range(1, self.wins)]
-        if self.square:
+        if self.square and not around:
             return [self.other_core(), self.other_a(), self.other_b()]
         return [self.other_core()] + [self.at_chip(j)[1] for j in range(1, self.chips)]
 
-    def partners(self, all_wins, along):
-        return self.near(all_wins) + [self.at_dp(j)[1] for j in range(1, self.dps if along else 1)]
-
-    def greet(self, all_wins=False, along=True):
+    def partners(self, all_wins, along, around):
+        return self.near(all_wins, around) + [self.at_dp(j)[1] for j in range(1, self.dps if along else 1)]
+
+    def greet(self, all_wins=False, along=True, around=False):
         barrier = pltpu.get_barrier_semaphore()
-        for to in self.partners(all_wins, along):
+        for to in self.partners(all_wins, along, around):
             pl.semaphore_signal(barrier, inc=1, device_id=to, device_id_type=MESH)
 
-    def greeted(self, all_wins=False, along=True):
-        pl.semaphore_wait(pltpu.get_barrier_semaphore(), len(self.partners(all_wins, along)))
+    def greeted(self, all_wins=False, along=True, around=False):
+        pl.semaphore_wait(pltpu.get_barrier_semaphore(), len(self.partners(all_wins, along, around)))
 
 
 def rows_of(wins, dps):
@@ -430,18 +431,36 @@
             [out[:, :D] + row(vecs, QUERY_BIAS), out[:, D : 2 * D], out[:, 2 * D :] + row(vecs, VALUE_BIAS)], axis=1
         ).astype(bf16)
 
-    def sends():
+    parts = (pl.ds(0, 2 * D), pl.ds(2 * D, D))
+
+    def remote(src, dst, to, k):
+        return pltpu.make_async_remote_copy(
+            src_ref=src, dst_ref=dst, send_sem=sem.at[2 * k], recv_sem=sem.at[2 * k + 1], device_id=to, device_id_type=MESH
+        )
+
+    def direct(part):
+        lanes, first = parts[part], 2 * place.chips * part
+        targets = [place.other_core()] + [place.at_chip(j)[1] for j in range(1, place.chips)]
+        return [remote(packed.at[:, lanes], gathered.at[mine, lanes], to, first + j) for j, to in enumerate(targets)]
+
+    def onward(part):
+        lanes, first = parts[part], 2 * place.chips * part + place.chips
         copies = []
-        for j in range(1, wins):
-            copies.append(pltpu.make_async_remote_copy(
-                src_ref=packed, dst_ref=gathered.at[mine], send_sem=sem.at[2 * j - 2], recv_sem=sem.at[2 * j - 1],
-                device_id={"win": lax.rem(place.win + j, wins)}, device_id_type=MESH,
-            ))
+        for j in range(1, place.chips):
+            chip = lax.rem(place.chip - j + place.chips, place.chips)
+            theirs = gathered.at[pl.ds(pl.multiple_of((chip * 2 + place.core) * count, 16), count), lanes]
+            copies.append(remote(theirs, theirs, place.other_core(), first + j))
         return copies
+
+    def pass_on(part):
+        for c in direct(part):
+            c.wait()
+        for c in onward(part):
+            c.start()
 
     @pl.when(step == 0)
     def _():
-        place.greet(all_wins=True, along=False)
+        place.greet(around=True, along=False)
         for at, v in (
             (GAIN1, in_gain), (SHIFT1, in_shift), (GAIN2, mlp_gain), (SHIFT2, mlp_shift), (OUT_BIAS, out_bias), (DOWN_BIAS, down_bias),
         ):
@@ -460,9 +479,10 @@
         packed[:, : 2 * D] = own[:, D:]
         packed[:, 2 * D :] = normed
         gathered[mine] = packed[...]
-        place.greeted(all_wins=True, along=False)
-        for c in sends():
-            c.start()
+        place.greeted(around=True, along=False)
+        for part in range(2):
+            for c in direct(part):
+                c.start()
         ids = images[...].astype(f32)
         image_col[...] = jnp.broadcast_to(ids, (128, group)).T
 
@@ -472,11 +492,13 @@
     local_in[...] = normed_rows.reshape(local_in.shape)
     triple[...] = project(normed_rows).reshape(triple.shape)
 
+    for part, when in enumerate(FRONT_SLOTS):
+        pl.when(step == when)(functools.partial(pass_on, part))
+
     @pl.when(step == pl.num_programs(0) - 1)
     def _():
-        for c in sends():
+        for c in onward(0):
             c.wait()
-        gathered_out[...] = gathered[...]
         own_ids = image_col[mine]
         own_row = jnp.concatenate([own_ids] * 8, axis=0).T[0:1]
         same = image_col[:, 0:1] == own_row
@@ -495,6 +517,9 @@
         normed_mid = normed_low(vhat_mid, vecs, GAIN1, SHIFT1)
         local_in0[...] = normed_mid
         triple0[...] = project(normed_mid)
+        for c in onward(1):
+            c.wait()
+        gathered_out[...] = gathered[...]
 
 
 def expand(x):
@@ -895,9 +920,8 @@
     def end():
         late_step(3)
         owners_begin()
-        early_step(5)
+        early_step(6)
         late_step(4)
-        early_step(6)
         region_end()
         small_begin()
         late_step(5)
@@ -909,9 +933,13 @@
         early_step(8)
         late_step(8)
 
+    def middle():
+        late_step(2)
+        early_step(5)
+
     hooks = {
         0: lambda: late_step(1),
-        3: lambda: late_step(2),
+        3: middle,
         4: end,
     }
     for when, todo in hooks.items():
@@ -961,7 +989,7 @@
          whole_out((group, 3 * D), bf16), whole_out((2, group, 8 * count), bf16), whole_out((count, D), bf16),
          whole_out((count, D), f32), whole_out((count, 3 * D), bf16), whole_out((count, D), bf16)],
         [pltpu.VMEM((group, 3 * D), bf16), pltpu.VMEM((count, 3 * D), bf16), pltpu.VMEM((group, 128), f32),
-         pltpu.SemaphoreType.DMA((2 * wins,))],
+         pltpu.SemaphoreType.DMA((8 * wins,))],
         name="front", collective_id=2,
     )
     steps = (count // WC,)

time: 201 us -> 194 us (0.965)
  Pallas kernels: 200 us -> 193 us
    pallas_call x6, Pallas kernels: 200 us -> 193 us  [call(): pl.pallas_call(body, grid=grid, in_specs=[spec(*entry[1:]) for entry in i...]
where the time goes in v5:
time: 194 us
  Pallas kernels  193 us (99%)
    pallas_call x6, Pallas kernels, call(): pl.pallas_call(body, grid=grid, in_specs=[spec(*entry[1:]) for entry in i...  193 us

profile of v5, /device:TPU:0, one launch (start us, length us, event | category | flops | bytes accessed | tf_op | source)
XLA Modules:
  0.0 193.7 jit_solution(12295140709911401625)
XLA Ops:
  0.6 18.0 %front.1 = (bf16[49,48,1536]{2,1,0:T(8,128)(2,1)}, bf16[49,48,512]{2,1,0:T(8,128)(2,1)}, f32[16,512]{1,0:T(8,128)}, bf16[48,1536]{1,0:T(8,128)(2,1)}, bf16[384,1...) custom-call(bf16[49,48,512]{2,1,0:T(8,128)(2,1)} %bitcast.22, ...), custom_call_target="tpu_custom_call" | custom-call | tf_op jit(solution)/shard_map/front/pallas_call | solution.py:51
  18.7 17.2 %local_fwd.1 = (bf16[50,48,512]{2,1,0:T(8,128)(2,1)}, bf16[48,64,1024]{2,1,0:T(8,128)(2,1)}) custom-call(bf16[49,48,1536]{2,1,0:T(8,128)(2,1)} %get-tuple-element.69.triple, bf16[48,1536]{1,0:T(8,128)(2,1)} %get-tuple-element.70.triple0), custom_call_target="tpu_custom_call" | custom-call | tf_op jit(solution)/shard_map/local_fwd/pallas_call | solution.py:51
  35.9 48.3 %mlp.1 = (bf16[49,48,512]{2,1,0:T(8,128)(2,1)}, bf16[48,512]{1,0:T(8,128)(2,1)}, bf16[50,48,512]{2,1,0:T(8,128)(2,1)}, bf16[50,48,512]{2,1,0:T(8,128)(2,1)}, bf1...) custom-call(bf16[49,48,512]{2,1,0:T(8,128)(2,1)} %bitcast.23, ...), custom_call_target="tpu_custom_call" | custom-call | tf_op jit(solution)/shard_map/mlp/pallas_call | solution.py:51
  84.2 44.2 %back.1 = (bf16[50,48,1536]{2,1,0:T(8,128)(2,1)}, bf16[16,2048]{1,0:T(8,128)(2,1)}, bf16[16,2048]{1,0:T(8,128)(2,1)}, bf16[384,1024]{1,0:T(8,128)(2,1)}, bf16[48...) custom-call(bf16[49,48,1536]{2,1,0:T(8,128)(2,1)} %get-tuple-element, ...), custom_call_target="tpu_custom_call" | custom-call | tf_op jit(solution)/shard_map/back/pallas_call | solution.py:51
  128.4 55.5 %tail.1 = (bf16[49,48,512]{2,1,0:T(8,128)(2,1)}, bf16[48,512]{1,0:T(8,128)(2,1)}, f32[16,512]{1,0:T(8,128)}, bf16[2,4,64,2048]{3,2,1,0:T(8,128)(2,1)}, bf16[2,4,...) custom-call(bf16[49,48,512]{2,1,0:T(8,128)(2,1)} %bitcast.24, ...), custom_call_target="tpu_custom_call" | custom-call | tf_op jit(solution)/shard_map/tail/pallas_call | solution.py:51
  183.9 9.7 %last.1 = (bf16[49,48,512]{2,1,0:T(8,128)(2,1)}, bf16[48,512]{1,0:T(8,128)(2,1)}, f32[512]{0:T(512)}, f32[512]{0:T(512)}, f32[512,1536]{1,0:T(8,128)}, /*index=5...) custom-call(bf16[512,2048]{1,0:T(8,128)(2,1)} %bitcast.26, ...), custom_call_target="tpu_custom_call" | custom-call | tf_op jit(solution)/shard_map/last/pallas_call | solution.py:51

commit v6 on v5

--- a/solution.py
+++ b/solution.py
@@ -528,10 +528,7 @@
 
 
 def query_side(rows, weights):
-    lane = lax.broadcasted_iota(jnp.int32, (1, 128), 1) // HD
-    out = tn(rows, weights)
-    pairs = jnp.concatenate([out[0:64, 0:128], out[64:128, 128:256]], axis=0).T
-    return jnp.where(lane % 2 == 0, pairs[0:64], pairs[64:128])
+    return fold_group(tn(weights, rows), 4)
 
 
 def load_triple(t, triple, triple0, patch):
@@ -1046,7 +1043,7 @@
     )
     up_sum, down_sum = up_sum.reshape(D, FF), down_sum.reshape(D, FF)
     first_sum, second_sum = first_sum.reshape(D, 2 * D), second_sum.reshape(D, 2 * D)
-    n = 4
+    n = 2
     down = lambda i: (i, 0)
     vector = lambda size: ((((size,), f32)), (size,), lambda i: (0,))
     token = -(-patch // n)

time: 194 us -> 192 us (0.990)
  Pallas kernels: 193 us -> 191 us
where the time goes in v6:
time: 192 us
  Pallas kernels  191 us (99%)
    pallas_call x6, Pallas kernels, call(): pl.pallas_call(body, grid=grid, in_specs=[spec(*entry[1:]) for entry in i...  191 us

profile of v6, /device:TPU:0, one launch (start us, length us, event | category | flops | bytes accessed | tf_op | source)
XLA Modules:
  0.0 192.1 jit_solution(5123658115179365306)
XLA Ops:
  0.6 18.0 %front.1 = (bf16[49,48,1536]{2,1,0:T(8,128)(2,1)}, bf16[49,48,512]{2,1,0:T(8,128)(2,1)}, f32[16,512]{1,0:T(8,128)}, bf16[48,1536]{1,0:T(8,128)(2,1)}, bf16[384,1...) custom-call(bf16[49,48,512]{2,1,0:T(8,128)(2,1)} %bitcast.22, ...), custom_call_target="tpu_custom_call" | custom-call | tf_op jit(solution)/shard_map/front/pallas_call | solution.py:51
  18.7 16.9 %local_fwd.1 = (bf16[50,48,512]{2,1,0:T(8,128)(2,1)}, bf16[48,64,1024]{2,1,0:T(8,128)(2,1)}) custom-call(bf16[49,48,1536]{2,1,0:T(8,128)(2,1)} %get-tuple-element.69.triple, bf16[48,1536]{1,0:T(8,128)(2,1)} %get-tuple-element.70.triple0), custom_call_target="tpu_custom_call" | custom-call | tf_op jit(solution)/shard_map/local_fwd/pallas_call | solution.py:51
  35.6 48.3 %mlp.1 = (bf16[49,48,512]{2,1,0:T(8,128)(2,1)}, bf16[48,512]{1,0:T(8,128)(2,1)}, bf16[50,48,512]{2,1,0:T(8,128)(2,1)}, bf16[50,48,512]{2,1,0:T(8,128)(2,1)}, bf1...) custom-call(bf16[49,48,512]{2,1,0:T(8,128)(2,1)} %bitcast.23, ...), custom_call_target="tpu_custom_call" | custom-call | tf_op jit(solution)/shard_map/mlp/pallas_call | solution.py:51
  83.9 44.1 %back.1 = (bf16[50,48,1536]{2,1,0:T(8,128)(2,1)}, bf16[16,2048]{1,0:T(8,128)(2,1)}, bf16[16,2048]{1,0:T(8,128)(2,1)}, bf16[384,1024]{1,0:T(8,128)(2,1)}, bf16[48...) custom-call(bf16[49,48,1536]{2,1,0:T(8,128)(2,1)} %get-tuple-element, ...), custom_call_target="tpu_custom_call" | custom-call | tf_op jit(solution)/shard_map/back/pallas_call | solution.py:51
  128.0 55.6 %tail.1 = (bf16[49,48,512]{2,1,0:T(8,128)(2,1)}, bf16[48,512]{1,0:T(8,128)(2,1)}, f32[16,512]{1,0:T(8,128)}, bf16[2,4,64,2048]{3,2,1,0:T(8,128)(2,1)}, bf16[2,4,...) custom-call(bf16[49,48,512]{2,1,0:T(8,128)(2,1)} %bitcast.24, ...), custom_call_target="tpu_custom_call" | custom-call | tf_op jit(solution)/shard_map/tail/pallas_call | solution.py:51
  183.5 8.4 %last.1 = (bf16[49,48,512]{2,1,0:T(8,128)(2,1)}, bf16[48,512]{1,0:T(8,128)(2,1)}, f32[512]{0:T(512)}, f32[512]{0:T(512)}, f32[512,1536]{1,0:T(8,128)}, /*index=5...) custom-call(bf16[512,2048]{1,0:T(8,128)(2,1)} %bitcast.26, ...), custom_call_target="tpu_custom_call" | custom-call | tf_op jit(solution)/shard_map/last/pallas_call | solution.py:51

commit v7 on v6

--- a/solution.py
+++ b/solution.py
@@ -752,9 +752,10 @@
     for f in range(FF // FB):
         at = slice(FB * f, FB * f + FB)
         hidden = nn(mlp_in, w_up[:, at]) + up_row[:, at]
+        grad_active = nt(grad_result, w_down[at, :])
         active, slope = gelu_both(hidden)
         active = active.astype(bf16)
-        grad_hidden = (nt(grad_result, w_down[at, :]) * slope).astype(bf16)
+        grad_hidden = (grad_active * slope).astype(bf16)
         result += nn(active, w_down[at, :])
         grad_in += nt(grad_hidden, w_up[:, at])
         up_acc[:, at] += nn(mlp_in_t, grad_hidden)

time: 192 us -> 192 us (level)
  no operation moved by 1% of the time
where the time goes in v7:
time: 192 us
  Pallas kernels  191 us (99%)
    pallas_call x6, Pallas kernels, call(): pl.pallas_call(body, grid=grid, in_specs=[spec(*entry[1:]) for entry in i...  191 us

profile of v7, /device:TPU:0, one launch (start us, length us, event | category | flops | bytes accessed | tf_op | source)
XLA Modules:
  0.0 192.0 jit_solution(8038884619422382736)
XLA Ops:
  0.6 18.0 %front.1 = (bf16[49,48,1536]{2,1,0:T(8,128)(2,1)}, bf16[49,48,512]{2,1,0:T(8,128)(2,1)}, f32[16,512]{1,0:T(8,128)}, bf16[48,1536]{1,0:T(8,128)(2,1)}, bf16[384,1...) custom-call(bf16[49,48,512]{2,1,0:T(8,128)(2,1)} %bitcast.22, ...), custom_call_target="tpu_custom_call" | custom-call | tf_op jit(solution)/shard_map/front/pallas_call | solution.py:51
  18.7 16.9 %local_fwd.1 = (bf16[50,48,512]{2,1,0:T(8,128)(2,1)}, bf16[48,64,1024]{2,1,0:T(8,128)(2,1)}) custom-call(bf16[49,48,1536]{2,1,0:T(8,128)(2,1)} %get-tuple-element.69.triple, bf16[48,1536]{1,0:T(8,128)(2,1)} %get-tuple-element.70.triple0), custom_call_target="tpu_custom_call" | custom-call | tf_op jit(solution)/shard_map/local_fwd/pallas_call | solution.py:51
  35.6 48.3 %mlp.1 = (bf16[49,48,512]{2,1,0:T(8,128)(2,1)}, bf16[48,512]{1,0:T(8,128)(2,1)}, bf16[50,48,512]{2,1,0:T(8,128)(2,1)}, bf16[50,48,512]{2,1,0:T(8,128)(2,1)}, bf1...) custom-call(bf16[49,48,512]{2,1,0:T(8,128)(2,1)} %bitcast.23, ...), custom_call_target="tpu_custom_call" | custom-call | tf_op jit(solution)/shard_map/mlp/pallas_call | solution.py:51
  83.9 44.1 %back.1 = (bf16[50,48,1536]{2,1,0:T(8,128)(2,1)}, bf16[16,2048]{1,0:T(8,128)(2,1)}, bf16[16,2048]{1,0:T(8,128)(2,1)}, bf16[384,1024]{1,0:T(8,128)(2,1)}, bf16[48...) custom-call(bf16[49,48,1536]{2,1,0:T(8,128)(2,1)} %get-tuple-element, ...), custom_call_target="tpu_custom_call" | custom-call | tf_op jit(solution)/shard_map/back/pallas_call | solution.py:51
  127.9 55.5 %tail.1 = (bf16[49,48,512]{2,1,0:T(8,128)(2,1)}, bf16[48,512]{1,0:T(8,128)(2,1)}, f32[16,512]{1,0:T(8,128)}, bf16[2,4,64,2048]{3,2,1,0:T(8,128)(2,1)}, bf16[2,4,...) custom-call(bf16[49,48,512]{2,1,0:T(8,128)(2,1)} %bitcast.24, ...), custom_call_target="tpu_custom_call" | custom-call | tf_op jit(solution)/shard_map/tail/pallas_call | solution.py:51
  183.5 8.4 %last.1 = (bf16[49,48,512]{2,1,0:T(8,128)(2,1)}, bf16[48,512]{1,0:T(8,128)(2,1)}, f32[512]{0:T(512)}, f32[512]{0:T(512)}, f32[512,1536]{1,0:T(8,128)}, /*index=5...) custom-call(bf16[512,2048]{1,0:T(8,128)(2,1)} %bitcast.26, ...), custom_call_target="tpu_custom_call" | custom-call | tf_op jit(solution)/shard_map/last/pallas_call | solution.py:51
